TPU v7x, 32 devices: a whole 2x2x4 slice. The times are simulated.
32 devices in a mesh: dp: 16 (over z, y, core), head: 2 (over x).
Axes of the slice: x: 2, y: 2, z: 4, core: 2. Of those that a mesh axis runs over, the one named last changes fastest.
Arguments:
- tokens: bfloat16 [16384, 768], P(('dp', 'head')), may hold values from -6 to 6
- w_heads: bfloat16 [768, 2304], replicated, may hold values from -0.21875 to 0.21875
- b_heads: bfloat16 [2304], replicated, may hold values from -3 to 3
- w_merge: bfloat16 [768, 768], replicated, may hold values from -3 to 3
- b_merge: bfloat16 [768], replicated, may hold values from -3 to 3
- gain_first: bfloat16 [768], replicated, may hold values from 0.25 to 1.75
- bias_first: bfloat16 [768], replicated, may hold values from -3 to 3
- w_expand: bfloat16 [768, 3072], replicated, may hold values from -0.21875 to 0.21875
- b_expand: bfloat16 [3072], replicated, may hold values from -3 to 3
- w_reduce: bfloat16 [3072, 768], replicated, may hold values from -0.109375 to 0.109375
- b_reduce: bfloat16 [768], replicated, may hold values from -3 to 3
- gain_second: bfloat16 [768], replicated, may hold values from 0.25 to 1.75
- bias_second: bfloat16 [768], replicated, may hold values from -3 to 3
- seq_lengths: int32 [16, 4], P('dp'), may hold values from 1 to 640, 896 in all within a row
- cotangent: bfloat16 [16384, 768], P(('dp', 'head')), may hold values from -6 to 6
Outputs:
- block_output: bfloat16 [16384, 768], P(('dp', 'head'))
- input_grad: float32 [16384, 768], P(('dp', 'head'))
- grad_w_heads: float32 [768, 2304], P(('dp', 'head'))
- grad_b_scores: float32 [1536], P(('dp', 'head'))
- grad_b_values: float32 [768], P(('dp', 'head'))
- grad_w_merge: float32 [768, 768], P(('dp', 'head'))
- grad_b_merge: float32 [768], P(('dp', 'head'))
- grad_gain_first: float32 [768], P(('dp', 'head'))
- grad_bias_first: float32 [768], P(('dp', 'head'))
- grad_w_expand: float32 [768, 3072], P(('dp', 'head'))
- grad_b_expand: float32 [3072], P(('dp', 'head'))
- grad_w_reduce: float32 [3072, 768], P(('dp', 'head'))
- grad_b_reduce: float32 [768], P(('dp', 'head'))
- grad_gain_second: float32 [768], P(('dp', 'head'))
- grad_bias_second: float32 [768], P(('dp', 'head'))
Inputs may be any that keep to these rules, and one draw needn't show every extreme that they name: `seq_lengths`: row g lists the lengths of the 4 sequences of token group g in order; each row sums to 896 and its largest entry is 640; the last 128 rows of each group are padding.
All inputs are finite; a program needn't handle non-finite values.
Results may differ from a plain program's by a relative error of at most 0.012.
Values may be sent and summed in bfloat16 or wider, within the bound.
No kernel may reach another device: no remote copies, remote signals or barrier semaphores. Data moves between devices by JAX's collectives and lax.ppermute only.
A program may use at most 192 MiB of HBM per device.

v0:
```python
import functools
import math

import jax
import jax.numpy as jnp
from jax import lax
from jax.experimental import pallas as pl
from jax.experimental.pallas import tpu as pltpu
from jax.sharding import PartitionSpec as P

D = 768
PAIRS = 6
FF = 3072
LANES = 128
HALF = 64
BF = jnp.bfloat16
F32 = jnp.float32
AXES = ("dp", "head")
VMEM_LIMIT = 8 << 20
VMEM_FFN = 16 << 20
VMEM_ATTN = 10 << 20
FF_BLOCK = 768
FFN_BLOCK = 1024
FFN_STEPS = FF // FFN_BLOCK
MATMUL_PER_US = 1.15e9
COST_EXPAND = 1
VMEM_BACK = 16 << 20
COST_KEPT = 0.5
COST_BACK = 3
COST_SENT = 0.5
COST_HEADS = 0.1
COST_INPUT = 0.1
FF_STEPS = FF // FF_BLOCK


def dot(a, b):
    return jnp.dot(a, b, preferred_element_type=F32)


def dot_t(a, b):
    return lax.dot_general(a, b, (((0,), (0,)), ((), ())), preferred_element_type=F32)


def dot_r(a, b):
    return lax.dot_general(a, b, (((1,), (1,)), ((), ())), preferred_element_type=F32)


def call(kernel, name, scal, grid, ins, outs, scratch=(), us=0.1, vmem=VMEM_LIMIT):
    def spec(b, m):
        if b is None:
            return pl.BlockSpec(memory_space=pltpu.VMEM if m is None else m)
        return pl.BlockSpec(b, m)

    in_specs = [spec(b, m) for _, b, m in ins]
    out_specs = [spec(b, m) for _, _, b, m in outs]
    return pl.pallas_call(
        kernel,
        name=name,
        grid_spec=pltpu.PrefetchScalarGridSpec(
            num_scalar_prefetch=1,
            grid=grid,
            in_specs=in_specs,
            out_specs=out_specs,
            scratch_shapes=list(scratch),
        ),
        out_shape=[jax.ShapeDtypeStruct(s, d) for s, d, _, _ in outs],
        compiler_params=pltpu.CompilerParams(vmem_limit_bytes=vmem),
        cost_estimate=pl.CostEstimate(flops=int(us * MATMUL_PER_US), bytes_accessed=1, transcendentals=0),
    )(scal, *[a for a, _, _ in ins])


def lane_masks():
    lane = lax.broadcasted_iota(jnp.int32, (1, LANES), 1)
    even = (lane < HALF).astype(F32)
    return lane, even.astype(BF), (1.0 - even).astype(BF)


def both_heads(pair):
    lane, even, odd = lane_masks()
    return jnp.concatenate([pair * even, pair * odd], axis=0)


def own_lanes(stacked):
    rows = stacked.shape[0] // 2
    lane = lax.broadcasted_iota(jnp.int32, (1, LANES), 1)
    return jnp.where(lane < HALF, stacked[:rows], stacked[rows:])


def square_masks():
    row = lax.broadcasted_iota(jnp.int32, (LANES, LANES), 0)
    lane = lax.broadcasted_iota(jnp.int32, (LANES, LANES), 1)
    upper = row < HALF
    return lane, upper, upper == (lane < HALF)


def high_low(v):
    high = v.astype(BF).astype(F32)
    return high, v - high


def tables(scal, rows, seqs, tcol, trow):
    pos = lax.broadcasted_iota(jnp.int32, (1, rows), 1) + scal[seqs] * rows
    seg = jnp.zeros((1, rows), jnp.int32)
    first = jnp.zeros((1, rows), jnp.int32)
    length = jnp.ones((1, rows), jnp.int32)
    at_boundary = jnp.int32(0)
    begin = jnp.int32(0)
    for s in range(seqs):
        end = begin + scal[s]
        inside = (pos >= begin) & (pos < end)
        first = jnp.where(inside, begin, first)
        length = jnp.where(inside, jnp.maximum(scal[s], 1), length)
        seg = seg + (pos >= end).astype(jnp.int32)
        at_boundary = at_boundary + (rows - 1 >= end).astype(jnp.int32)
        begin = end
    live = (seg < seqs).astype(F32)
    angle = 0.5 * math.pi * (pos - first).astype(F32) / length.astype(F32)
    cos_w = jnp.cos(angle) * live
    sin_w = jnp.sin(angle) * live
    crossing = (seg == at_boundary).astype(F32)
    which = lax.broadcasted_iota(jnp.int32, (LANES, rows), 0)
    table = jnp.zeros((LANES, rows), F32)
    for n, entry in enumerate((cos_w, sin_w, seg.astype(F32), cos_w * crossing, sin_w * crossing)):
        table = jnp.where(which == n, entry, table)
    trow[...] = table[:8]
    tcol[...] = table.T


def pack_state(both, norm_cos, norm_sin, pair, norms):
    lane, upper, diag = square_masks()
    packed = jnp.where(diag, both[:LANES, :LANES], pltpu.roll(both[LANES:, :LANES], HALF, 1))
    cos_high, cos_low = high_low(norm_cos)
    sin_high, sin_low = high_low(norm_sin)
    for n, part in enumerate((cos_high, cos_low, sin_high, sin_low)):
        norms = jnp.where(lane == 4 * pair + n, part, norms)
    return packed.astype(BF), norms


def unpack_state(state_ref, pair):
    lane, upper, diag = square_masks()
    packed = state_ref[pair].astype(F32)
    norms = state_ref[PAIRS].astype(F32)
    of_cos = jnp.where(diag, packed, 0.0)
    of_sin = jnp.where(diag, pltpu.roll(packed, HALF, 1), 0.0)
    pick = lambda n: jnp.sum(
        jnp.where((lane == 4 * pair + n) | (lane == 4 * pair + n + 1), norms, 0.0), axis=1, keepdims=True
    )
    return of_cos, of_sin, pick(0), pick(2)


def turn(value, out):
    turned = value.T
    share = out.shape[1]
    for n in range(out.shape[0]):
        out[n] = turned[n * share : (n + 1) * share]


def kv_kernel(seqs, scal, tok, wk, wv, bk, bv, rk_o, v_o, st_o, tcol, trow, turned_o, norms):
    step = pl.program_id(0)
    rows = tok.shape[0]

    @pl.when(step == 0)
    def _():
        tables(scal, rows, seqs, tcol, trow)
        norms[...] = jnp.zeros_like(norms)
        turn(tok[...], turned_o)

    rk = jnp.maximum(dot(tok[...], wk[...]) + bk[...].astype(F32), 0.0).astype(BF)
    v = (dot(tok[...], wv[...]) + bv[...].astype(F32)).astype(BF)
    rk_o[...] = rk
    v_o[...] = v
    cos_b, sin_b = tcol[:, 3:4], tcol[:, 4:5]
    ones = jnp.ones((rows, LANES), BF)
    for n in range(2):
        pair = 2 * step + n
        cols = slice(n * LANES, (n + 1) * LANES)
        kp = rk[:, cols].astype(F32)
        left = jnp.concatenate([(kp * cos_b).astype(BF), (kp * sin_b).astype(BF)], axis=1)
        both = dot_t(left, jnp.concatenate([v[:, cols], ones], axis=1))
        packed, new_norms = pack_state(both, both[:LANES, LANES:], both[LANES:, LANES:], pair, norms[...])
        st_o[pair] = packed
        norms[...] = new_norms

    st_o[PAIRS] = norms[...].astype(BF)


def weights_block(tcol, trow, transposed):
    rows = tcol.shape[0]
    down = lax.broadcasted_iota(jnp.int32, (rows, rows), 0)
    along = lax.broadcasted_iota(jnp.int32, (rows, rows), 1)
    same = tcol[:, 2:3] == trow[2:3, :]
    causal = (down <= along) if transposed else (along <= down)
    value = tcol[:, 0:1] * trow[0:1, :] + tcol[:, 1:2] * trow[1:2, :]
    return jnp.where(same & causal, value, 0.0)


def weigh(stacked, weights):
    rows = weights.shape[0]
    return jnp.concatenate([stacked[:rows] * weights, stacked[rows:] * weights], axis=0).astype(BF)


def local_kernel(scal, tok, wq, bq, rk, v, tcol, trow, rq_o, num_o, den_o, weights):
    step = pl.program_id(0)
    rows = tok.shape[0]
    mid = rows // 2

    @pl.when(step == 0)
    def _():
        weights[...] = weights_block(tcol, trow, False)

    rq = jnp.maximum(dot(tok[...], wq[...]) + bq[...].astype(F32), 0.0).astype(BF)
    rq_o[...] = rq
    ones = jnp.ones((rows, LANES), BF)
    for n in range(2):
        cols = slice(n * LANES, (n + 1) * LANES)
        kp = rk[:, cols]
        values = jnp.concatenate([v[:, cols], ones], axis=1)
        first = weigh(dot_r(both_heads(rq[:, cols]), kp[:mid]), weights[:, :mid])
        second = weigh(dot_r(both_heads(rq[mid:, cols]), kp[mid:]), weights[mid:, mid:])
        sums = dot(first, values[:mid])
        late = dot(second, values[mid:])
        for own, out in ((slice(0, LANES), num_o), (slice(LANES, 2 * LANES), den_o)):
            total = own_lanes(sums[:, own])
            out[:mid, cols] = total[:mid]
            out[mid:, cols] = total[mid:] + own_lanes(late[:, own])


def normalise(entries):
    mean = jnp.mean(entries, axis=1, keepdims=True)
    centred = entries - mean
    var = jnp.mean(centred * centred, axis=1, keepdims=True)
    scale = lax.rsqrt(var + 1e-05)
    return centred * scale, scale


def merge_heads(
    head_at, scal, rq, num, den, st, tcol, tok, w_merge, b_merge, gain, bias, b_red,
    att_o, inv_o, mixed_o, xhat_o, scale_o, normed_o, acc_o, turned_o,
):
    cross = (scal[head_at] == 1).astype(F32)
    cos_b, sin_b = tcol[:, 3:4] * cross, tcol[:, 4:5] * cross
    sq_lane, upper, diag = square_masks()
    for pair in range(PAIRS):
        cols = slice(pair * LANES, (pair + 1) * LANES)
        qp = rq[:, cols].astype(F32)
        of_cos, of_sin, norm_cos, norm_sin = unpack_state(st, pair)
        top = jnp.concatenate([of_cos, jnp.where(diag, norm_cos, 0.0)], axis=1)
        low = jnp.concatenate([of_sin, jnp.where(diag, norm_sin, 0.0)], axis=1)
        right = jnp.concatenate([top, low], axis=0).astype(BF)
        left = jnp.concatenate([(qp * cos_b).astype(BF), (qp * sin_b).astype(BF)], axis=1)
        prior = dot(left, right)
        inverse = 1.0 / (den[:, cols] + prior[:, LANES:] + 1.0)
        attended = (num[:, cols] + prior[:, :LANES]) * inverse
        att_o[:, cols] = attended
        inv_o[:, cols] = inverse
        mixed_o[:, cols] = attended.astype(BF)
    first_in = tok[...].astype(F32) + dot(mixed_o[...], w_merge[...]) + b_merge[...].astype(F32)
    xhat, scale = normalise(first_in)
    normed = xhat * gain[...].astype(F32) + bias[...].astype(F32)
    xhat_o[...] = xhat
    scale_o[...] = jnp.broadcast_to(scale, scale_o.shape)
    normed_o[...] = normed.astype(BF)
    acc_o[...] = normed + b_red[...].astype(F32)
    turn(mixed_o[...], turned_o.at[0])
    turn(normed_o[...], turned_o.at[1])


def expand_reduce(normed, w_exp, b_exp, w_red, act_o, slope_o, acc_o):
    rows = normed.shape[0]
    pre = [dot(normed[at : at + rows // 2], w_exp[...]) + b_exp[...].astype(F32) for at in (0, rows // 2)]
    for at, x in zip((0, rows // 2), pre):
        part = slice(at, at + rows // 2)
        cdf = 0.5 + 0.5 * lax.erf(x * (2.0**-0.5))
        pdf = jnp.exp(-0.5 * x * x) * (1.0 / math.sqrt(2.0 * math.pi))
        act = (x * cdf).astype(BF)
        act_o[part] = act
        slope_o[part] = (cdf + x * pdf).astype(BF)
        acc_o[part] += dot(act, w_red[...])


def ffn_kernel(head_at, scal, *refs):
    w_exp, b_exp, w_red = refs[11:14]
    normed_o, acc_o = refs[19:21]
    act_o, slope_o = refs[22:]

    @pl.when(pl.program_id(0) == 0)
    def _():
        merge_heads(head_at, scal, *refs[:11], *refs[14:22])

    expand_reduce(normed_o, w_exp, b_exp, w_red, act_o, slope_o, acc_o)


def second_kernel(core_at, scal, second, cot, gain, bias, out_o, grad_o, full_o, keep_o, send_o, sums_o):
    xhat, scale = normalise(second[...])
    gain_w = gain[...].astype(F32)
    out_o[...] = (xhat * gain_w + bias[...].astype(F32)).astype(BF)
    cot_w = cot[...].astype(F32)
    t = cot_w * gain_w
    grad = scale * (
        t - jnp.mean(t, axis=1, keepdims=True) - xhat * jnp.mean(t * xhat, axis=1, keepdims=True)
    )
    low = grad.astype(BF)
    grad_o[...] = grad
    full_o[...] = low
    first = scal[core_at] == 0
    half = D // 2
    left, right = grad[:, :half], grad[:, half:]
    keep_o[...] = jnp.where(first, left, right).astype(BF)
    send_o[...] = jnp.where(first, right, left).astype(BF)
    sums_o[0:1] = jnp.sum(cot_w * xhat, axis=0, keepdims=True)
    sums_o[1:2] = jnp.sum(cot_w, axis=0, keepdims=True)
    sums_o[2:3] = jnp.sum(low.astype(F32), axis=0, keepdims=True)


def head_lanes(pair, lane, first):
    at = 4 * pair + jnp.where(first, 0, 2)
    return (lane == at) | (lane == at + 1)


def weight_copies(half, w_exp, w_red, exp_buf, red_buf, sems, n):
    at = pl.ds(pl.multiple_of((half * exp_buf.shape[0] + n) * FF_BLOCK, FF_BLOCK), FF_BLOCK)
    return (
        pltpu.make_async_copy(w_red.at[at, :], red_buf.at[n], sems.at[0, n]),
        pltpu.make_async_copy(w_exp.at[:, at], exp_buf.at[n], sems.at[1, n]),
    )


def back_steps(half, full, slope, w_exp, w_red, out_o, bexp_o, exp_buf, red_buf, sems):
    blocks = exp_buf.shape[0]
    copies = [weight_copies(half, w_exp, w_red, exp_buf, red_buf, sems, n) for n in range(blocks)]
    for pair in copies:
        for copy in pair:
            copy.start()
    total = None
    for n, (of_red, of_exp) in enumerate(copies):
        cols = slice(n * FF_BLOCK, (n + 1) * FF_BLOCK)
        at = pl.ds(pl.multiple_of((half * blocks + n) * FF_BLOCK, FF_BLOCK), FF_BLOCK)
        of_red.wait()
        pre_grad = (dot_r(full[...], red_buf[n]) * slope[:, at].astype(F32)).astype(BF)
        bexp_o[:, cols] = jnp.sum(pre_grad.astype(F32), axis=0, keepdims=True)
        out_o[n] = pre_grad
        of_exp.wait()
        part = dot_r(pre_grad, exp_buf[n])
        total = part if total is None else total + part
    return total


def back_sent_kernel(core_at, scal, full, slope, w_exp, w_red, grad2, sent_o, bexp_o, acc, exp_buf, red_buf, sems):
    half = 1 - scal[core_at]
    acc[...] = grad2[...] + back_steps(half, full, slope, w_exp, w_red, sent_o, bexp_o, exp_buf, red_buf, sems)


def back_kernel(
    core_at, scal, full, slope, w_exp, w_red, acc_in, gain, xhat, scale, w_merge, att, inv, rq, tcol,
    kept_o, first_o, mk_o, ms_o, w_o, e_o, st_o, bexp_o, sums_o,
    acc, exp_buf, red_buf, sems,
):
    half = scal[core_at]
    acc[...] = acc_in[...] + back_steps(half, full, slope, w_exp, w_red, kept_o, bexp_o, exp_buf, red_buf, sems)
    back_rest(
        core_at, scal, acc, gain, xhat, scale, w_merge, att, inv, rq, tcol,
        first_o, mk_o, ms_o, w_o, e_o, st_o, sums_o,
    )


def back_rest(
    core_at, scal, acc, gain, xhat, scale, w_merge, att, inv, rq, tcol,
    first_o, mk_o, ms_o, w_o, e_o, st_o, sums_o,
):
    grad_normed = acc[...]
    xh = xhat[...]
    t = grad_normed * gain[...].astype(F32)
    first = scale[:, 0:1] * (
        t - jnp.mean(t, axis=1, keepdims=True) - xh * jnp.mean(t * xh, axis=1, keepdims=True)
    )
    low = first.astype(BF)
    first_o[...] = first
    sums_o[0:1] = jnp.sum(grad_normed * xh, axis=0, keepdims=True)
    sums_o[1:2] = jnp.sum(grad_normed, axis=0, keepdims=True)
    sums_o[2:3] = jnp.sum(low.astype(F32), axis=0, keepdims=True)
    is_first = scal[core_at] == 0
    left, right = first[:, : D // 2], first[:, D // 2 :]
    mk_o[...] = jnp.where(is_first, left, right).astype(BF)
    ms_o[...] = jnp.where(is_first, right, left).astype(BF)
    cos_b, sin_b = tcol[:, 3:4], tcol[:, 4:5]
    w = (dot_r(low, w_merge[...]).astype(BF).astype(F32) * inv[...]).astype(BF)
    w_o[...] = w
    high, rest = high_low(w.astype(F32) * att[...])
    column = lax.broadcasted_iota(jnp.int32, (D, LANES), 0)
    target = lax.broadcasted_iota(jnp.int32, (D, LANES), 1)
    picks = (target == 2 * (column // HALF)).astype(F32).astype(BF)
    e_high, e_low = high_low(-(dot(high.astype(BF), picks) + dot(rest.astype(BF), picks)))
    e = (e_high + pltpu.roll(e_low, 1, 1)).astype(BF)
    e_o[...] = e
    norms = jnp.zeros((LANES, LANES), F32)
    sq_lane, upper, diag = square_masks()
    for pair in range(PAIRS):
        cols = slice(pair * LANES, (pair + 1) * LANES)
        qp = rq[:, cols].astype(F32)
        left = jnp.concatenate([(qp * cos_b).astype(BF), (qp * sin_b).astype(BF)], axis=1)
        both = dot_t(left, jnp.concatenate([w[:, cols], e], axis=1))
        mine = head_lanes(pair, sq_lane, upper)
        norm = lambda part: jnp.sum(jnp.where(mine, part, 0.0), axis=1, keepdims=True)
        packed, norms = pack_state(both, norm(both[:LANES, LANES:]), norm(both[LANES:, LANES:]), pair, norms)
        st_o[pair] = packed
    st_o[PAIRS] = norms.astype(BF)


def attn_sent_kernel(head_at, core_at, scal, rq, rk, v, w, e, prior, later, tcol, trow, early_o, late_o, sums_o, weights, weights_t):
    weights[...] = weights_block(tcol, trow, False)
    weights_t[...] = weights_block(tcol, trow, True)
    first = (1 - scal[core_at]) * (PAIRS // 2)
    attn_back(head_at, first, scal, rq, rk, v, w, e, prior, later, tcol, weights, weights_t, early_o, late_o, sums_o)


def attn_kept_kernel(head_at, core_at, scal, rq, rk, v, w, e, prior, later, tcol, weights, weights_t, early_o, late_o, sums_o):
    step = pl.program_id(0)
    attn_back_pair(
        head_at, scal[core_at] * (PAIRS // 2) + step, step,
        scal, rq, rk, v, w, e, prior, later, tcol, weights, weights_t, early_o, late_o, sums_o,
    )


def attn_back(head_at, first, scal, rq, rk, v, w, e, prior, later, tcol, weights, weights_t, early_o, late_o, sums_o):
    for n in range(PAIRS // 2):
        attn_back_pair(
            head_at, first + n, n, scal, rq, rk, v, w, e, prior, later, tcol, weights, weights_t, early_o, late_o, sums_o
        )


def attn_back_pair(
    head_at, pair, slot, scal, rq, rk, v, w, e, prior, later, tcol, weights, weights_t, early_o, late_o, sums_o
):
    rows = rq.shape[0]
    mid = rows // 2
    cols = pl.ds(pl.multiple_of(pair * LANES, LANES), LANES)
    out = pl.ds(pl.multiple_of(slot * LANES, LANES), LANES)

    qp, kp, vp, wp = rq[:, cols], rk[:, cols], v[:, cols], w[:, cols]
    lane, even, odd = lane_masks()
    of_even = ((lane == 4 * pair) | (lane == 4 * pair + 1)).astype(F32).astype(BF)
    of_odd = ((lane == 4 * pair + 2) | (lane == 4 * pair + 3)).astype(F32).astype(BF)
    ones = jnp.ones((rows, LANES), BF)
    we = jnp.concatenate([wp, e[...]], axis=1)
    by_head = (jnp.concatenate([even, of_even], axis=1), jnp.concatenate([odd, of_odd], axis=1))
    ve = jnp.concatenate([vp, ones], axis=1)
    stack = lambda a, lo, hi: jnp.concatenate([a[lo:hi] * m for m in by_head], axis=0)

    grads = weigh(dot_r(stack(we, 0, rows), ve[:mid]), weights[:, :mid])
    dq = own_lanes(dot(grads, kp[:mid]))
    grads = weigh(dot_r(stack(we, mid, rows), ve[mid:]), weights[mid:, mid:])
    dq_late = own_lanes(dot(grads, kp[mid:]))

    grads = weigh(dot_r(stack(ve, 0, rows), we[mid:]), weights_t[:, mid:])
    dk = own_lanes(dot(grads, qp[mid:]))
    grads = weigh(dot_r(stack(ve, 0, mid), we[:mid]), weights_t[:mid, :mid])
    dk_early = own_lanes(dot(grads, qp[:mid]))

    scores = weigh(dot_r(both_heads(kp), qp[mid:]), weights_t[:, mid:])
    dv = own_lanes(dot(scores, wp[mid:]))
    scores = weigh(dot_r(both_heads(kp[:mid]), qp[:mid]), weights_t[:mid, :mid])
    dv_early = own_lanes(dot(scores, wp[:mid]))

    dq = jnp.concatenate([dq[:mid], dq[mid:] + dq_late], axis=0)
    dk = jnp.concatenate([dk[:mid] + dk_early, dk[mid:]], axis=0)
    dv = jnp.concatenate([dv[:mid] + dv_early, dv[mid:]], axis=0)

    sq_lane, upper, diag = square_masks()
    cos_b, sin_b = tcol[:, 3:4], tcol[:, 4:5]
    is_late = (scal[head_at] == 1).astype(F32)
    early = 1.0 - is_late

    def with_norms(parts, where):
        side = lambda total, norm: jnp.concatenate([total, jnp.where(where, norm, 0.0)], axis=1)
        of_cos, of_sin, norm_cos, norm_sin = parts
        return jnp.concatenate([side(of_cos, norm_cos), side(of_sin, norm_sin)], axis=0).astype(BF)

    prior_parts = unpack_state(prior, pair)
    into = dot_r(we, with_norms(prior_parts, head_lanes(pair, sq_lane, upper)))
    dq = dq + is_late * (cos_b * into[:, :LANES] + sin_b * into[:, LANES:])
    later_parts = unpack_state(later, pair)
    into = dot_r(ve, with_norms(later_parts, sq_lane == 0))
    dk = dk + early * (cos_b * into[:, :LANES] + sin_b * into[:, LANES:])
    kw = kp.astype(F32)
    left = jnp.concatenate([(kw * (cos_b * early)).astype(BF), (kw * (sin_b * early)).astype(BF)], axis=1)
    dv = dv + dot(left, jnp.concatenate(later_parts[:2], axis=0).astype(BF))

    dq = jnp.where(qp.astype(F32) > 0, dq, 0.0).astype(BF)
    dk = jnp.where(kw > 0, dk, 0.0).astype(BF)
    dv = dv.astype(BF)
    for n, part in enumerate((dq, dk, dv)):
        total = jnp.sum(part.astype(F32), axis=0, keepdims=True)
        sums_o[n, :, out] = jnp.broadcast_to(total, (sums_o.shape[1], LANES))
        early_o[n, :, out] = part[:mid]
        late_o[n, :, out] = part[mid:]


def input_kernel(scal, first, keep_early, keep_late, send_early, send_late, w_keep, w_send, out_o):
    @pl.when(pl.program_id(0) == 0)
    def _():
        out_o[...] = first[...]

    rows = lambda early, late: jnp.concatenate([early[0], late[0]], axis=0)
    out_o[...] += dot_r(rows(keep_early, keep_late), w_keep[...]) + dot_r(rows(send_early, send_late), w_send[...])


def place(values, piece_rows, tz, tys, x, y, z, extra, outs):
    xk, xs, yk, ys = outs
    width = xk.shape[-1]
    slot_z = tz ^ z
    pieces = {}
    at = 0
    for ty in tys:
        for tc in range(2):
            for tx in range(2):
                part = values[at * piece_rows : (at + 1) * piece_rows]
                blocks = [part[:, n : n + width] for n in range(0, part.shape[1], width)]
                if extra is not None:
                    blocks.append(extra[at])
                pieces[ty, tc, tx] = jnp.concatenate(blocks, axis=0) if len(blocks) > 1 else blocks[0]
                at += 1
    for ty in tys:
        slot = ty ^ y
        a, b = pieces[ty, 0, 0], pieces[ty, 0, 1]
        xk[slot, slot_z] = jnp.where(x == 0, a, b).astype(BF)
        xs[slot, slot_z] = jnp.where(x == 0, b, a).astype(BF)
    return pieces


def place_y(pieces, tz, tys, x, y, z, outs):
    xk, xs, yk, ys = outs
    slot_z = tz ^ z
    for tx in range(2):
        slot = tx ^ x
        a, b = pieces[0, 1, tx], pieces[1, 1, tx]
        yk[slot, slot_z] = jnp.where(y == 0, a, b).astype(BF)
        ys[slot, slot_z] = jnp.where(y == 0, b, a).astype(BF)


def reduce_grad_kernel(pos_at, scal, a_own, a_oth, b_own, b_oth, kept, near):
    tz = pl.program_id(0)
    x, y, z = (scal[pos_at + n] for n in range(3))
    values = dot_t(a_own[...], b_own[...]) + dot_t(a_oth[...], b_oth[...])
    rows = values.shape[0] // 8
    slot = tz ^ z

    def put(out):
        for n in range(8):
            ty, tc, tx = n // 4, n // 2 % 2, n % 2
            out[slot // 2, tc, tx ^ x, ty ^ y] = values[n * rows : (n + 1) * rows].astype(BF)

    @pl.when(slot % 2 == 0)
    def _():
        put(kept)

    @pl.when(slot % 2 == 1)
    def _():
        put(near)


def expand_grad_kernel(pos_at, scal, a_own, a_oth, b_own, b_oth, m_own, m_oth, c_own, c_oth, *outs):
    tz = pl.program_id(0)
    x, y, z = (scal[pos_at + n] for n in range(3))
    an, ao = a_own[0, 0], a_oth[0, 0]
    parts = [dot(an, b_own[n]) + dot(ao, b_oth[n]) for n in range(b_own.shape[0])]
    parts.append(dot(m_own[0, 0], c_own[...]) + dot(m_oth[0, 0], c_oth[...]))
    values = jnp.concatenate(parts, axis=1)
    pieces = place(values, values.shape[0] // 8, tz, (0, 1), x, y, z, None, outs)
    place_y(pieces, tz, (0, 1), x, y, z, outs)


def share_lanes(entries, devices, at, width):
    n = entries.shape[1]
    share = n // devices
    owner = lax.broadcasted_iota(jnp.int32, (devices, n), 0)
    column = lax.broadcasted_iota(jnp.int32, (devices, n), 1)
    mine = (column >= owner * share) & (column < (owner + 1) * share)
    high, low = high_low(jnp.where(mine, entries, 0.0))
    both = jnp.concatenate([high, low], axis=0).astype(BF)
    source = lax.broadcasted_iota(jnp.int32, (n, width), 0)
    target = lax.broadcasted_iota(jnp.int32, (n, width), 1)
    picks = (target >= at) & (target < at + share) & (lax.rem(source, share) == target - at)
    spread = dot(both, picks.astype(F32).astype(BF))
    return spread[:devices] + spread[devices:]


def heads_grad_kernel(
    pos_at, scal, a_own, a_oth, own_early, own_late, oth_early, oth_late, kept_h, sent_h, sums_1, kept_e, sent_e, sums_2, *refs, devices
):
    outs, table = refs[:-1], refs[-1]
    tz = pl.program_id(0)
    x, y, z = (scal[pos_at + n] for n in range(3))
    width = outs[0].shape[-1]

    @pl.when(tz == 0)
    def _():
        first_core = scal[pos_at - 1] == 0
        ordered = lambda kept, sent: [jnp.where(first_core, kept, sent), jnp.where(first_core, sent, kept)]
        sums_e = jnp.concatenate(ordered(kept_e[...], sent_e[...]), axis=1)
        of_heads = [part for n in range(3) for part in ordered(kept_h[n, 0:1], sent_h[n, 0:1])]
        total = jnp.zeros((devices, width), F32)
        at = 0
        for entries in (
            jnp.concatenate(of_heads[:4], axis=1), jnp.concatenate(of_heads[4:], axis=1), sums_1[2:3], sums_1[0:1], sums_1[1:2],
            sums_e, sums_2[2:3], sums_2[0:1], sums_2[1:2],
        ):
            total = total + share_lanes(entries, devices, at, width)
            at += entries.shape[1] // devices
        table[...] = total

    join = lambda early, late: jnp.concatenate(
        [jnp.concatenate([early[n], late[n]], axis=0) for n in range(early.shape[0])], axis=1
    )
    values = dot(a_own[0], join(own_early, own_late)) + dot(a_oth[0], join(oth_early, oth_late))
    line = lax.broadcasted_iota(jnp.int32, (8, width), 0)
    rows8 = table[pl.ds(pl.multiple_of(tz * 8, 8), 8)]
    extra = []
    for n in range(8):
        high, low = high_low(rows8[n : n + 1])
        extra.append(jnp.where(line == 0, high, jnp.where(line == 1, low, 0.0)))
    pieces = place(values, values.shape[0] // 8, tz, (0, 1), x, y, z, extra, outs)
    place_y(pieces, tz, (0, 1), x, y, z, outs)


class Ring:
    def __init__(self, n_dp):
        self.n_dp = n_dp
        self.devices = 2 * n_dp

    def swap(self, value, bits):
        return lax.ppermute(value, AXES, [(i, i ^ bits) for i in range(self.devices)])

    def core(self, value):
        return self.swap(value, 2)

    def x(self, value):
        return self.swap(value, 1)

    def y(self, value):
        return self.swap(value, 4)

    def z(self, value, step):
        return self.swap(value, 8 * step)


def add_first_kernel(scal, xk, xr, yk, yr, xn, yn):
    wide = lambda ref: ref[0].astype(F32)
    xn[...] = (wide(xk) + wide(xr)).astype(BF)
    yn[...] = (wide(yk) + wide(yr)).astype(BF)


def add_second_kernel(scal, xk, xr, xm, yk, yr, ym, own, z1, z2, z3):
    for n, (keep, got, more) in enumerate(((xk, xr, xm), (yk, yr, ym))):
        total = lambda k: keep[0, k].astype(F32) + got[0, k].astype(F32) + more[k].astype(F32)
        own[n] = total(0)
        for k, out in ((1, z1), (2, z2), (3, z3)):
            out[n] = total(k).astype(BF)


def add_last_kernel(core_at, scal, own, z1, z2, z3, keep, send):
    first = scal[core_at] == 0
    total = lambda n: own[n] + z1[n].astype(F32) + z2[n].astype(F32) + z3[n].astype(F32)
    of_first, of_second = total(0), total(1)
    keep[...] = jnp.where(first, of_first, of_second)
    send[...] = jnp.where(first, of_second, of_first)


def add_second_half_kernel(scal, xk, xr, xm, yk, yr, ym, kept, sent):
    for n, (keep, got, more) in enumerate(((xk, xr, xm), (yk, yr, ym))):
        total = lambda k: keep[0, k].astype(F32) + got[0, k].astype(F32) + more[k].astype(F32)
        for k in range(2):
            kept[k, n] = total(2 * k)
            sent[k, n] = total(2 * k + 1).astype(BF)


def add_third_half_kernel(scal, kept, got, own, sent):
    own[...] = kept[0] + got[0].astype(F32)
    sent[...] = (kept[1] + got[1].astype(F32)).astype(BF)


def add_last_half_kernel(core_at, scal, own, got, keep, send):
    first = scal[core_at] == 0
    of_first, of_second = (own[n] + got[n].astype(F32) for n in range(2))
    keep[...] = jnp.where(first, of_first, of_second)
    send[...] = jnp.where(first, of_second, of_first)


def add_near_kernel(scal, kept, got, own, far):
    own[...] = kept[0].astype(F32) + got[0].astype(F32)
    far[...] = (kept[1].astype(F32) + got[1].astype(F32)).astype(BF)


def add_far_kernel(scal, own, got, kept, sent):
    for n in range(2):
        kept[n] = own[n, 0] + got[n, 0].astype(F32)
        sent[n] = (own[n, 1] + got[n, 1].astype(F32)).astype(BF)


def add_side_kernel(scal, kept, got, own, sent):
    for n in range(2):
        own[n] = kept[n, 0] + got[n, 0].astype(F32)
        sent[n] = (kept[n, 1] + got[n, 1].astype(F32)).astype(BF)


def add_end_kernel(core_at, scal, own, got, keep, send):
    first = scal[core_at] == 0
    of_first, of_second = (own[n] + got[n].astype(F32) for n in range(2))
    keep[...] = jnp.where(first, of_first, of_second)
    send[...] = jnp.where(first, of_second, of_first)


class Scatter:
    def __init__(self, ring, core_at, name, sent):
        self.ring, self.core_at, self.name = ring, core_at, name
        self.xk, self.xs, self.yk, self.ys = sent

    def send(self, *others):
        self.xr, self.yr = self.ring.x(after(self.xs, *others)), self.ring.y(after(self.ys, *others))

    def first(self, scal, us=0.1):
        shape = self.xk.shape[1:]
        part = lambda a: (a, (1,) + shape, lambda j, s: (1, 0, 0, 0))
        xn, yn = call(
            add_first_kernel, self.name + "_add1", scal, (1,), [part(a) for a in (self.xk, self.xr, self.yk, self.yr)],
            [(shape, BF, None, None)] * 2, us=us,
        )
        self.xn, self.yn = xn, yn
        return xn

    def send_first(self, *others):
        self.xm, self.ym = self.ring.y(after(self.xn, *others)), self.ring.x(after(self.yn, *others))

    def second(self, scal):
        shape = self.xk.shape[1:]
        piece = (2,) + shape[1:]
        part = lambda a: (a, (1,) + shape, lambda j, s: (0, 0, 0, 0))
        whole = lambda a: (a, None, None)
        self.own, *self.sends = call(
            add_second_kernel, self.name + "_add2", scal, (1,),
            [part(self.xk), part(self.xr), whole(self.xm), part(self.yk), part(self.yr), whole(self.ym)],
            [(piece, F32, None, None)] + [(piece, BF, None, None)] * 3,
        )
        return self.own

    def send_second(self, *others):
        self.arrived = [self.ring.z(after(v, *others), k + 1) for k, v in enumerate(self.sends)]

    def last(self, scal):
        piece = self.own.shape[1:]
        keep, send = call(
            functools.partial(add_last_kernel, self.core_at), self.name + "_add3", scal, (1,),
            [(a, None, None) for a in (self.own, *self.arrived)], [(piece, F32, None, None)] * 2,
        )
        return keep, self.ring.core(send)


class HalvingScatter(Scatter):
    def second(self, scal):
        shape = self.xk.shape[1:]
        piece = (2, 2) + shape[1:]
        part = lambda a: (a, (1,) + shape, lambda j, s: (0, 0, 0, 0))
        whole = lambda a: (a, None, None)
        self.kept, self.near = call(
            add_second_half_kernel, self.name + "_add2", scal, (1,),
            [part(self.xk), part(self.xr), whole(self.xm), part(self.yk), part(self.yr), whole(self.ym)],
            [(piece, F32, None, None), (piece, BF, None, None)],
        )
        return self.kept

    def send_second(self):
        self.got = self.ring.z(self.near, 1)

    def third(self, scal):
        piece = self.kept.shape[1:]
        self.own, self.far = call(
            add_third_half_kernel, self.name + "_add3", scal, (1,),
            [(a, None, None) for a in (self.kept, self.got)], [(piece, F32, None, None), (piece, BF, None, None)],
        )
        return self.own

    def send_third(self):
        self.arrived = self.ring.z(self.far, 2)

    def last(self, scal):
        piece = self.own.shape[1:]
        keep, send = call(
            functools.partial(add_last_half_kernel, self.core_at), self.name + "_add4", scal, (1,),
            [(a, None, None) for a in (self.own, self.arrived)], [(piece, F32, None, None)] * 2,
        )
        return keep, self.ring.core(send)


class DepthScatter:
    def __init__(self, ring, core_at, name, sent):
        self.ring, self.core_at, self.name = ring, core_at, name
        self.kept, self.near = sent

    def call(self, kernel, step, scal, ins, outs):
        whole = lambda a: (a, None, None)
        return call(kernel, self.name + step, scal, (), [*map(whole, ins)], [(s, d, None, None) for s, d in outs])

    def send_near(self):
        self.got = self.ring.z(self.near, 1)

    def add_near(self, scal):
        shape = self.kept.shape[1:]
        self.own, self.far = self.call(add_near_kernel, "_add1", scal, (self.kept, self.got), [(shape, F32), (shape, BF)])
        return self.own

    def send_far(self):
        self.got = self.ring.z(self.far, 2)

    def add_far(self, scal):
        shape = self.own.shape[:1] + self.own.shape[2:]
        self.kept, self.side = self.call(add_far_kernel, "_add2", scal, (self.own, self.got), [(shape, F32), (shape, BF)])
        return self.kept

    def send_side(self):
        self.got = self.ring.x(self.side)

    def add_side(self, scal):
        shape = self.kept.shape[:1] + self.kept.shape[2:]
        self.own, sent = self.call(add_side_kernel, "_add3", scal, (self.kept, self.got), [(shape, F32), (shape, BF)])
        self.got = self.ring.y(sent)
        return self.own

    def last(self, scal):
        shape = self.own.shape[1:]
        keep, send = self.call(
            functools.partial(add_end_kernel, self.core_at), "_add4", scal, (self.own, self.got), [(shape, F32)] * 2
        )
        return keep, self.ring.core(send)


def after(value, *others):
    if not others:
        return value
    return lax.optimization_barrier((value,) + others)[0]


def side_by_side(core_at, scal, own, got):
    first = scal[core_at] == 0
    return [jnp.where(first, own, got), jnp.where(first, got, own)]


def finish_kernel(
    core_at, scal, own, got, reduce_own, reduce_got, expand_own, expand_got,
    heads_o, reduce_o, expand_o, merge_o, *shares_o,
):
    width = own.shape[1]
    rows = heads_o.shape[0]
    for n, part in enumerate(side_by_side(core_at, scal, reduce_own[...], reduce_got[...])):
        reduce_o[:, n * width : (n + 1) * width] = part
    blocks = expand_own.shape[0] // rows - 1
    for n, part in enumerate(side_by_side(core_at, scal, expand_own[...], expand_got[...])):
        for k in range(blocks):
            at = (n * blocks + k) * width
            expand_o[:, at : at + width] = part[k * rows : (k + 1) * rows]
        merge_o[:, n * width : (n + 1) * width] = part[blocks * rows :]
    for n, part in enumerate(side_by_side(core_at, scal, own[...], got[...])):
        for k in range(3):
            at = (2 * k + n) * width
            heads_o[:, at : at + width] = part[k * rows : (k + 1) * rows]
    entries = own[3 * rows :] + got[3 * rows :]
    entries = entries[0:1] + entries[1:2]
    at = 0
    for share in shares_o:
        n = share.shape[1]
        moved = entries if at == 0 else pltpu.roll(entries, width - at, 1)
        share[...] = moved[:, :n]
        at += n


def per_device(
    tokens, w_heads, b_heads, w_merge, b_merge, gain_first, bias_first, w_expand, b_expand,
    w_reduce, b_reduce, gain_second, bias_second, seq_lengths, cotangent,
):
    rows = tokens.shape[0]
    seqs = seq_lengths.shape[1]
    n_dp = lax.axis_size("dp")
    ring = Ring(n_dp)
    head = lax.axis_index("head")
    dp = lax.axis_index("dp")
    core = dp % 2
    place_of = jnp.stack([head, core, head, (dp // 2) % 2, dp // 4]).astype(jnp.int32)
    scal = jnp.concatenate([seq_lengths[0].astype(jnp.int32), place_of])
    head_at, core_at, pos_at = seqs, seqs + 1, seqs + 2
    first_core = core == 0
    line = lambda v: v.reshape(1, -1)
    b_heads, b_merge, gain_first, bias_first, b_expand, b_reduce, gain_second, bias_second = map(
        line, (b_heads, b_merge, gain_first, bias_first, b_expand, b_reduce, gain_second, bias_second)
    )
    wide_shape = (rows, D)
    quarter = 256

    turned = ((4, D // 4, rows), BF, None, None)
    rk, v, state, tcol, trow, tokens_t = call(
        functools.partial(kv_kernel, seqs), "keys_values", scal, (3,),
        [
            (tokens, None, None),
            (w_heads, (D, quarter), lambda j, s: (0, 3 + j)),
            (w_heads, (D, quarter), lambda j, s: (0, 6 + j)),
            (b_heads, (1, quarter), lambda j, s: (0, 3 + j)),
            (b_heads, (1, quarter), lambda j, s: (0, 6 + j)),
        ],
        [
            (wide_shape, BF, (rows, quarter), lambda j, s: (0, j)),
            (wide_shape, BF, (rows, quarter), lambda j, s: (0, j)),
            ((PAIRS + 1, LANES, LANES), BF, None, None),
            ((rows, LANES), F32, None, None),
            ((8, rows), F32, None, None), turned,
        ],
        [pltpu.VMEM((LANES, LANES), F32)],
        us=4,
    )
    prior = ring.x(state)

    fast = n_dp == 16
    order = scal
    if fast:
        tokens_o = ring.core(tokens_t)
    rq, num, den = call(
        local_kernel, "local_attention", scal, (3,),
        [
            (tokens, None, None),
            (w_heads, (D, quarter), lambda j, s: (0, j)),
            (b_heads, (1, quarter), lambda j, s: (0, j)),
            (rk, (rows, quarter), lambda j, s: (0, j)),
            (v, (rows, quarter), lambda j, s: (0, j)),
            (tcol, None, None),
            (trow, None, None),
        ],
        [
            (wide_shape, BF, (rows, quarter), lambda j, s: (0, j)),
            (wide_shape, F32, (rows, quarter), lambda j, s: (0, j)),
            (wide_shape, F32, (rows, quarter), lambda j, s: (0, j)),
        ],
        [pltpu.VMEM((rows, rows), F32)],
        us=6,
    )

    if fast:
        order = after(scal, tokens_o)
    att, inv, mixed, xhat, scale, normed, second, turned_own, act, slope = call(
        functools.partial(ffn_kernel, head_at), "feed_forward", order, (FFN_STEPS,),
        [
            (rq, None, None), (num, None, None), (den, None, None), (prior, None, None),
            (tcol, None, None), (tokens, None, None), (w_merge, None, None), (b_merge, None, None),
            (gain_first, None, None), (bias_first, None, None), (b_reduce, None, None),
            (w_expand, (D, FFN_BLOCK), lambda j, s: (0, j)),
            (b_expand, (1, FFN_BLOCK), lambda j, s: (0, j)),
            (w_reduce, (FFN_BLOCK, D), lambda j, s: (j, 0)),
        ],
        [
            (wide_shape, F32, None, None), (wide_shape, F32, None, None), (wide_shape, BF, None, None),
            (wide_shape, F32, None, None), ((rows, LANES), F32, None, None), (wide_shape, BF, None, None),
            (wide_shape, F32, None, None), ((2, 4, D // 4, rows), BF, None, None),
            ((rows, FF), BF, (rows, FFN_BLOCK), lambda j, s: (0, j)),
            ((rows, FF), BF, (rows, FFN_BLOCK), lambda j, s: (0, j)),
        ],
        us=11, vmem=VMEM_FFN,
    )

    half_shape = (rows, D // 2)
    result, grad_second, branch, bg_keep, bg_send, sums_second = call(
        functools.partial(second_kernel, core_at), "second_norm", scal, (1,),
        [(second, None, None), (cotangent, None, None), (gain_second, None, None), (bias_second, None, None)],
        [
            (wide_shape, BF, None, None), (wide_shape, F32, None, None), (wide_shape, BF, None, None),
            (half_shape, BF, None, None), (half_shape, BF, None, None), ((8, D), F32, None, None),
        ],
        us=2.6,
    )

    devices = ring.devices
    small, large = D // devices, FF // devices
    whole = lambda a: (a, None, None)
    part = lambda a, n: (a, (1, 1, D // 4, rows), lambda j, s: (n, j, 0, 0))
    by_z = lambda a: (a, (1, D // 4, rows), lambda j, s: (j, 0, 0))
    by_col = lambda a: (a, (rows, FF // 4), lambda j, s: (0, j))

    def group(kernel, name, scal, grid, ins, piece_rows, us, scratch=(), kind=Scatter):
        shape = (2, 4, piece_rows, D // 2)
        sent = call(
            functools.partial(kernel, pos_at), name, scal, grid, ins, [(shape, BF, None, None)] * 4, scratch, us
        )
        return kind(ring, core_at, name, sent)

    ff_half = FF_STEPS // 2
    in_hbm = lambda a: (a, None, pltpu.HBM)
    hidden = ((ff_half, rows, FF_BLOCK), BF, None, None)
    hidden_sums = ((1, FF // 2), F32, None, None)
    buffers = [
        pltpu.VMEM((ff_half, D, FF_BLOCK), BF), pltpu.VMEM((ff_half, FF_BLOCK, D), BF),
        pltpu.SemaphoreType.DMA((2, ff_half)),
    ]
    hidden_in = [whole(branch), whole(slope), in_hbm(w_expand), in_hbm(w_reduce)]
    pg_send, sum_sent, partial = call(
        functools.partial(back_sent_kernel, core_at), "feed_forward_back_sent", scal, (),
        [*hidden_in, whole(grad_second)],
        [hidden, hidden_sums, (wide_shape, F32, None, None)], buffers,
        us=5, vmem=VMEM_BACK,
    )
    order = scal
    if fast:
        pg_o = ring.core(pg_send)
        act_o, turned_other, bg_o = map(ring.core, (act, turned_own, bg_send))
        pieces = ((2, 2, 2, 2, large, D // 2), BF, None, None)
        sent = call(
            functools.partial(reduce_grad_kernel, pos_at), "grad_reduce", after(scal, partial, turned_other), (4,),
            [by_col(act), by_col(act_o), whole(bg_keep), whole(bg_o)], [pieces, pieces], us=6,
        )
        reduced = DepthScatter(ring, core_at, "grad_reduce", sent)
        reduced.send_near()
        order = after(scal, reduced.near)

    pg_keep, grad_first, mg_keep, mg_send, w_att, e_att, later, sum_kept, sums_first = call(
        functools.partial(back_kernel, core_at), "feed_forward_back", order, (),
        [
            *hidden_in,
            (partial, None, None), (gain_first, None, None), (xhat, None, None), (scale, None, None),
            (w_merge, None, None), (att, None, None), (inv, None, None), (rq, None, None), (tcol, None, None),
        ],
        [
            hidden, (wide_shape, F32, None, None), (half_shape, BF, None, None), (half_shape, BF, None, None),
            (wide_shape, BF, None, None), ((rows, LANES), BF, None, None),
            ((PAIRS + 1, LANES, LANES), BF, None, None), hidden_sums, ((8, D), F32, None, None),
        ],
        [pltpu.VMEM(wide_shape, F32), *buffers],
        us=COST_BACK, vmem=VMEM_BACK,
    )
    later = ring.x(later)

    if fast:
        mg_o = ring.core(mg_send)
        expanded = group(
            expand_grad_kernel, "grad_expand", scal, (4,),
            [
                part(turned_own, 1), part(turned_other, 1), whole(pg_keep), whole(pg_o),
                part(turned_own, 0), part(turned_other, 0), whole(mg_keep), whole(mg_o),
            ],
            5 * small, COST_EXPAND, kind=HalvingScatter,
        )
        expanded.send(later)
        order = after(scal, expanded.xs, later)

    by_pair = [*map(whole, (rq, rk, v, w_att))]
    both_states = [whole(e_att), whole(prior), whole(later), whole(tcol)]
    pj_out = [((3, rows // 2, D // 2), BF, None, None)] * 2
    pj_sums = ((3, 8, D // 2), F32, None, None)
    table = ((rows, rows), F32, None, None)
    *pj_send, sum_heads_sent, weights, weights_t = call(
        functools.partial(attn_sent_kernel, head_at, core_at), "attention_back_sent", order, (),
        [*by_pair, *both_states, whole(trow)], [*pj_out, pj_sums, table, table], us=COST_SENT, vmem=VMEM_ATTN,
    )
    order = scal
    if fast:
        pj_o = [ring.core(v) for v in pj_send]
        order = after(scal, reduced.add_near(after(scal, pj_send[0])))
        reduced.send_far()
    *pj_keep, sum_heads_kept = call(
        functools.partial(attn_kept_kernel, head_at, core_at), "attention_back_kept", order, (PAIRS // 2,),
        [*by_pair, *both_states, whole(weights), whole(weights_t)], [*pj_out, pj_sums], us=COST_KEPT, vmem=VMEM_ATTN,
    )

    if fast:
        order = after(scal, expanded.first(after(scal, pj_keep[0])))
        expanded.send_first()
        heads = group(
            functools.partial(heads_grad_kernel, devices=devices), "grad_heads", order, (4,),
            [
                by_z(tokens_t), by_z(tokens_o), *map(whole, (*pj_keep, *pj_o)),
                *map(whole, (sum_heads_kept, sum_heads_sent, sums_first, sum_kept, sum_sent, sums_second)),
            ],
            3 * small + 8, COST_HEADS, [pltpu.VMEM((devices, D // 2), F32)],
        )
        heads.send()
        order = after(scal, heads.xs)

    of_part = lambda a: (a, (1, rows // 2, D // 2), lambda j, s: (j, 0, 0))
    (input_grad,) = call(
        input_kernel, "input_grad", order, (3,),
        [
            whole(grad_first), *map(of_part, (*pj_keep, *pj_send)),
            (w_heads, (D, D // 2), lambda j, s: (0, 2 * j + s[core_at])),
            (w_heads, (D, D // 2), lambda j, s: (0, 2 * j + 1 - s[core_at])),
        ],
        [(wide_shape, F32, None, None)],
        us=COST_INPUT,
    )

    if fast:
        order = reduced.add_far(after(scal, input_grad))
        order = expanded.second(after(scal, order))
        expanded.send_second()
        reduced.send_side()
        order = heads.first(after(scal, order))
        heads.send_first()
        order = expanded.third(after(scal, order))
        expanded.send_third()
        order = heads.second(after(scal, order))
        heads.send_second()
        order = reduced.add_side(after(scal, order))
        expand_own, expand_got = expanded.last(after(scal, order))
        reduce_own, reduce_got = reduced.last(after(scal, expand_own))
        heads_own, heads_got = heads.last(after(scal, reduce_own))
        out = lambda n, m: ((n, m), F32, None, None)
        counts = (2 * small, small, small, small, small, large, small, small, small)
        w_heads_grad, w_reduce_grad, w_expand_grad, w_merge_grad, *shares = call(
            functools.partial(finish_kernel, core_at), "finish", scal, (),
            [*map(whole, (heads_own, heads_got, reduce_own, reduce_got, expand_own, expand_got))],
            [out(small, 3 * D), out(large, D), out(small, FF), out(small, D), *(out(1, n) for n in counts)],
        )
        shares = [share.reshape(-1) for share in shares]
        grads = (
            w_heads_grad, *shares[:2], w_merge_grad, *shares[2:5], w_expand_grad, shares[5], w_reduce_grad,
            *shares[6:],
        )
    else:
        by_core = lambda keep, send: jnp.concatenate(
            [jnp.where(first_core, keep, send), jnp.where(first_core, send, keep)], axis=1
        )
        flat = lambda v: v.transpose(1, 0, 2).reshape(rows, -1)
        by_heads = lambda keep, send: jnp.concatenate(
            [by_core(keep[n], send[n]) for n in range(3)], axis=1
        )
        pj_keep, pj_send = (jnp.concatenate(v, axis=1) for v in (pj_keep, pj_send))
        sum_heads = by_heads(sum_heads_kept, sum_heads_sent)[0]
        scatter = lambda v: lax.psum_scatter(v, AXES, scatter_dimension=0, tiled=True)
        grads = (
            scatter(dot_t(tokens, by_heads(pj_keep, pj_send))),
            scatter(sum_heads[: 2 * D]), scatter(sum_heads[2 * D :]),
            scatter(dot_t(mixed, by_core(mg_keep, mg_send))),
            scatter(sums_first[2]), scatter(sums_first[0]), scatter(sums_first[1]),
            scatter(dot_t(normed, by_core(flat(pg_keep), flat(pg_send)))),
            scatter(by_core(sum_kept, sum_sent)[0]),
            scatter(dot_t(act, branch)),
            scatter(sums_second[2]), scatter(sums_second[0]), scatter(sums_second[1]),
        )
    return (result, input_grad) + tuple(grads)


def solution(mesh):
    in_specs = (P(AXES, None),) + (P(),) * 12 + (P("dp", None), P(AXES, None))
    row, one = P(AXES, None), P(AXES)
    out_specs = (row, row, row, one, one, row, one, one, one, row, one, row, one, one, one)
    return jax.shard_map(
        per_device, mesh=mesh, in_specs=in_specs, out_specs=out_specs, check_vma=False
    )
```

profile of v0, /device:TPU:0, one launch (start us, length us, event | category | flops | bytes accessed | tf_op | source)
XLA Modules:
  0.0 136.9 jit_solution(1542061327909150806)
XLA Ops:
  0.7 0.7 reshape.81.bk.bv.bq
  1.4 0.7 concatenate.3.scal
  2.1 2.0 %copy-done = bf16[768,2304]{1,0:T(8,128)(2,1)S(1)} copy-done((bf16[768,2304]{1,0:T(8,128)(2,1)S(1)}, bf16[768,2304]{1,0:T(8,128)(2,1)}, u32[]{:S(2)}) %copy-start) | copy-done | bytes 3538968
  4.1 1.1 copy-done.3
  5.3 4.1 %keys_values.1 = (bf16[512,768]{1,0:T(8,128)(2,1)S(1)}, bf16[512,768]{1,0:T(8,128)(2,1)S(1)}, bf16[7,128,128]{2,1,0:T(8,128)(2,1)S(1)}, f32[512,128]{1,0:T(8,128...) custom-call(s32[9]{0:T(128)S(1)} %concatenate.3.scal, bf16[512,768]{1,0:T(8,128)(2,1)S(1)} %copy-done.3, ...), custom_call_target="tpu_custom_call" | custom-call | flops 4600000000 | bytes 1 | tf_op jit(solution)/shard_map/keys_values/pallas_call | solution.py:56
  9.9 2.6 %collective-permute-start.1 = (bf16[7,128,128]{2,1,0:T(8,128)(2,1)S(1)}, bf16[7,128,128]{2,1,0:T(8,128)(2,1)S(1)}, u32[]{:S(2)}, u32[]{:S(2)}) collective-permute-start(bf16[7,128,128]{2,1,0:T(8,128)(2,1)S(1)} %get-tuple-element.134), channel_id=1, source_target_pairs={{0,1},{1,0},{2,3},{3,2},{4,5},{5,4},{6,7},{7,6},{8,9},{9,8},{10,11... | collective-permute-start | bytes 688136 | tf_op jit(solution)/shard_map/ppermute | solution.py:631
  12.5 5.7 %local_attention.1 = (bf16[512,768]{1,0:T(8,128)(2,1)S(1)}, f32[512,768]{1,0:T(8,128)S(1)}, f32[512,768]{1,0:T(8,128)S(1)}) custom-call(s32[9]{0:T(128)S(1)} %concatenate.3.scal, bf16[512,768]{1,0:T(8,128)(2,1)S(1)} %copy-done.3, bf16[768,2304]{1,0:T(8,128)(2,1)S(1)} %copy-done, bf16[1,2304]{1,0:T(2,128)(2,1)S(1)} %reshape.81.bk.bv.bq, ...), custom_call_target="tpu_custom_call" | custom-call | flops 6899999744 | bytes 1 | tf_op jit(solution)/shard_map/local_attention/pallas_call | solution.py:56
  18.7 10.3 %feed_forward.1 = (f32[512,768]{1,0:T(8,128)S(1)}, f32[512,768]{1,0:T(8,128)S(1)}, bf16[512,768]{1,0:T(8,128)(2,1)}, f32[512,768]{1,0:T(8,128)S(1)}, f32[512,128...) custom-call(s32[9]{0:T(128)S(1)} %concatenate.3.scal, ...), custom_call_target="tpu_custom_call" | custom-call | flops 12650000384 | bytes 1 | tf_op jit(solution)/shard_map/feed_forward/pallas_call | solution.py:56
  29.6 2.6 %second_norm.1 = (bf16[512,768]{1,0:T(8,128)(2,1)}, f32[512,768]{1,0:T(8,128)S(1)}, bf16[512,768]{1,0:T(8,128)(2,1)S(1)}, bf16[512,384]{1,0:T(8,128)(2,1)S(1)}, ...) custom-call(s32[9]{0:T(128)S(1)} %concatenate.3.scal, f32[512,768]{1,0:T(8,128)S(1)} %get-tuple-element.135.second, ...), custom_call_target="tpu_custom_call" | custom-call | flops 2990000128 | bytes 1 | tf_op jit(solution)/shard_map/second_norm/pallas_call | solution.py:56
  32.2 5.6 %feed_forward_back_sent.1 = (bf16[2,512,768]{2,1,0:T(8,128)(2,1)S(1)}, f32[1,1536]{1,0:T(1,128)S(1)}, f32[512,768]{1,0:T(8,128)S(1)}) custom-call(s32[9]{0:T(128)S(1)} %concatenate.3.scal, bf16[512,768]{1,0:T(8,128)(2,1)S(1)} %get-tuple-element.138.full, bf16[512,3072]{1,0:T(8,128)(2,1)S(1)} %get-tuple-element.139.slope, bf16[768,3072]{1,0:T(8,128)(2,1)S(1)} %bitcast.15, ...), custom_call_target="tpu_custom_call" | custom-call | flops 5750000128 | bytes 1 | tf_op jit(solution)/shard_map/feed_forward_back_sent/pallas_call | solution.py:56
  38.4 5.4 %grad_reduce.1 = (bf16[2,2,2,2,96,384]{5,4,3,2,1,0:T(8,128)(2,1)S(1)}, bf16[2,2,2,2,96,384]{5,4,3,2,1,0:T(8,128)(2,1)S(1)}) custom-call(s32[9]{0:T(128)S(1)} %concatenate.3.scal, bf16[512,3072]{1,0:T(8,128)(2,1)S(1)} %get-tuple-element.143.a_own, bf16[512,3072]{1,0:T(8,128)(2,1)S(1)} %collective-permute-done.3.a_oth, ...), custom_call_target="tpu_custom_call" | custom-call | flops 6899999744 | bytes 1 | tf_op jit(solution)/shard_map/grad_reduce/pallas_call | solution.py:56
  43.8 1.9 %collective-permute-start.8 = (bf16[2,2,2,2,96,384]{5,4,3,2,1,0:T(8,128)(2,1)S(1)}, bf16[2,2,2,2,96,384]{5,4,3,2,1,0:T(8,128)(2,1)S(1)}, u32[]{:S(2)}, u32[]{:S(2)}) collective-permute-start(bf16[2,2,2,2,96,384]{5,4,3,2,1,0:T(8,128)(2,1)S(1)} %get-tuple-element.146), channel_id=1, source_target_pairs={{0,8},{1,9},{2,10},{3,11},{4,12},{5,13},{6,14},{7,15},{8,0},{9,1},... | collective-permute-start | bytes 3538952 | tf_op jit(solution)/shard_map/ppermute | solution.py:631
  45.7 8.7 %feed_forward_back.1 = (bf16[2,512,768]{2,1,0:T(8,128)(2,1)S(1)}, f32[512,768]{1,0:T(8,128)S(1)}, bf16[512,384]{1,0:T(8,128)(2,1)S(1)}, bf16[512,384]{1,0:T(8,12...) custom-call(s32[9]{0:T(128)S(1)} %concatenate.3.scal, ...), custom_call_target="tpu_custom_call" | custom-call | flops 3449999872 | bytes 1 | tf_op jit(solution)/shard_map/feed_forward_back/pallas_call | solution.py:56
  54.5 1.6 %collective-permute-start.7 = (bf16[7,128,128]{2,1,0:T(8,128)(2,1)S(1)}, bf16[7,128,128]{2,1,0:T(8,128)(2,1)S(1)}, u32[]{:S(2)}, u32[]{:S(2)}) collective-permute-start(bf16[7,128,128]{2,1,0:T(8,128)(2,1)S(1)} %get-tuple-element.157), channel_id=1, source_target_pairs={{0,1},{1,0},{2,3},{3,2},{4,5},{5,4},{6,7},{7,6},{8,9},{9,8},{10,11... | collective-permute-start | bytes 688136 | tf_op jit(solution)/shard_map/ppermute | solution.py:631
  56.2 4.9 %grad_expand.1 = (bf16[2,4,120,384]{3,2,1,0:T(8,128)(2,1)S(1)}, bf16[2,4,120,384]{3,2,1,0:T(8,128)(2,1)S(1)}, bf16[2,4,120,384]{3,2,1,0:T(8,128)(2,1)S(1)}, bf16[2,4,120,384]{3,2,1,0:T(8,128)(2,1)S(1)}) custom-call(s32[9]{0:T(128)S(1)} %concatenate.3.scal, bf16[2,4,192,512]{3,2,1,0:T(8,128)(2,1)S(1)} %get-tuple-element.137.a_own.m_own, ...), custom_call_target="tpu_custom_call" | custom-call | flops 1150000000 | bytes 1 | tf_op jit(solution)/shard_map/grad_expand/pallas_call | solution.py:56
  61.1 1.4 %collective-permute-done.7.later = bf16[7,128,128]{2,1,0:T(8,128)(2,1)S(1)} collective-permute-done((bf16[7,128,128]{2,1,0:T(8,128)(2,1)S(1)}, bf16[7,128,128]{2,1,0:T(8,128)(2,1)S(1)}, u32[]{:S(2)}, u32[]{:S(2)}) %collective-permute-start.7) | collective-permute-done | bytes 229408 | tf_op jit(solution)/shard_map/ppermute | solution.py:631
  62.5 1.5 %collective-permute-start.9 = (bf16[2,4,120,384]{3,2,1,0:T(8,128)(2,1)S(1)}, bf16[2,4,120,384]{3,2,1,0:T(8,128)(2,1)S(1)}, u32[]{:S(2)}, u32[]{:S(2)}) collective-permute-start(bf16[2,4,120,384]{3,2,1,0:T(8,128)(2,1)S(1)} %get-tuple-element.171), channel_id=1, source_target_pairs={{0,1},{1,0},{2,3},{3,2},{4,5},{5,4},{6,7},{7,6},{8,9},{9,8},{10,11... | collective-permute-start | bytes 2211848 | tf_op jit(solution)/shard_map/ppermute | solution.py:631
  64.0 1.5 %collective-permute-start.10 = (bf16[2,4,120,384]{3,2,1,0:T(8,128)(2,1)S(1)}, bf16[2,4,120,384]{3,2,1,0:T(8,128)(2,1)S(1)}, u32[]{:S(2)}, u32[]{:S(2)}) collective-permute-start(bf16[2,4,120,384]{3,2,1,0:T(8,128)(2,1)S(1)} %get-tuple-element.174), channel_id=1, source_target_pairs={{0,4},{1,5},{2,6},{3,7},{4,0},{5,1},{6,2},{7,3},{8,12},{9,13},{10,... | collective-permute-start | bytes 2211848 | tf_op jit(solution)/shard_map/ppermute | solution.py:631
  65.5 5.8 %attention_back_sent.1 = (bf16[3,256,384]{2,1,0:T(8,128)(2,1)S(1)}, bf16[3,256,384]{2,1,0:T(8,128)(2,1)S(1)}, f32[3,8,384]{2,1,0:T(8,128)S(1)}, f32[512,512]{1,0:T(8,128)S(1)}, f32[512,512]{1,0:T(8,128)S(1)}) custom-call(s32[9]{0:T(128)S(1)} %concatenate.3.scal, bf16[512,768]{1,0:T(8,128)(2,1)S(1)} %get-tuple-element.131.refs_0_.rq, ...), custom_call_target="tpu_custom_call" | custom-call | flops 575000000 | bytes 1 | tf_op jit(solution)/shard_map/attention_back_sent/pallas_call | solution.py:56
  71.9 0.8 grad_reduce_add1.1
  72.7 2.8 %collective-permute-start.13 = (bf16[2,2,2,96,384]{4,3,2,1,0:T(8,128)(2,1)S(1)}, bf16[2,2,2,96,384]{4,3,2,1,0:T(8,128)(2,1)S(1)}, u32[]{:S(2)}, u32[]{:S(2)}) collective-permute-start(bf16[2,2,2,96,384]{4,3,2,1,0:T(8,128)(2,1)S(1)} %get-tuple-element.189), channel_id=1, source_target_pairs={{0,16},{1,17},{2,18},{3,19},{4,20},{5,21},{6,22},{7,23},{8,24},{9,... | collective-permute-start | bytes 1769480 | tf_op jit(solution)/shard_map/ppermute | solution.py:631
  75.5 6.3 %attention_back_kept.1 = (bf16[3,256,384]{2,1,0:T(8,128)(2,1)S(1)}, bf16[3,256,384]{2,1,0:T(8,128)(2,1)S(1)}, f32[3,8,384]{2,1,0:T(8,128)S(1)}) custom-call(s32[9]{0:T(128)S(1)} %concatenate.3.scal, bf16[512,768]{1,0:T(8,128)(2,1)S(1)} %get-tuple-element.131.refs_0_.rq, bf16[512,768]{1,0:T(8,128)(2,1)S(1)} %get-tuple-element.127.rk, ...), custom_call_target="tpu_custom_call" | custom-call | flops 575000000 | bytes 1 | tf_op jit(solution)/shard_map/attention_back_kept/pallas_call | solution.py:56
  81.8 0.7 grad_expand_add1.1
  82.5 1.6 %collective-permute-start.15 = (bf16[4,120,384]{2,1,0:T(8,128)(2,1)S(1)}, bf16[4,120,384]{2,1,0:T(8,128)(2,1)S(1)}, u32[]{:S(2)}, u32[]{:S(2)}) collective-permute-start(bf16[4,120,384]{2,1,0:T(8,128)(2,1)S(1)} %get-tuple-element.192), channel_id=1, source_target_pairs={{0,1},{1,0},{2,3},{3,2},{4,5},{5,4},{6,7},{7,6},{8,9},{9,8},{10,11... | collective-permute-start | bytes 1105928 | tf_op jit(solution)/shard_map/ppermute | solution.py:631
  84.0 1.5 %collective-permute-start.14 = (bf16[4,120,384]{2,1,0:T(8,128)(2,1)S(1)}, bf16[4,120,384]{2,1,0:T(8,128)(2,1)S(1)}, u32[]{:S(2)}, u32[]{:S(2)}) collective-permute-start(bf16[4,120,384]{2,1,0:T(8,128)(2,1)S(1)} %get-tuple-element.175), channel_id=1, source_target_pairs={{0,4},{1,5},{2,6},{3,7},{4,0},{5,1},{6,2},{7,3},{8,12},{9,13},{10,... | collective-permute-start | bytes 1105928 | tf_op jit(solution)/shard_map/ppermute | solution.py:631
  85.6 5.1 %grad_heads.1 = (bf16[2,4,80,384]{3,2,1,0:T(8,128)(2,1)S(1)}, bf16[2,4,80,384]{3,2,1,0:T(8,128)(2,1)S(1)}, bf16[2,4,80,384]{3,2,1,0:T(8,128)(2,1)S(1)}, bf16[2,4,80,384]{3,2,1,0:T(8,128)(2,1)S(1)}) custom-call(s32[9]{0:T(128)S(1)} %concatenate.3.scal, bf16[4,192,512]{2,1,0:T(8,128)(2,1)S(1)} %get-tuple-element.125.a_own, ...), custom_call_target="tpu_custom_call" | custom-call | flops 115000000 | bytes 1 | tf_op jit(solution)/shard_map/grad_heads/pallas_call | solution.py:56
  91.8 5.3 %input_grad.1 = f32[512,768]{1,0:T(8,128)} custom-call(s32[9]{0:T(128)S(1)} %concatenate.3.scal, f32[512,768]{1,0:T(8,128)S(1)} %get-tuple-element.187.first, bf16[3,256,384]{2,1,0:T(8,128)(2,1)S(1)} %get-tuple-element.168.own_early.keep_early, bf16[3,256,384]{2,1,0:T(8,128)(2,1)S(1)} %get-tuple-element.177.own_late.keep_late, ...), custom_call_target="tpu_custom_call" | custom-call | flops 115000000 | bytes 1 | tf_op jit(solution)/shard_map/input_grad/pallas_call | solution.py:56
  97.1 4.5 %collective-permute-done.13.got = bf16[2,2,2,96,384]{4,3,2,1,0:T(8,128)(2,1)S(1)} collective-permute-done((bf16[2,2,2,96,384]{4,3,2,1,0:T(8,128)(2,1)S(1)}, bf16[2,2,2,96,384]{4,3,2,1,0:T(8,128)(2,1)S(1)}, u32[]{:S(2)}, u32[]{:S(2)}) %collective-permute-start.13) | collective-permute-done | bytes 589856 | tf_op jit(solution)/shard_map/ppermute | solution.py:631
  101.6 0.6 grad_reduce_add2.1
  102.2 0.8 grad_expand_add2.1
  103.2 1.4 %collective-permute-start.21 = (bf16[2,2,96,384]{3,2,1,0:T(8,128)(2,1)S(1)}, bf16[2,2,96,384]{3,2,1,0:T(8,128)(2,1)S(1)}, u32[]{:S(2)}, u32[]{:S(2)}) collective-permute-start(bf16[2,2,96,384]{3,2,1,0:T(8,128)(2,1)S(1)} %get-tuple-element.206), channel_id=1, source_target_pairs={{0,1},{1,0},{2,3},{3,2},{4,5},{5,4},{6,7},{7,6},{8,9},{9,8},{10,11... | collective-permute-start | bytes 884744 | tf_op jit(solution)/shard_map/ppermute | solution.py:631
  104.6 0.7 grad_heads_add1.1
  105.3 0.7 collective-permute-start.20
  106.0 1.4 %collective-permute-start.19 = (bf16[4,80,384]{2,1,0:T(8,128)(2,1)S(1)}, bf16[4,80,384]{2,1,0:T(8,128)(2,1)S(1)}, u32[]{:S(2)}, u32[]{:S(2)}) collective-permute-start(bf16[4,80,384]{2,1,0:T(8,128)(2,1)S(1)} %get-tuple-element.198), channel_id=1, source_target_pairs={{0,4},{1,5},{2,6},{3,7},{4,0},{5,1},{6,2},{7,3},{8,12},{9,13},{10,... | collective-permute-start | bytes 737288 | tf_op jit(solution)/shard_map/ppermute | solution.py:631
  107.4 6.0 %collective-permute-done.18.got = bf16[2,2,120,384]{3,2,1,0:T(8,128)(2,1)S(1)} collective-permute-done((bf16[2,2,120,384]{3,2,1,0:T(8,128)(2,1)S(1)}, bf16[2,2,120,384]{3,2,1,0:T(8,128)(2,1)S(1)}, u32[]{:S(2)}, u32[]{:S(2)}) %collective-permute-start.18) | collective-permute-done | bytes 368672 | tf_op jit(solution)/shard_map/ppermute | solution.py:631
  113.4 0.6 grad_expand_add3.1
  114.0 1.4 %collective-permute-start.22 = (bf16[2,120,384]{2,1,0:T(8,128)(2,1)S(1)}, bf16[2,120,384]{2,1,0:T(8,128)(2,1)S(1)}, u32[]{:S(2)}, u32[]{:S(2)}) collective-permute-start(bf16[2,120,384]{2,1,0:T(8,128)(2,1)S(1)} %get-tuple-element.209), channel_id=1, source_target_pairs={{0,16},{1,17},{2,18},{3,19},{4,20},{5,21},{6,22},{7,23},{8,24},{9,... | collective-permute-start | bytes 552968 | tf_op jit(solution)/shard_map/ppermute | solution.py:631
  115.4 1.7 %collective-permute-done.20.ym = bf16[4,80,384]{2,1,0:T(8,128)(2,1)S(1)} collective-permute-done((bf16[4,80,384]{2,1,0:T(8,128)(2,1)S(1)}, bf16[4,80,384]{2,1,0:T(8,128)(2,1)S(1)}, u32[]{:S(2)}, u32[]{:S(2)}) %collective-permute-start.20) | collective-permute-done | bytes 245792 | tf_op jit(solution)/shard_map/ppermute | solution.py:631
  117.1 0.7 grad_heads_add2.1
  118.5 1.5 %collective-permute-start.23 = (bf16[2,96,384]{2,1,0:T(8,128)(2,1)S(1)}, bf16[2,96,384]{2,1,0:T(8,128)(2,1)S(1)}, u32[]{:S(2)}, u32[]{:S(2)}) collective-permute-start(bf16[2,96,384]{2,1,0:T(8,128)(2,1)S(1)} %get-tuple-element.212), channel_id=1, source_target_pairs={{0,4},{1,5},{2,6},{3,7},{4,0},{5,1},{6,2},{7,3},{8,12},{9,13},{10,... | collective-permute-start | bytes 442376 | tf_op jit(solution)/shard_map/ppermute | solution.py:631
  119.9 0.7 collective-permute-start.24
  120.6 3.1 %collective-permute-start.25 = (bf16[2,80,384]{2,1,0:T(8,128)(2,1)S(1)}, bf16[2,80,384]{2,1,0:T(8,128)(2,1)S(1)}, u32[]{:S(2)}, u32[]{:S(2)}) collective-permute-start(bf16[2,80,384]{2,1,0:T(8,128)(2,1)S(1)} %get-tuple-element.216), channel_id=1, source_target_pairs={{0,16},{1,17},{2,18},{3,19},{4,20},{5,21},{6,22},{7,23},{8,24},{9,... | collective-permute-start | bytes 368648 | tf_op jit(solution)/shard_map/ppermute | solution.py:631
  123.7 1.1 collective-permute-start.26
  126.6 3.6 %collective-permute-done.24.z1 = bf16[2,80,384]{2,1,0:T(8,128)(2,1)S(1)} collective-permute-done((bf16[2,80,384]{2,1,0:T(8,128)(2,1)S(1)}, bf16[2,80,384]{2,1,0:T(8,128)(2,1)S(1)}, u32[]{:S(2)}, u32[]{:S(2)}) %collective-permute-start.24) | collective-permute-done | bytes 122912 | tf_op jit(solution)/shard_map/ppermute | solution.py:631
  130.2 3.0 %collective-permute-done.25.z2 = bf16[2,80,384]{2,1,0:T(8,128)(2,1)S(1)} collective-permute-done((bf16[2,80,384]{2,1,0:T(8,128)(2,1)S(1)}, bf16[2,80,384]{2,1,0:T(8,128)(2,1)S(1)}, u32[]{:S(2)}, u32[]{:S(2)}) %collective-permute-start.25) | collective-permute-done | bytes 122912 | tf_op jit(solution)/shard_map/ppermute | solution.py:631
  133.2 0.6 grad_heads_add3.1
  133.9 1.3 collective-permute-done.27.got
  135.3 1.5 %finish.1 = (f32[24,2304]{1,0:T(8,128)}, f32[96,768]{1,0:T(8,128)}, f32[24,3072]{1,0:T(8,128)}, f32[24,768]{1,0:T(8,128)}, f32[1,48]{1,0:T(1,128)}, /*index=5*/f...) custom-call(s32[9]{0:T(128)S(1)} %concatenate.3.scal, ...), custom_call_target="tpu_custom_call" | custom-call | flops 115000000 | bytes 1 | tf_op jit(solution)/shard_map/finish/pallas_call | solution.py:56
  (81 shorter events, 6.5 us)
Async XLA Ops:
  2.1 2.0 %copy-start = (bf16[768,2304]{1,0:T(8,128)(2,1)S(1)}, bf16[768,2304]{1,0:T(8,128)(2,1)}, u32[]{:S(2)}) copy-start(bf16[768,2304]{1,0:T(8,128)(2,1)} %w_send.1) | copy-start | bytes 10616836
  4.1 1.1 copy-start.3
  5.3 13.4 %slice-start = ((s8[4718592]{0:T(1024)(128)(4,1)}), s8[4194304]{0:T(1024)(128)(4,1)S(1)}, s32[]{:S(2)}) async-start(s8[4718592]{0:T(1024)(128)(4,1)} %bitcast.14), calls=%async_computation | async-start | bytes 8388608
  5.3 13.4 %slice-start.2 = ((s8[4718592]{0:T(1024)(128)(4,1)}), s8[4194304]{0:T(1024)(128)(4,1)S(1)}, s32[]{:S(2)}) async-start(s8[4718592]{0:T(1024)(128)(4,1)} %bitcast.16), calls=%async_computation.2 | async-start | bytes 8388608
  9.4 9.0 %collective-permute-start = (bf16[4,192,512]{2,1,0:T(8,128)(2,1)S(1)}, bf16[4,192,512]{2,1,0:T(8,128)(2,1)S(1)}, u32[]{:S(2)}, u32[]{:S(2)}) collective-permute-start(bf16[4,192,512]{2,1,0:T(8,128)(2,1)S(1)} %get-tuple-element.125.a_own), channel_id=1, source_target_pairs={{0,2},{1,3},{2,0},{3,1},{4,6},{5,7},{6,4},{7,5},{8,10},{9,11},{10,... | collective-permute-start | bytes 2359304 | tf_op jit(solution)/shard_map/ppermute | solution.py:631
  9.9 8.8 %collective-permute-start.1 = (bf16[7,128,128]{2,1,0:T(8,128)(2,1)S(1)}, bf16[7,128,128]{2,1,0:T(8,128)(2,1)S(1)}, u32[]{:S(2)}, u32[]{:S(2)}) collective-permute-start(bf16[7,128,128]{2,1,0:T(8,128)(2,1)S(1)} %get-tuple-element.134), channel_id=1, source_target_pairs={{0,1},{1,0},{2,3},{3,2},{4,5},{5,4},{6,7},{7,6},{8,9},{9,8},{10,11... | collective-permute-start | bytes 688136 | tf_op jit(solution)/shard_map/ppermute | solution.py:631
  12.4 5.8 %copy-start.7 = (bf16[768]{0:T(1024)(128)(2,1)S(1)}, bf16[768]{0:T(1024)(128)(2,1)}, u32[]{:S(2)}) copy-start(bf16[768]{0:T(1024)(128)(2,1)} %param.20) | copy-start | bytes 4612
  12.4 5.8 %copy-start.8 = (bf16[768]{0:T(1024)(128)(2,1)S(1)}, bf16[768]{0:T(1024)(128)(2,1)}, u32[]{:S(2)}) copy-start(bf16[768]{0:T(1024)(128)(2,1)} %param.19) | copy-start | bytes 4612
  12.4 5.8 %copy-start.9 = (bf16[768]{0:T(1024)(128)(2,1)S(1)}, bf16[768]{0:T(1024)(128)(2,1)}, u32[]{:S(2)}) copy-start(bf16[768]{0:T(1024)(128)(2,1)} %param.21) | copy-start | bytes 4612
  12.4 5.9 %copy-start.10 = (bf16[768]{0:T(1024)(128)(2,1)S(1)}, bf16[768]{0:T(1024)(128)(2,1)}, u32[]{:S(2)}) copy-start(bf16[768]{0:T(1024)(128)(2,1)} %param.25) | copy-start | bytes 4612
  12.5 5.9 %copy-start.6 = (bf16[3072]{0:T(1024)(128)(2,1)S(1)}, bf16[3072]{0:T(1024)(128)(2,1)}, u32[]{:S(2)}) copy-start(bf16[3072]{0:T(1024)(128)(2,1)} %param.23) | copy-start | bytes 18436
  12.5 6.2 %slice-start.1 = ((s8[4718592]{0:T(1024)(128)(4,1)}), s8[524288]{0:T(1024)(128)(4,1)S(1)}, s32[]{:S(2)}) async-start(s8[4718592]{0:T(1024)(128)(4,1)} %bitcast.14), calls=%async_computation.1 | async-start | bytes 1048576
  12.5 6.2 %slice-start.3 = ((s8[4718592]{0:T(1024)(128)(4,1)}), s8[524288]{0:T(1024)(128)(4,1)S(1)}, s32[]{:S(2)}) async-start(s8[4718592]{0:T(1024)(128)(4,1)} %bitcast.16), calls=%async_computation.3 | async-start | bytes 1048576
  12.5 6.2 %copy-start.2 = (bf16[768,768]{1,0:T(8,128)(2,1)S(1)}, bf16[768,768]{1,0:T(8,128)(2,1)}, u32[]{:S(2)}) copy-start(bf16[768,768]{1,0:T(8,128)(2,1)} %w_merge.1) | copy-start | bytes 3538948
  12.5 6.2 %copy-start.4 = (bf16[512,768]{1,0:T(8,128)(2,1)S(1)}, bf16[512,768]{1,0:T(8,128)(2,1)}, u32[]{:S(2)}) copy-start(bf16[512,768]{1,0:T(8,128)(2,1)} %refs_5_.1) | copy-start | bytes 2359300
  18.7 10.9 %copy-start.11 = (bf16[768]{0:T(1024)(128)(2,1)S(1)}, bf16[768]{0:T(1024)(128)(2,1)}, u32[]{:S(2)}) copy-start(bf16[768]{0:T(1024)(128)(2,1)} %param.26) | copy-start | bytes 4612
  18.7 10.9 %copy-start.12 = (bf16[768]{0:T(1024)(128)(2,1)S(1)}, bf16[768]{0:T(1024)(128)(2,1)}, u32[]{:S(2)}) copy-start(bf16[768]{0:T(1024)(128)(2,1)} %param.27) | copy-start | bytes 4612
  18.7 10.9 %copy-start.5 = (bf16[512,768]{1,0:T(8,128)(2,1)S(1)}, bf16[512,768]{1,0:T(8,128)(2,1)}, u32[]{:S(2)}) copy-start(bf16[512,768]{1,0:T(8,128)(2,1)} %cot.1) | copy-start | bytes 2359300
  29.1 9.4 %collective-permute-start.3 = (bf16[512,3072]{1,0:T(8,128)(2,1)S(1)}, bf16[512,3072]{1,0:T(8,128)(2,1)S(1)}, u32[]{:S(2)}, u32[]{:S(2)}) collective-permute-start(bf16[512,3072]{1,0:T(8,128)(2,1)S(1)} %get-tuple-element.143.a_own), channel_id=1, source_target_pairs={{0,2},{1,3},{2,0},{3,1},{4,6},{5,7},{6,4},{7,5},{8,10},{9,11},{10,... | collective-permute-start | bytes 9437192 | tf_op jit(solution)/shard_map/ppermute | solution.py:631
  29.1 9.3 %collective-permute-start.2 = (bf16[2,4,192,512]{3,2,1,0:T(8,128)(2,1)S(1)}, bf16[2,4,192,512]{3,2,1,0:T(8,128)(2,1)S(1)}, u32[]{:S(2)}, u32[]{:S(2)}) collective-permute-start(bf16[2,4,192,512]{3,2,1,0:T(8,128)(2,1)S(1)} %get-tuple-element.137.a_own.m_own), channel_id=1, source_target_pairs={{0,2},{1,3},{2,0},{3,1},{4,6},{5,7},{6,4},{7,5},{8,10},{9,11},{10,... | collective-permute-start | bytes 4718600 | tf_op jit(solution)/shard_map/ppermute | solution.py:631
  32.2 6.2 %collective-permute-start.4 = (bf16[512,384]{1,0:T(8,128)(2,1)S(1)}, bf16[512,384]{1,0:T(8,128)(2,1)S(1)}, u32[]{:S(2)}, u32[]{:S(2)}) collective-permute-start(bf16[512,384]{1,0:T(8,128)(2,1)S(1)} %get-tuple-element.145), channel_id=1, source_target_pairs={{0,2},{1,3},{2,0},{3,1},{4,6},{5,7},{6,4},{7,5},{8,10},{9,11},{10,... | collective-permute-start | bytes 1179656 | tf_op jit(solution)/shard_map/ppermute | solution.py:631
  37.8 18.2 %collective-permute-start.5 = (bf16[2,512,768]{2,1,0:T(8,128)(2,1)S(1)}, bf16[2,512,768]{2,1,0:T(8,128)(2,1)S(1)}, u32[]{:S(2)}, u32[]{:S(2)}) collective-permute-start(bf16[2,512,768]{2,1,0:T(8,128)(2,1)S(1)} %get-tuple-element.153), channel_id=1, source_target_pairs={{0,2},{1,3},{2,0},{3,1},{4,6},{5,7},{6,4},{7,5},{8,10},{9,11},{10,... | collective-permute-start | bytes 4718600 | tf_op jit(solution)/shard_map/ppermute | solution.py:631
  43.8 28.1 %collective-permute-start.8 = (bf16[2,2,2,2,96,384]{5,4,3,2,1,0:T(8,128)(2,1)S(1)}, bf16[2,2,2,2,96,384]{5,4,3,2,1,0:T(8,128)(2,1)S(1)}, u32[]{:S(2)}, u32[]{:S(2)}) collective-permute-start(bf16[2,2,2,2,96,384]{5,4,3,2,1,0:T(8,128)(2,1)S(1)} %get-tuple-element.146), channel_id=1, source_target_pairs={{0,8},{1,9},{2,10},{3,11},{4,12},{5,13},{6,14},{7,15},{8,0},{9,1},... | collective-permute-start | bytes 3538952 | tf_op jit(solution)/shard_map/ppermute | solution.py:631
  54.4 1.8 %collective-permute-start.6 = (bf16[512,384]{1,0:T(8,128)(2,1)S(1)}, bf16[512,384]{1,0:T(8,128)(2,1)S(1)}, u32[]{:S(2)}, u32[]{:S(2)}) collective-permute-start(bf16[512,384]{1,0:T(8,128)(2,1)S(1)} %get-tuple-element.155), channel_id=1, source_target_pairs={{0,2},{1,3},{2,0},{3,1},{4,6},{5,7},{6,4},{7,5},{8,10},{9,11},{10,... | collective-permute-start | bytes 1179656 | tf_op jit(solution)/shard_map/ppermute | solution.py:631
  54.5 8.0 %collective-permute-start.7 = (bf16[7,128,128]{2,1,0:T(8,128)(2,1)S(1)}, bf16[7,128,128]{2,1,0:T(8,128)(2,1)S(1)}, u32[]{:S(2)}, u32[]{:S(2)}) collective-permute-start(bf16[7,128,128]{2,1,0:T(8,128)(2,1)S(1)} %get-tuple-element.157), channel_id=1, source_target_pairs={{0,1},{1,0},{2,3},{3,2},{4,5},{5,4},{6,7},{7,6},{8,9},{9,8},{10,11... | collective-permute-start | bytes 688136 | tf_op jit(solution)/shard_map/ppermute | solution.py:631
  62.5 19.3 %collective-permute-start.9 = (bf16[2,4,120,384]{3,2,1,0:T(8,128)(2,1)S(1)}, bf16[2,4,120,384]{3,2,1,0:T(8,128)(2,1)S(1)}, u32[]{:S(2)}, u32[]{:S(2)}) collective-permute-start(bf16[2,4,120,384]{3,2,1,0:T(8,128)(2,1)S(1)} %get-tuple-element.171), channel_id=1, source_target_pairs={{0,1},{1,0},{2,3},{3,2},{4,5},{5,4},{6,7},{7,6},{8,9},{9,8},{10,11... | collective-permute-start | bytes 2211848 | tf_op jit(solution)/shard_map/ppermute | solution.py:631
  64.0 17.8 %collective-permute-start.10 = (bf16[2,4,120,384]{3,2,1,0:T(8,128)(2,1)S(1)}, bf16[2,4,120,384]{3,2,1,0:T(8,128)(2,1)S(1)}, u32[]{:S(2)}, u32[]{:S(2)}) collective-permute-start(bf16[2,4,120,384]{3,2,1,0:T(8,128)(2,1)S(1)} %get-tuple-element.174), channel_id=1, source_target_pairs={{0,4},{1,5},{2,6},{3,7},{4,0},{5,1},{6,2},{7,3},{8,12},{9,13},{10,... | collective-permute-start | bytes 2211848 | tf_op jit(solution)/shard_map/ppermute | solution.py:631
  71.3 14.3 %collective-permute-start.12 = (bf16[3,256,384]{2,1,0:T(8,128)(2,1)S(1)}, bf16[3,256,384]{2,1,0:T(8,128)(2,1)S(1)}, u32[]{:S(2)}, u32[]{:S(2)}) collective-permute-start(bf16[3,256,384]{2,1,0:T(8,128)(2,1)S(1)} %get-tuple-element.178.send_late), channel_id=1, source_target_pairs={{0,2},{1,3},{2,0},{3,1},{4,6},{5,7},{6,4},{7,5},{8,10},{9,11},{10,... | collective-permute-start | bytes 1769480 | tf_op jit(solution)/shard_map/ppermute | solution.py:631
  71.3 14.2 %collective-permute-start.11 = (bf16[3,256,384]{2,1,0:T(8,128)(2,1)S(1)}, bf16[3,256,384]{2,1,0:T(8,128)(2,1)S(1)}, u32[]{:S(2)}, u32[]{:S(2)}) collective-permute-start(bf16[3,256,384]{2,1,0:T(8,128)(2,1)S(1)} %get-tuple-element.161.send_early), channel_id=1, source_target_pairs={{0,2},{1,3},{2,0},{3,1},{4,6},{5,7},{6,4},{7,5},{8,10},{9,11},{10,... | collective-permute-start | bytes 1769480 | tf_op jit(solution)/shard_map/ppermute | solution.py:631
  72.7 28.9 %collective-permute-start.13 = (bf16[2,2,2,96,384]{4,3,2,1,0:T(8,128)(2,1)S(1)}, bf16[2,2,2,96,384]{4,3,2,1,0:T(8,128)(2,1)S(1)}, u32[]{:S(2)}, u32[]{:S(2)}) collective-permute-start(bf16[2,2,2,96,384]{4,3,2,1,0:T(8,128)(2,1)S(1)} %get-tuple-element.189), channel_id=1, source_target_pairs={{0,16},{1,17},{2,18},{3,19},{4,20},{5,21},{6,22},{7,23},{8,24},{9,... | collective-permute-start | bytes 1769480 | tf_op jit(solution)/shard_map/ppermute | solution.py:631
  82.5 19.7 %collective-permute-start.15 = (bf16[4,120,384]{2,1,0:T(8,128)(2,1)S(1)}, bf16[4,120,384]{2,1,0:T(8,128)(2,1)S(1)}, u32[]{:S(2)}, u32[]{:S(2)}) collective-permute-start(bf16[4,120,384]{2,1,0:T(8,128)(2,1)S(1)} %get-tuple-element.192), channel_id=1, source_target_pairs={{0,1},{1,0},{2,3},{3,2},{4,5},{5,4},{6,7},{7,6},{8,9},{9,8},{10,11... | collective-permute-start | bytes 1105928 | tf_op jit(solution)/shard_map/ppermute | solution.py:631
  84.0 18.2 %collective-permute-start.14 = (bf16[4,120,384]{2,1,0:T(8,128)(2,1)S(1)}, bf16[4,120,384]{2,1,0:T(8,128)(2,1)S(1)}, u32[]{:S(2)}, u32[]{:S(2)}) collective-permute-start(bf16[4,120,384]{2,1,0:T(8,128)(2,1)S(1)} %get-tuple-element.175), channel_id=1, source_target_pairs={{0,4},{1,5},{2,6},{3,7},{4,0},{5,1},{6,2},{7,3},{8,12},{9,13},{10,... | collective-permute-start | bytes 1105928 | tf_op jit(solution)/shard_map/ppermute | solution.py:631
  85.6 6.3 %copy-start.1 = (bf16[768,2304]{1,0:T(8,128)(2,1)S(1)}, bf16[768,2304]{1,0:T(8,128)(2,1)}, u32[]{:S(2)}) copy-start(bf16[768,2304]{1,0:T(8,128)(2,1)} %w_send.1) | copy-start | bytes 10616836
  90.7 13.9 %collective-permute-start.17 = (bf16[2,4,80,384]{3,2,1,0:T(8,128)(2,1)S(1)}, bf16[2,4,80,384]{3,2,1,0:T(8,128)(2,1)S(1)}, u32[]{:S(2)}, u32[]{:S(2)}) collective-permute-start(bf16[2,4,80,384]{3,2,1,0:T(8,128)(2,1)S(1)} %get-tuple-element.197), channel_id=1, source_target_pairs={{0,4},{1,5},{2,6},{3,7},{4,0},{5,1},{6,2},{7,3},{8,12},{9,13},{10,... | collective-permute-start | bytes 1474568 | tf_op jit(solution)/shard_map/ppermute | solution.py:631
  91.3 13.3 %collective-permute-start.16 = (bf16[2,4,80,384]{3,2,1,0:T(8,128)(2,1)S(1)}, bf16[2,4,80,384]{3,2,1,0:T(8,128)(2,1)S(1)}, u32[]{:S(2)}, u32[]{:S(2)}) collective-permute-start(bf16[2,4,80,384]{3,2,1,0:T(8,128)(2,1)S(1)} %get-tuple-element.185), channel_id=1, source_target_pairs={{0,1},{1,0},{2,3},{3,2},{4,5},{5,4},{6,7},{7,6},{8,9},{9,8},{10,11... | collective-permute-start | bytes 1474568 | tf_op jit(solution)/shard_map/ppermute | solution.py:631
  103.1 10.3 %collective-permute-start.18 = (bf16[2,2,120,384]{3,2,1,0:T(8,128)(2,1)S(1)}, bf16[2,2,120,384]{3,2,1,0:T(8,128)(2,1)S(1)}, u32[]{:S(2)}, u32[]{:S(2)}) collective-permute-start(bf16[2,2,120,384]{3,2,1,0:T(8,128)(2,1)S(1)} %get-tuple-element.200), channel_id=1, source_target_pairs={{0,8},{1,9},{2,10},{3,11},{4,12},{5,13},{6,14},{7,15},{8,0},{9,1},... | collective-permute-start | bytes 1105928 | tf_op jit(solution)/shard_map/ppermute | solution.py:631
  103.2 14.7 %collective-permute-start.21 = (bf16[2,2,96,384]{3,2,1,0:T(8,128)(2,1)S(1)}, bf16[2,2,96,384]{3,2,1,0:T(8,128)(2,1)S(1)}, u32[]{:S(2)}, u32[]{:S(2)}) collective-permute-start(bf16[2,2,96,384]{3,2,1,0:T(8,128)(2,1)S(1)} %get-tuple-element.206), channel_id=1, source_target_pairs={{0,1},{1,0},{2,3},{3,2},{4,5},{5,4},{6,7},{7,6},{8,9},{9,8},{10,11... | collective-permute-start | bytes 884744 | tf_op jit(solution)/shard_map/ppermute | solution.py:631
  105.3 11.9 %collective-permute-start.20 = (bf16[4,80,384]{2,1,0:T(8,128)(2,1)S(1)}, bf16[4,80,384]{2,1,0:T(8,128)(2,1)S(1)}, u32[]{:S(2)}, u32[]{:S(2)}) collective-permute-start(bf16[4,80,384]{2,1,0:T(8,128)(2,1)S(1)} %get-tuple-element.203), channel_id=1, source_target_pairs={{0,1},{1,0},{2,3},{3,2},{4,5},{5,4},{6,7},{7,6},{8,9},{9,8},{10,11... | collective-permute-start | bytes 737288 | tf_op jit(solution)/shard_map/ppermute | solution.py:631
  106.0 11.2 %collective-permute-start.19 = (bf16[4,80,384]{2,1,0:T(8,128)(2,1)S(1)}, bf16[4,80,384]{2,1,0:T(8,128)(2,1)S(1)}, u32[]{:S(2)}, u32[]{:S(2)}) collective-permute-start(bf16[4,80,384]{2,1,0:T(8,128)(2,1)S(1)} %get-tuple-element.198), channel_id=1, source_target_pairs={{0,4},{1,5},{2,6},{3,7},{4,0},{5,1},{6,2},{7,3},{8,12},{9,13},{10,... | collective-permute-start | bytes 737288 | tf_op jit(solution)/shard_map/ppermute | solution.py:631
  114.0 10.8 %collective-permute-start.22 = (bf16[2,120,384]{2,1,0:T(8,128)(2,1)S(1)}, bf16[2,120,384]{2,1,0:T(8,128)(2,1)S(1)}, u32[]{:S(2)}, u32[]{:S(2)}) collective-permute-start(bf16[2,120,384]{2,1,0:T(8,128)(2,1)S(1)} %get-tuple-element.209), channel_id=1, source_target_pairs={{0,16},{1,17},{2,18},{3,19},{4,20},{5,21},{6,22},{7,23},{8,24},{9,... | collective-permute-start | bytes 552968 | tf_op jit(solution)/shard_map/ppermute | solution.py:631
  118.5 7.0 %collective-permute-start.23 = (bf16[2,96,384]{2,1,0:T(8,128)(2,1)S(1)}, bf16[2,96,384]{2,1,0:T(8,128)(2,1)S(1)}, u32[]{:S(2)}, u32[]{:S(2)}) collective-permute-start(bf16[2,96,384]{2,1,0:T(8,128)(2,1)S(1)} %get-tuple-element.212), channel_id=1, source_target_pairs={{0,4},{1,5},{2,6},{3,7},{4,0},{5,1},{6,2},{7,3},{8,12},{9,13},{10,... | collective-permute-start | bytes 442376 | tf_op jit(solution)/shard_map/ppermute | solution.py:631
  119.9 10.2 %collective-permute-start.24 = (bf16[2,80,384]{2,1,0:T(8,128)(2,1)S(1)}, bf16[2,80,384]{2,1,0:T(8,128)(2,1)S(1)}, u32[]{:S(2)}, u32[]{:S(2)}) collective-permute-start(bf16[2,80,384]{2,1,0:T(8,128)(2,1)S(1)} %get-tuple-element.215), channel_id=1, source_target_pairs={{0,8},{1,9},{2,10},{3,11},{4,12},{5,13},{6,14},{7,15},{8,0},{9,1},... | collective-permute-start | bytes 368648 | tf_op jit(solution)/shard_map/ppermute | solution.py:631
  120.6 12.6 %collective-permute-start.25 = (bf16[2,80,384]{2,1,0:T(8,128)(2,1)S(1)}, bf16[2,80,384]{2,1,0:T(8,128)(2,1)S(1)}, u32[]{:S(2)}, u32[]{:S(2)}) collective-permute-start(bf16[2,80,384]{2,1,0:T(8,128)(2,1)S(1)} %get-tuple-element.216), channel_id=1, source_target_pairs={{0,16},{1,17},{2,18},{3,19},{4,20},{5,21},{6,22},{7,23},{8,24},{9,... | collective-permute-start | bytes 368648 | tf_op jit(solution)/shard_map/ppermute | solution.py:631
  123.7 9.5 %collective-permute-start.26 = (bf16[2,80,384]{2,1,0:T(8,128)(2,1)S(1)}, bf16[2,80,384]{2,1,0:T(8,128)(2,1)S(1)}, u32[]{:S(2)}, u32[]{:S(2)}) collective-permute-start(bf16[2,80,384]{2,1,0:T(8,128)(2,1)S(1)} %get-tuple-element.217), channel_id=1, source_target_pairs={{0,24},{1,25},{2,26},{3,27},{4,28},{5,29},{6,30},{7,31},{8,16},{9,... | collective-permute-start | bytes 368648 | tf_op jit(solution)/shard_map/ppermute | solution.py:631
  125.4 9.9 %collective-permute-start.29 = (f32[120,384]{1,0:T(8,128)S(1)}, f32[120,384]{1,0:T(8,128)S(1)}, u32[]{:S(2)}, u32[]{:S(2)}) collective-permute-start(f32[120,384]{1,0:T(8,128)S(1)} %get-tuple-element.221), channel_id=1, source_target_pairs={{0,2},{1,3},{2,0},{3,1},{4,6},{5,7},{6,4},{7,5},{8,10},{9,11},{10,... | collective-permute-start | bytes 552968 | tf_op jit(solution)/shard_map/ppermute | solution.py:631
  126.1 9.2 %collective-permute-start.28 = (f32[96,384]{1,0:T(8,128)S(1)}, f32[96,384]{1,0:T(8,128)S(1)}, u32[]{:S(2)}, u32[]{:S(2)}) collective-permute-start(f32[96,384]{1,0:T(8,128)S(1)} %get-tuple-element.220), channel_id=1, source_target_pairs={{0,2},{1,3},{2,0},{3,1},{4,6},{5,7},{6,4},{7,5},{8,10},{9,11},{10,... | collective-permute-start | bytes 442376 | tf_op jit(solution)/shard_map/ppermute | solution.py:631
  133.8 1.4 %collective-permute-start.27 = (f32[80,384]{1,0:T(8,128)S(1)}, f32[80,384]{1,0:T(8,128)S(1)}, u32[]{:S(2)}, u32[]{:S(2)}) collective-permute-start(f32[80,384]{1,0:T(8,128)S(1)} %get-tuple-element.219), channel_id=1, source_target_pairs={{0,2},{1,3},{2,0},{3,1},{4,6},{5,7},{6,4},{7,5},{8,10},{9,11},{10,... | collective-permute-start | bytes 368648 | tf_op jit(solution)/shard_map/ppermute | solution.py:631
where the time goes:
time: 138 us; the launch traced here: 137 us
  Pallas kernels  78.6 us (57%)
  starting transfers between devices  30.3 us (22%)
  waiting for transfers between devices  22.1 us (16%)
  local copies, waits for them, and re-layouts  4.69 us (3%)
    pallas_call x24, Pallas kernels, call(): pl.pallas_call(kernel, name=name, grid_spec=pltpu.PrefetchScalarGridSpec(...  78.6 us
    ppermute x30, starting transfers between devices, swap(): lax.ppermute(value, AXES, [(i, i ^ bits) for i in range(self.devices)])  30.3 us
    ppermute x30, waiting for transfers between devices, swap(): lax.ppermute(value, AXES, [(i, i ^ bits) for i in range(self.devices)])  22.1 us
    unnamed x34, local copies, waits for them, and re-layouts  3.21 us
  transfers between devices with their start and end apart: 30, of which 9 were waited for; matrix products, arithmetic and copies ran while one was open for 0% of the time, Pallas kernels for 46%

commit v1 on v0

--- a/solution.py
+++ b/solution.py
@@ -559,14 +559,15 @@
 
 
 def expand_grad_kernel(pos_at, scal, a_own, a_oth, b_own, b_oth, m_own, m_oth, c_own, c_oth, *outs):
-    tz = pl.program_id(0)
     x, y, z = (scal[pos_at + n] for n in range(3))
-    an, ao = a_own[0, 0], a_oth[0, 0]
-    parts = [dot(an, b_own[n]) + dot(ao, b_oth[n]) for n in range(b_own.shape[0])]
-    parts.append(dot(m_own[0, 0], c_own[...]) + dot(m_oth[0, 0], c_oth[...]))
-    values = jnp.concatenate(parts, axis=1)
-    pieces = place(values, values.shape[0] // 8, tz, (0, 1), x, y, z, None, outs)
-    place_y(pieces, tz, (0, 1), x, y, z, outs)
+    for half in range(2):
+        tz = 2 * pl.program_id(0) + half
+        an, ao = a_own[0, half], a_oth[0, half]
+        parts = [dot(an, b_own[n]) + dot(ao, b_oth[n]) for n in range(b_own.shape[0])]
+        parts.append(dot(m_own[0, half], c_own[...]) + dot(m_oth[0, half], c_oth[...]))
+        values = jnp.concatenate(parts, axis=1)
+        pieces = place(values, values.shape[0] // 8, tz, (0, 1), x, y, z, None, outs)
+        place_y(pieces, tz, (0, 1), x, y, z, outs)
 
 
 def share_lanes(entries, devices, at, width):
@@ -975,7 +976,7 @@
     devices = ring.devices
     small, large = D // devices, FF // devices
     whole = lambda a: (a, None, None)
-    part = lambda a, n: (a, (1, 1, D // 4, rows), lambda j, s: (n, j, 0, 0))
+    part = lambda a, n: (a, (1, 2, D // 4, rows), lambda j, s: (n, j, 0, 0))
     by_z = lambda a: (a, (1, D // 4, rows), lambda j, s: (j, 0, 0))
     by_col = lambda a: (a, (rows, FF // 4), lambda j, s: (0, j))
 
@@ -1034,7 +1035,7 @@
     if fast:
         mg_o = ring.core(mg_send)
         expanded = group(
-            expand_grad_kernel, "grad_expand", scal, (4,),
+            expand_grad_kernel, "grad_expand", scal, (2,),
             [
                 part(turned_own, 1), part(turned_other, 1), whole(pg_keep), whole(pg_o),
                 part(turned_own, 0), part(turned_other, 0), whole(mg_keep), whole(mg_o),

time: 138 us -> 138 us (level)
  no operation moved by 1% of the time
where the time goes in v1:
time: 138 us; the launch traced here: 137 us
  Pallas kernels  78.3 us (57%)
  starting transfers between devices  30.3 us (22%)
  waiting for transfers between devices  22.4 us (16%)
  local copies, waits for them, and re-layouts  4.69 us (3%)
    pallas_call x24, Pallas kernels, call(): pl.pallas_call(kernel, name=name, grid_spec=pltpu.PrefetchScalarGridSpec(...  78.3 us
    ppermute x30, starting transfers between devices, swap(): lax.ppermute(value, AXES, [(i, i ^ bits) for i in range(self.devices)])  30.3 us
    ppermute x30, waiting for transfers between devices, swap(): lax.ppermute(value, AXES, [(i, i ^ bits) for i in range(self.devices)])  22.4 us
    unnamed x34, local copies, waits for them, and re-layouts  3.21 us
  transfers between devices with their start and end apart: 30, of which 9 were waited for; matrix products, arithmetic and copies ran while one was open for 0% of the time, Pallas kernels for 46%

profile of v1, /device:TPU:0, one launch (start us, length us, event | category | flops | bytes accessed | tf_op | source)
XLA Modules:
  0.0 136.9 jit_solution(4176385604502434661)
XLA Ops:
  0.7 0.7 reshape.81.bk.bv.bq
  1.4 0.7 concatenate.3.scal
  2.1 2.0 %copy-done = bf16[768,2304]{1,0:T(8,128)(2,1)S(1)} copy-done((bf16[768,2304]{1,0:T(8,128)(2,1)S(1)}, bf16[768,2304]{1,0:T(8,128)(2,1)}, u32[]{:S(2)}) %copy-start) | copy-done | bytes 3538968
  4.1 1.1 copy-done.3
  5.3 4.1 %keys_values.1 = (bf16[512,768]{1,0:T(8,128)(2,1)S(1)}, bf16[512,768]{1,0:T(8,128)(2,1)S(1)}, bf16[7,128,128]{2,1,0:T(8,128)(2,1)S(1)}, f32[512,128]{1,0:T(8,128...) custom-call(s32[9]{0:T(128)S(1)} %concatenate.3.scal, bf16[512,768]{1,0:T(8,128)(2,1)S(1)} %copy-done.3, ...), custom_call_target="tpu_custom_call" | custom-call | flops 4600000000 | bytes 1 | tf_op jit(solution)/shard_map/keys_values/pallas_call | solution.py:56
  9.9 2.6 %collective-permute-start.1 = (bf16[7,128,128]{2,1,0:T(8,128)(2,1)S(1)}, bf16[7,128,128]{2,1,0:T(8,128)(2,1)S(1)}, u32[]{:S(2)}, u32[]{:S(2)}) collective-permute-start(bf16[7,128,128]{2,1,0:T(8,128)(2,1)S(1)} %get-tuple-element.134), channel_id=1, source_target_pairs={{0,1},{1,0},{2,3},{3,2},{4,5},{5,4},{6,7},{7,6},{8,9},{9,8},{10,11... | collective-permute-start | bytes 688136 | tf_op jit(solution)/shard_map/ppermute | solution.py:632
  12.5 5.7 %local_attention.1 = (bf16[512,768]{1,0:T(8,128)(2,1)S(1)}, f32[512,768]{1,0:T(8,128)S(1)}, f32[512,768]{1,0:T(8,128)S(1)}) custom-call(s32[9]{0:T(128)S(1)} %concatenate.3.scal, bf16[512,768]{1,0:T(8,128)(2,1)S(1)} %copy-done.3, bf16[768,2304]{1,0:T(8,128)(2,1)S(1)} %copy-done, bf16[1,2304]{1,0:T(2,128)(2,1)S(1)} %reshape.81.bk.bv.bq, ...), custom_call_target="tpu_custom_call" | custom-call | flops 6899999744 | bytes 1 | tf_op jit(solution)/shard_map/local_attention/pallas_call | solution.py:56
  18.7 10.3 %feed_forward.1 = (f32[512,768]{1,0:T(8,128)S(1)}, f32[512,768]{1,0:T(8,128)S(1)}, bf16[512,768]{1,0:T(8,128)(2,1)}, f32[512,768]{1,0:T(8,128)S(1)}, f32[512,128...) custom-call(s32[9]{0:T(128)S(1)} %concatenate.3.scal, ...), custom_call_target="tpu_custom_call" | custom-call | flops 12650000384 | bytes 1 | tf_op jit(solution)/shard_map/feed_forward/pallas_call | solution.py:56
  29.6 2.6 %second_norm.1 = (bf16[512,768]{1,0:T(8,128)(2,1)}, f32[512,768]{1,0:T(8,128)S(1)}, bf16[512,768]{1,0:T(8,128)(2,1)S(1)}, bf16[512,384]{1,0:T(8,128)(2,1)S(1)}, ...) custom-call(s32[9]{0:T(128)S(1)} %concatenate.3.scal, f32[512,768]{1,0:T(8,128)S(1)} %get-tuple-element.135.second, ...), custom_call_target="tpu_custom_call" | custom-call | flops 2990000128 | bytes 1 | tf_op jit(solution)/shard_map/second_norm/pallas_call | solution.py:56
  32.2 5.6 %feed_forward_back_sent.1 = (bf16[2,512,768]{2,1,0:T(8,128)(2,1)S(1)}, f32[1,1536]{1,0:T(1,128)S(1)}, f32[512,768]{1,0:T(8,128)S(1)}) custom-call(s32[9]{0:T(128)S(1)} %concatenate.3.scal, bf16[512,768]{1,0:T(8,128)(2,1)S(1)} %get-tuple-element.138.full, bf16[512,3072]{1,0:T(8,128)(2,1)S(1)} %get-tuple-element.139.slope, bf16[768,3072]{1,0:T(8,128)(2,1)S(1)} %bitcast.15, ...), custom_call_target="tpu_custom_call" | custom-call | flops 5750000128 | bytes 1 | tf_op jit(solution)/shard_map/feed_forward_back_sent/pallas_call | solution.py:56
  38.4 5.4 %grad_reduce.1 = (bf16[2,2,2,2,96,384]{5,4,3,2,1,0:T(8,128)(2,1)S(1)}, bf16[2,2,2,2,96,384]{5,4,3,2,1,0:T(8,128)(2,1)S(1)}) custom-call(s32[9]{0:T(128)S(1)} %concatenate.3.scal, bf16[512,3072]{1,0:T(8,128)(2,1)S(1)} %get-tuple-element.143.a_own, bf16[512,3072]{1,0:T(8,128)(2,1)S(1)} %collective-permute-done.3.a_oth, ...), custom_call_target="tpu_custom_call" | custom-call | flops 6899999744 | bytes 1 | tf_op jit(solution)/shard_map/grad_reduce/pallas_call | solution.py:56
  43.8 1.9 %collective-permute-start.8 = (bf16[2,2,2,2,96,384]{5,4,3,2,1,0:T(8,128)(2,1)S(1)}, bf16[2,2,2,2,96,384]{5,4,3,2,1,0:T(8,128)(2,1)S(1)}, u32[]{:S(2)}, u32[]{:S(2)}) collective-permute-start(bf16[2,2,2,2,96,384]{5,4,3,2,1,0:T(8,128)(2,1)S(1)} %get-tuple-element.146), channel_id=1, source_target_pairs={{0,8},{1,9},{2,10},{3,11},{4,12},{5,13},{6,14},{7,15},{8,0},{9,1},... | collective-permute-start | bytes 3538952 | tf_op jit(solution)/shard_map/ppermute | solution.py:632
  45.7 8.7 %feed_forward_back.1 = (bf16[2,512,768]{2,1,0:T(8,128)(2,1)S(1)}, f32[512,768]{1,0:T(8,128)S(1)}, bf16[512,384]{1,0:T(8,128)(2,1)S(1)}, bf16[512,384]{1,0:T(8,12...) custom-call(s32[9]{0:T(128)S(1)} %concatenate.3.scal, ...), custom_call_target="tpu_custom_call" | custom-call | flops 3449999872 | bytes 1 | tf_op jit(solution)/shard_map/feed_forward_back/pallas_call | solution.py:56
  54.5 1.6 %collective-permute-start.7 = (bf16[7,128,128]{2,1,0:T(8,128)(2,1)S(1)}, bf16[7,128,128]{2,1,0:T(8,128)(2,1)S(1)}, u32[]{:S(2)}, u32[]{:S(2)}) collective-permute-start(bf16[7,128,128]{2,1,0:T(8,128)(2,1)S(1)} %get-tuple-element.157), channel_id=1, source_target_pairs={{0,1},{1,0},{2,3},{3,2},{4,5},{5,4},{6,7},{7,6},{8,9},{9,8},{10,11... | collective-permute-start | bytes 688136 | tf_op jit(solution)/shard_map/ppermute | solution.py:632
  56.2 4.6 %grad_expand.1 = (bf16[2,4,120,384]{3,2,1,0:T(8,128)(2,1)S(1)}, bf16[2,4,120,384]{3,2,1,0:T(8,128)(2,1)S(1)}, bf16[2,4,120,384]{3,2,1,0:T(8,128)(2,1)S(1)}, bf16[2,4,120,384]{3,2,1,0:T(8,128)(2,1)S(1)}) custom-call(s32[9]{0:T(128)S(1)} %concatenate.3.scal, bf16[2,4,192,512]{3,2,1,0:T(8,128)(2,1)S(1)} %get-tuple-element.137.a_own.m_own, ...), custom_call_target="tpu_custom_call" | custom-call | flops 1150000000 | bytes 1 | tf_op jit(solution)/shard_map/grad_expand/pallas_call | solution.py:56
  60.7 1.7 %collective-permute-done.7.later = bf16[7,128,128]{2,1,0:T(8,128)(2,1)S(1)} collective-permute-done((bf16[7,128,128]{2,1,0:T(8,128)(2,1)S(1)}, bf16[7,128,128]{2,1,0:T(8,128)(2,1)S(1)}, u32[]{:S(2)}, u32[]{:S(2)}) %collective-permute-start.7) | collective-permute-done | bytes 229408 | tf_op jit(solution)/shard_map/ppermute | solution.py:632
  62.5 1.5 %collective-permute-start.9 = (bf16[2,4,120,384]{3,2,1,0:T(8,128)(2,1)S(1)}, bf16[2,4,120,384]{3,2,1,0:T(8,128)(2,1)S(1)}, u32[]{:S(2)}, u32[]{:S(2)}) collective-permute-start(bf16[2,4,120,384]{3,2,1,0:T(8,128)(2,1)S(1)} %get-tuple-element.171), channel_id=1, source_target_pairs={{0,1},{1,0},{2,3},{3,2},{4,5},{5,4},{6,7},{7,6},{8,9},{9,8},{10,11... | collective-permute-start | bytes 2211848 | tf_op jit(solution)/shard_map/ppermute | solution.py:632
  64.0 1.5 %collective-permute-start.10 = (bf16[2,4,120,384]{3,2,1,0:T(8,128)(2,1)S(1)}, bf16[2,4,120,384]{3,2,1,0:T(8,128)(2,1)S(1)}, u32[]{:S(2)}, u32[]{:S(2)}) collective-permute-start(bf16[2,4,120,384]{3,2,1,0:T(8,128)(2,1)S(1)} %get-tuple-element.174), channel_id=1, source_target_pairs={{0,4},{1,5},{2,6},{3,7},{4,0},{5,1},{6,2},{7,3},{8,12},{9,13},{10,... | collective-permute-start | bytes 2211848 | tf_op jit(solution)/shard_map/ppermute | solution.py:632
  65.5 5.8 %attention_back_sent.1 = (bf16[3,256,384]{2,1,0:T(8,128)(2,1)S(1)}, bf16[3,256,384]{2,1,0:T(8,128)(2,1)S(1)}, f32[3,8,384]{2,1,0:T(8,128)S(1)}, f32[512,512]{1,0:T(8,128)S(1)}, f32[512,512]{1,0:T(8,128)S(1)}) custom-call(s32[9]{0:T(128)S(1)} %concatenate.3.scal, bf16[512,768]{1,0:T(8,128)(2,1)S(1)} %get-tuple-element.131.refs_0_.rq, ...), custom_call_target="tpu_custom_call" | custom-call | flops 575000000 | bytes 1 | tf_op jit(solution)/shard_map/attention_back_sent/pallas_call | solution.py:56
  71.9 0.8 grad_reduce_add1.1
  72.7 2.8 %collective-permute-start.13 = (bf16[2,2,2,96,384]{4,3,2,1,0:T(8,128)(2,1)S(1)}, bf16[2,2,2,96,384]{4,3,2,1,0:T(8,128)(2,1)S(1)}, u32[]{:S(2)}, u32[]{:S(2)}) collective-permute-start(bf16[2,2,2,96,384]{4,3,2,1,0:T(8,128)(2,1)S(1)} %get-tuple-element.189), channel_id=1, source_target_pairs={{0,16},{1,17},{2,18},{3,19},{4,20},{5,21},{6,22},{7,23},{8,24},{9,... | collective-permute-start | bytes 1769480 | tf_op jit(solution)/shard_map/ppermute | solution.py:632
  75.5 6.3 %attention_back_kept.1 = (bf16[3,256,384]{2,1,0:T(8,128)(2,1)S(1)}, bf16[3,256,384]{2,1,0:T(8,128)(2,1)S(1)}, f32[3,8,384]{2,1,0:T(8,128)S(1)}) custom-call(s32[9]{0:T(128)S(1)} %concatenate.3.scal, bf16[512,768]{1,0:T(8,128)(2,1)S(1)} %get-tuple-element.131.refs_0_.rq, bf16[512,768]{1,0:T(8,128)(2,1)S(1)} %get-tuple-element.127.rk, ...), custom_call_target="tpu_custom_call" | custom-call | flops 575000000 | bytes 1 | tf_op jit(solution)/shard_map/attention_back_kept/pallas_call | solution.py:56
  81.8 0.7 grad_expand_add1.1
  82.5 1.6 %collective-permute-start.15 = (bf16[4,120,384]{2,1,0:T(8,128)(2,1)S(1)}, bf16[4,120,384]{2,1,0:T(8,128)(2,1)S(1)}, u32[]{:S(2)}, u32[]{:S(2)}) collective-permute-start(bf16[4,120,384]{2,1,0:T(8,128)(2,1)S(1)} %get-tuple-element.192), channel_id=1, source_target_pairs={{0,1},{1,0},{2,3},{3,2},{4,5},{5,4},{6,7},{7,6},{8,9},{9,8},{10,11... | collective-permute-start | bytes 1105928 | tf_op jit(solution)/shard_map/ppermute | solution.py:632
  84.0 1.5 %collective-permute-start.14 = (bf16[4,120,384]{2,1,0:T(8,128)(2,1)S(1)}, bf16[4,120,384]{2,1,0:T(8,128)(2,1)S(1)}, u32[]{:S(2)}, u32[]{:S(2)}) collective-permute-start(bf16[4,120,384]{2,1,0:T(8,128)(2,1)S(1)} %get-tuple-element.175), channel_id=1, source_target_pairs={{0,4},{1,5},{2,6},{3,7},{4,0},{5,1},{6,2},{7,3},{8,12},{9,13},{10,... | collective-permute-start | bytes 1105928 | tf_op jit(solution)/shard_map/ppermute | solution.py:632
  85.6 5.1 %grad_heads.1 = (bf16[2,4,80,384]{3,2,1,0:T(8,128)(2,1)S(1)}, bf16[2,4,80,384]{3,2,1,0:T(8,128)(2,1)S(1)}, bf16[2,4,80,384]{3,2,1,0:T(8,128)(2,1)S(1)}, bf16[2,4,80,384]{3,2,1,0:T(8,128)(2,1)S(1)}) custom-call(s32[9]{0:T(128)S(1)} %concatenate.3.scal, bf16[4,192,512]{2,1,0:T(8,128)(2,1)S(1)} %get-tuple-element.125.a_own, ...), custom_call_target="tpu_custom_call" | custom-call | flops 115000000 | bytes 1 | tf_op jit(solution)/shard_map/grad_heads/pallas_call | solution.py:56
  91.8 5.3 %input_grad.1 = f32[512,768]{1,0:T(8,128)} custom-call(s32[9]{0:T(128)S(1)} %concatenate.3.scal, f32[512,768]{1,0:T(8,128)S(1)} %get-tuple-element.187.first, bf16[3,256,384]{2,1,0:T(8,128)(2,1)S(1)} %get-tuple-element.168.own_early.keep_early, bf16[3,256,384]{2,1,0:T(8,128)(2,1)S(1)} %get-tuple-element.177.own_late.keep_late, ...), custom_call_target="tpu_custom_call" | custom-call | flops 115000000 | bytes 1 | tf_op jit(solution)/shard_map/input_grad/pallas_call | solution.py:56
  97.1 4.5 %collective-permute-done.13.got = bf16[2,2,2,96,384]{4,3,2,1,0:T(8,128)(2,1)S(1)} collective-permute-done((bf16[2,2,2,96,384]{4,3,2,1,0:T(8,128)(2,1)S(1)}, bf16[2,2,2,96,384]{4,3,2,1,0:T(8,128)(2,1)S(1)}, u32[]{:S(2)}, u32[]{:S(2)}) %collective-permute-start.13) | collective-permute-done | bytes 589856 | tf_op jit(solution)/shard_map/ppermute | solution.py:632
  101.6 0.6 grad_reduce_add2.1
  102.2 0.8 grad_expand_add2.1
  103.2 1.4 %collective-permute-start.21 = (bf16[2,2,96,384]{3,2,1,0:T(8,128)(2,1)S(1)}, bf16[2,2,96,384]{3,2,1,0:T(8,128)(2,1)S(1)}, u32[]{:S(2)}, u32[]{:S(2)}) collective-permute-start(bf16[2,2,96,384]{3,2,1,0:T(8,128)(2,1)S(1)} %get-tuple-element.206), channel_id=1, source_target_pairs={{0,1},{1,0},{2,3},{3,2},{4,5},{5,4},{6,7},{7,6},{8,9},{9,8},{10,11... | collective-permute-start | bytes 884744 | tf_op jit(solution)/shard_map/ppermute | solution.py:632
  104.6 0.7 grad_heads_add1.1
  105.3 0.7 collective-permute-start.20
  106.0 1.4 %collective-permute-start.19 = (bf16[4,80,384]{2,1,0:T(8,128)(2,1)S(1)}, bf16[4,80,384]{2,1,0:T(8,128)(2,1)S(1)}, u32[]{:S(2)}, u32[]{:S(2)}) collective-permute-start(bf16[4,80,384]{2,1,0:T(8,128)(2,1)S(1)} %get-tuple-element.198), channel_id=1, source_target_pairs={{0,4},{1,5},{2,6},{3,7},{4,0},{5,1},{6,2},{7,3},{8,12},{9,13},{10,... | collective-permute-start | bytes 737288 | tf_op jit(solution)/shard_map/ppermute | solution.py:632
  107.4 6.0 %collective-permute-done.18.got = bf16[2,2,120,384]{3,2,1,0:T(8,128)(2,1)S(1)} collective-permute-done((bf16[2,2,120,384]{3,2,1,0:T(8,128)(2,1)S(1)}, bf16[2,2,120,384]{3,2,1,0:T(8,128)(2,1)S(1)}, u32[]{:S(2)}, u32[]{:S(2)}) %collective-permute-start.18) | collective-permute-done | bytes 368672 | tf_op jit(solution)/shard_map/ppermute | solution.py:632
  113.4 0.6 grad_expand_add3.1
  114.0 1.4 %collective-permute-start.22 = (bf16[2,120,384]{2,1,0:T(8,128)(2,1)S(1)}, bf16[2,120,384]{2,1,0:T(8,128)(2,1)S(1)}, u32[]{:S(2)}, u32[]{:S(2)}) collective-permute-start(bf16[2,120,384]{2,1,0:T(8,128)(2,1)S(1)} %get-tuple-element.209), channel_id=1, source_target_pairs={{0,16},{1,17},{2,18},{3,19},{4,20},{5,21},{6,22},{7,23},{8,24},{9,... | collective-permute-start | bytes 552968 | tf_op jit(solution)/shard_map/ppermute | solution.py:632
  115.4 1.7 %collective-permute-done.20.ym = bf16[4,80,384]{2,1,0:T(8,128)(2,1)S(1)} collective-permute-done((bf16[4,80,384]{2,1,0:T(8,128)(2,1)S(1)}, bf16[4,80,384]{2,1,0:T(8,128)(2,1)S(1)}, u32[]{:S(2)}, u32[]{:S(2)}) %collective-permute-start.20) | collective-permute-done | bytes 245792 | tf_op jit(solution)/shard_map/ppermute | solution.py:632
  117.1 0.7 grad_heads_add2.1
  118.5 1.5 %collective-permute-start.23 = (bf16[2,96,384]{2,1,0:T(8,128)(2,1)S(1)}, bf16[2,96,384]{2,1,0:T(8,128)(2,1)S(1)}, u32[]{:S(2)}, u32[]{:S(2)}) collective-permute-start(bf16[2,96,384]{2,1,0:T(8,128)(2,1)S(1)} %get-tuple-element.212), channel_id=1, source_target_pairs={{0,4},{1,5},{2,6},{3,7},{4,0},{5,1},{6,2},{7,3},{8,12},{9,13},{10,... | collective-permute-start | bytes 442376 | tf_op jit(solution)/shard_map/ppermute | solution.py:632
  119.9 0.7 collective-permute-start.24
  120.6 3.1 %collective-permute-start.25 = (bf16[2,80,384]{2,1,0:T(8,128)(2,1)S(1)}, bf16[2,80,384]{2,1,0:T(8,128)(2,1)S(1)}, u32[]{:S(2)}, u32[]{:S(2)}) collective-permute-start(bf16[2,80,384]{2,1,0:T(8,128)(2,1)S(1)} %get-tuple-element.216), channel_id=1, source_target_pairs={{0,16},{1,17},{2,18},{3,19},{4,20},{5,21},{6,22},{7,23},{8,24},{9,... | collective-permute-start | bytes 368648 | tf_op jit(solution)/shard_map/ppermute | solution.py:632
  123.7 1.1 collective-permute-start.26
  126.6 3.6 %collective-permute-done.24.z1 = bf16[2,80,384]{2,1,0:T(8,128)(2,1)S(1)} collective-permute-done((bf16[2,80,384]{2,1,0:T(8,128)(2,1)S(1)}, bf16[2,80,384]{2,1,0:T(8,128)(2,1)S(1)}, u32[]{:S(2)}, u32[]{:S(2)}) %collective-permute-start.24) | collective-permute-done | bytes 122912 | tf_op jit(solution)/shard_map/ppermute | solution.py:632
  130.2 3.0 %collective-permute-done.25.z2 = bf16[2,80,384]{2,1,0:T(8,128)(2,1)S(1)} collective-permute-done((bf16[2,80,384]{2,1,0:T(8,128)(2,1)S(1)}, bf16[2,80,384]{2,1,0:T(8,128)(2,1)S(1)}, u32[]{:S(2)}, u32[]{:S(2)}) %collective-permute-start.25) | collective-permute-done | bytes 122912 | tf_op jit(solution)/shard_map/ppermute | solution.py:632
  133.2 0.6 grad_heads_add3.1
  133.9 1.3 collective-permute-done.27.got
  135.3 1.5 %finish.1 = (f32[24,2304]{1,0:T(8,128)}, f32[96,768]{1,0:T(8,128)}, f32[24,3072]{1,0:T(8,128)}, f32[24,768]{1,0:T(8,128)}, f32[1,48]{1,0:T(1,128)}, /*index=5*/f...) custom-call(s32[9]{0:T(128)S(1)} %concatenate.3.scal, ...), custom_call_target="tpu_custom_call" | custom-call | flops 115000000 | bytes 1 | tf_op jit(solution)/shard_map/finish/pallas_call | solution.py:56
  (81 shorter events, 6.5 us)
Async XLA Ops:
  2.1 2.0 %copy-start = (bf16[768,2304]{1,0:T(8,128)(2,1)S(1)}, bf16[768,2304]{1,0:T(8,128)(2,1)}, u32[]{:S(2)}) copy-start(bf16[768,2304]{1,0:T(8,128)(2,1)} %w_send.1) | copy-start | bytes 10616836
  4.1 1.1 copy-start.3
  5.3 13.4 %slice-start = ((s8[4718592]{0:T(1024)(128)(4,1)}), s8[4194304]{0:T(1024)(128)(4,1)S(1)}, s32[]{:S(2)}) async-start(s8[4718592]{0:T(1024)(128)(4,1)} %bitcast.14), calls=%async_computation | async-start | bytes 8388608
  5.3 13.4 %slice-start.2 = ((s8[4718592]{0:T(1024)(128)(4,1)}), s8[4194304]{0:T(1024)(128)(4,1)S(1)}, s32[]{:S(2)}) async-start(s8[4718592]{0:T(1024)(128)(4,1)} %bitcast.16), calls=%async_computation.2 | async-start | bytes 8388608
  9.4 9.0 %collective-permute-start = (bf16[4,192,512]{2,1,0:T(8,128)(2,1)S(1)}, bf16[4,192,512]{2,1,0:T(8,128)(2,1)S(1)}, u32[]{:S(2)}, u32[]{:S(2)}) collective-permute-start(bf16[4,192,512]{2,1,0:T(8,128)(2,1)S(1)} %get-tuple-element.125.a_own), channel_id=1, source_target_pairs={{0,2},{1,3},{2,0},{3,1},{4,6},{5,7},{6,4},{7,5},{8,10},{9,11},{10,... | collective-permute-start | bytes 2359304 | tf_op jit(solution)/shard_map/ppermute | solution.py:632
  9.9 8.8 %collective-permute-start.1 = (bf16[7,128,128]{2,1,0:T(8,128)(2,1)S(1)}, bf16[7,128,128]{2,1,0:T(8,128)(2,1)S(1)}, u32[]{:S(2)}, u32[]{:S(2)}) collective-permute-start(bf16[7,128,128]{2,1,0:T(8,128)(2,1)S(1)} %get-tuple-element.134), channel_id=1, source_target_pairs={{0,1},{1,0},{2,3},{3,2},{4,5},{5,4},{6,7},{7,6},{8,9},{9,8},{10,11... | collective-permute-start | bytes 688136 | tf_op jit(solution)/shard_map/ppermute | solution.py:632
  12.4 5.8 %copy-start.7 = (bf16[768]{0:T(1024)(128)(2,1)S(1)}, bf16[768]{0:T(1024)(128)(2,1)}, u32[]{:S(2)}) copy-start(bf16[768]{0:T(1024)(128)(2,1)} %param.20) | copy-start | bytes 4612
  12.4 5.8 %copy-start.8 = (bf16[768]{0:T(1024)(128)(2,1)S(1)}, bf16[768]{0:T(1024)(128)(2,1)}, u32[]{:S(2)}) copy-start(bf16[768]{0:T(1024)(128)(2,1)} %param.19) | copy-start | bytes 4612
  12.4 5.8 %copy-start.9 = (bf16[768]{0:T(1024)(128)(2,1)S(1)}, bf16[768]{0:T(1024)(128)(2,1)}, u32[]{:S(2)}) copy-start(bf16[768]{0:T(1024)(128)(2,1)} %param.21) | copy-start | bytes 4612
  12.4 5.9 %copy-start.10 = (bf16[768]{0:T(1024)(128)(2,1)S(1)}, bf16[768]{0:T(1024)(128)(2,1)}, u32[]{:S(2)}) copy-start(bf16[768]{0:T(1024)(128)(2,1)} %param.25) | copy-start | bytes 4612
  12.5 5.9 %copy-start.6 = (bf16[3072]{0:T(1024)(128)(2,1)S(1)}, bf16[3072]{0:T(1024)(128)(2,1)}, u32[]{:S(2)}) copy-start(bf16[3072]{0:T(1024)(128)(2,1)} %param.23) | copy-start | bytes 18436
  12.5 6.2 %slice-start.1 = ((s8[4718592]{0:T(1024)(128)(4,1)}), s8[524288]{0:T(1024)(128)(4,1)S(1)}, s32[]{:S(2)}) async-start(s8[4718592]{0:T(1024)(128)(4,1)} %bitcast.14), calls=%async_computation.1 | async-start | bytes 1048576
  12.5 6.2 %slice-start.3 = ((s8[4718592]{0:T(1024)(128)(4,1)}), s8[524288]{0:T(1024)(128)(4,1)S(1)}, s32[]{:S(2)}) async-start(s8[4718592]{0:T(1024)(128)(4,1)} %bitcast.16), calls=%async_computation.3 | async-start | bytes 1048576
  12.5 6.2 %copy-start.2 = (bf16[768,768]{1,0:T(8,128)(2,1)S(1)}, bf16[768,768]{1,0:T(8,128)(2,1)}, u32[]{:S(2)}) copy-start(bf16[768,768]{1,0:T(8,128)(2,1)} %w_merge.1) | copy-start | bytes 3538948
  12.5 6.2 %copy-start.4 = (bf16[512,768]{1,0:T(8,128)(2,1)S(1)}, bf16[512,768]{1,0:T(8,128)(2,1)}, u32[]{:S(2)}) copy-start(bf16[512,768]{1,0:T(8,128)(2,1)} %refs_5_.1) | copy-start | bytes 2359300
  18.7 10.9 %copy-start.11 = (bf16[768]{0:T(1024)(128)(2,1)S(1)}, bf16[768]{0:T(1024)(128)(2,1)}, u32[]{:S(2)}) copy-start(bf16[768]{0:T(1024)(128)(2,1)} %param.26) | copy-start | bytes 4612
  18.7 10.9 %copy-start.12 = (bf16[768]{0:T(1024)(128)(2,1)S(1)}, bf16[768]{0:T(1024)(128)(2,1)}, u32[]{:S(2)}) copy-start(bf16[768]{0:T(1024)(128)(2,1)} %param.27) | copy-start | bytes 4612
  18.7 10.9 %copy-start.5 = (bf16[512,768]{1,0:T(8,128)(2,1)S(1)}, bf16[512,768]{1,0:T(8,128)(2,1)}, u32[]{:S(2)}) copy-start(bf16[512,768]{1,0:T(8,128)(2,1)} %cot.1) | copy-start | bytes 2359300
  29.1 9.4 %collective-permute-start.3 = (bf16[512,3072]{1,0:T(8,128)(2,1)S(1)}, bf16[512,3072]{1,0:T(8,128)(2,1)S(1)}, u32[]{:S(2)}, u32[]{:S(2)}) collective-permute-start(bf16[512,3072]{1,0:T(8,128)(2,1)S(1)} %get-tuple-element.143.a_own), channel_id=1, source_target_pairs={{0,2},{1,3},{2,0},{3,1},{4,6},{5,7},{6,4},{7,5},{8,10},{9,11},{10,... | collective-permute-start | bytes 9437192 | tf_op jit(solution)/shard_map/ppermute | solution.py:632
  29.1 9.3 %collective-permute-start.2 = (bf16[2,4,192,512]{3,2,1,0:T(8,128)(2,1)S(1)}, bf16[2,4,192,512]{3,2,1,0:T(8,128)(2,1)S(1)}, u32[]{:S(2)}, u32[]{:S(2)}) collective-permute-start(bf16[2,4,192,512]{3,2,1,0:T(8,128)(2,1)S(1)} %get-tuple-element.137.a_own.m_own), channel_id=1, source_target_pairs={{0,2},{1,3},{2,0},{3,1},{4,6},{5,7},{6,4},{7,5},{8,10},{9,11},{10,... | collective-permute-start | bytes 4718600 | tf_op jit(solution)/shard_map/ppermute | solution.py:632
  32.2 6.2 %collective-permute-start.4 = (bf16[512,384]{1,0:T(8,128)(2,1)S(1)}, bf16[512,384]{1,0:T(8,128)(2,1)S(1)}, u32[]{:S(2)}, u32[]{:S(2)}) collective-permute-start(bf16[512,384]{1,0:T(8,128)(2,1)S(1)} %get-tuple-element.145), channel_id=1, source_target_pairs={{0,2},{1,3},{2,0},{3,1},{4,6},{5,7},{6,4},{7,5},{8,10},{9,11},{10,... | collective-permute-start | bytes 1179656 | tf_op jit(solution)/shard_map/ppermute | solution.py:632
  37.8 18.2 %collective-permute-start.5 = (bf16[2,512,768]{2,1,0:T(8,128)(2,1)S(1)}, bf16[2,512,768]{2,1,0:T(8,128)(2,1)S(1)}, u32[]{:S(2)}, u32[]{:S(2)}) collective-permute-start(bf16[2,512,768]{2,1,0:T(8,128)(2,1)S(1)} %get-tuple-element.153), channel_id=1, source_target_pairs={{0,2},{1,3},{2,0},{3,1},{4,6},{5,7},{6,4},{7,5},{8,10},{9,11},{10,... | collective-permute-start | bytes 4718600 | tf_op jit(solution)/shard_map/ppermute | solution.py:632
  43.8 28.1 %collective-permute-start.8 = (bf16[2,2,2,2,96,384]{5,4,3,2,1,0:T(8,128)(2,1)S(1)}, bf16[2,2,2,2,96,384]{5,4,3,2,1,0:T(8,128)(2,1)S(1)}, u32[]{:S(2)}, u32[]{:S(2)}) collective-permute-start(bf16[2,2,2,2,96,384]{5,4,3,2,1,0:T(8,128)(2,1)S(1)} %get-tuple-element.146), channel_id=1, source_target_pairs={{0,8},{1,9},{2,10},{3,11},{4,12},{5,13},{6,14},{7,15},{8,0},{9,1},... | collective-permute-start | bytes 3538952 | tf_op jit(solution)/shard_map/ppermute | solution.py:632
  54.4 1.8 %collective-permute-start.6 = (bf16[512,384]{1,0:T(8,128)(2,1)S(1)}, bf16[512,384]{1,0:T(8,128)(2,1)S(1)}, u32[]{:S(2)}, u32[]{:S(2)}) collective-permute-start(bf16[512,384]{1,0:T(8,128)(2,1)S(1)} %get-tuple-element.155), channel_id=1, source_target_pairs={{0,2},{1,3},{2,0},{3,1},{4,6},{5,7},{6,4},{7,5},{8,10},{9,11},{10,... | collective-permute-start | bytes 1179656 | tf_op jit(solution)/shard_map/ppermute | solution.py:632
  54.5 8.0 %collective-permute-start.7 = (bf16[7,128,128]{2,1,0:T(8,128)(2,1)S(1)}, bf16[7,128,128]{2,1,0:T(8,128)(2,1)S(1)}, u32[]{:S(2)}, u32[]{:S(2)}) collective-permute-start(bf16[7,128,128]{2,1,0:T(8,128)(2,1)S(1)} %get-tuple-element.157), channel_id=1, source_target_pairs={{0,1},{1,0},{2,3},{3,2},{4,5},{5,4},{6,7},{7,6},{8,9},{9,8},{10,11... | collective-permute-start | bytes 688136 | tf_op jit(solution)/shard_map/ppermute | solution.py:632
  62.5 19.3 %collective-permute-start.9 = (bf16[2,4,120,384]{3,2,1,0:T(8,128)(2,1)S(1)}, bf16[2,4,120,384]{3,2,1,0:T(8,128)(2,1)S(1)}, u32[]{:S(2)}, u32[]{:S(2)}) collective-permute-start(bf16[2,4,120,384]{3,2,1,0:T(8,128)(2,1)S(1)} %get-tuple-element.171), channel_id=1, source_target_pairs={{0,1},{1,0},{2,3},{3,2},{4,5},{5,4},{6,7},{7,6},{8,9},{9,8},{10,11... | collective-permute-start | bytes 2211848 | tf_op jit(solution)/shard_map/ppermute | solution.py:632
  64.0 17.8 %collective-permute-start.10 = (bf16[2,4,120,384]{3,2,1,0:T(8,128)(2,1)S(1)}, bf16[2,4,120,384]{3,2,1,0:T(8,128)(2,1)S(1)}, u32[]{:S(2)}, u32[]{:S(2)}) collective-permute-start(bf16[2,4,120,384]{3,2,1,0:T(8,128)(2,1)S(1)} %get-tuple-element.174), channel_id=1, source_target_pairs={{0,4},{1,5},{2,6},{3,7},{4,0},{5,1},{6,2},{7,3},{8,12},{9,13},{10,... | collective-permute-start | bytes 2211848 | tf_op jit(solution)/shard_map/ppermute | solution.py:632
  71.3 14.3 %collective-permute-start.12 = (bf16[3,256,384]{2,1,0:T(8,128)(2,1)S(1)}, bf16[3,256,384]{2,1,0:T(8,128)(2,1)S(1)}, u32[]{:S(2)}, u32[]{:S(2)}) collective-permute-start(bf16[3,256,384]{2,1,0:T(8,128)(2,1)S(1)} %get-tuple-element.178.send_late), channel_id=1, source_target_pairs={{0,2},{1,3},{2,0},{3,1},{4,6},{5,7},{6,4},{7,5},{8,10},{9,11},{10,... | collective-permute-start | bytes 1769480 | tf_op jit(solution)/shard_map/ppermute | solution.py:632
  71.3 14.2 %collective-permute-start.11 = (bf16[3,256,384]{2,1,0:T(8,128)(2,1)S(1)}, bf16[3,256,384]{2,1,0:T(8,128)(2,1)S(1)}, u32[]{:S(2)}, u32[]{:S(2)}) collective-permute-start(bf16[3,256,384]{2,1,0:T(8,128)(2,1)S(1)} %get-tuple-element.161.send_early), channel_id=1, source_target_pairs={{0,2},{1,3},{2,0},{3,1},{4,6},{5,7},{6,4},{7,5},{8,10},{9,11},{10,... | collective-permute-start | bytes 1769480 | tf_op jit(solution)/shard_map/ppermute | solution.py:632
  72.7 28.9 %collective-permute-start.13 = (bf16[2,2,2,96,384]{4,3,2,1,0:T(8,128)(2,1)S(1)}, bf16[2,2,2,96,384]{4,3,2,1,0:T(8,128)(2,1)S(1)}, u32[]{:S(2)}, u32[]{:S(2)}) collective-permute-start(bf16[2,2,2,96,384]{4,3,2,1,0:T(8,128)(2,1)S(1)} %get-tuple-element.189), channel_id=1, source_target_pairs={{0,16},{1,17},{2,18},{3,19},{4,20},{5,21},{6,22},{7,23},{8,24},{9,... | collective-permute-start | bytes 1769480 | tf_op jit(solution)/shard_map/ppermute | solution.py:632
  82.5 19.7 %collective-permute-start.15 = (bf16[4,120,384]{2,1,0:T(8,128)(2,1)S(1)}, bf16[4,120,384]{2,1,0:T(8,128)(2,1)S(1)}, u32[]{:S(2)}, u32[]{:S(2)}) collective-permute-start(bf16[4,120,384]{2,1,0:T(8,128)(2,1)S(1)} %get-tuple-element.192), channel_id=1, source_target_pairs={{0,1},{1,0},{2,3},{3,2},{4,5},{5,4},{6,7},{7,6},{8,9},{9,8},{10,11... | collective-permute-start | bytes 1105928 | tf_op jit(solution)/shard_map/ppermute | solution.py:632
  84.0 18.2 %collective-permute-start.14 = (bf16[4,120,384]{2,1,0:T(8,128)(2,1)S(1)}, bf16[4,120,384]{2,1,0:T(8,128)(2,1)S(1)}, u32[]{:S(2)}, u32[]{:S(2)}) collective-permute-start(bf16[4,120,384]{2,1,0:T(8,128)(2,1)S(1)} %get-tuple-element.175), channel_id=1, source_target_pairs={{0,4},{1,5},{2,6},{3,7},{4,0},{5,1},{6,2},{7,3},{8,12},{9,13},{10,... | collective-permute-start | bytes 1105928 | tf_op jit(solution)/shard_map/ppermute | solution.py:632
  85.6 6.3 %copy-start.1 = (bf16[768,2304]{1,0:T(8,128)(2,1)S(1)}, bf16[768,2304]{1,0:T(8,128)(2,1)}, u32[]{:S(2)}) copy-start(bf16[768,2304]{1,0:T(8,128)(2,1)} %w_send.1) | copy-start | bytes 10616836
  90.7 13.9 %collective-permute-start.17 = (bf16[2,4,80,384]{3,2,1,0:T(8,128)(2,1)S(1)}, bf16[2,4,80,384]{3,2,1,0:T(8,128)(2,1)S(1)}, u32[]{:S(2)}, u32[]{:S(2)}) collective-permute-start(bf16[2,4,80,384]{3,2,1,0:T(8,128)(2,1)S(1)} %get-tuple-element.197), channel_id=1, source_target_pairs={{0,4},{1,5},{2,6},{3,7},{4,0},{5,1},{6,2},{7,3},{8,12},{9,13},{10,... | collective-permute-start | bytes 1474568 | tf_op jit(solution)/shard_map/ppermute | solution.py:632
  91.3 13.3 %collective-permute-start.16 = (bf16[2,4,80,384]{3,2,1,0:T(8,128)(2,1)S(1)}, bf16[2,4,80,384]{3,2,1,0:T(8,128)(2,1)S(1)}, u32[]{:S(2)}, u32[]{:S(2)}) collective-permute-start(bf16[2,4,80,384]{3,2,1,0:T(8,128)(2,1)S(1)} %get-tuple-element.185), channel_id=1, source_target_pairs={{0,1},{1,0},{2,3},{3,2},{4,5},{5,4},{6,7},{7,6},{8,9},{9,8},{10,11... | collective-permute-start | bytes 1474568 | tf_op jit(solution)/shard_map/ppermute | solution.py:632
  103.1 10.3 %collective-permute-start.18 = (bf16[2,2,120,384]{3,2,1,0:T(8,128)(2,1)S(1)}, bf16[2,2,120,384]{3,2,1,0:T(8,128)(2,1)S(1)}, u32[]{:S(2)}, u32[]{:S(2)}) collective-permute-start(bf16[2,2,120,384]{3,2,1,0:T(8,128)(2,1)S(1)} %get-tuple-element.200), channel_id=1, source_target_pairs={{0,8},{1,9},{2,10},{3,11},{4,12},{5,13},{6,14},{7,15},{8,0},{9,1},... | collective-permute-start | bytes 1105928 | tf_op jit(solution)/shard_map/ppermute | solution.py:632
  103.2 14.7 %collective-permute-start.21 = (bf16[2,2,96,384]{3,2,1,0:T(8,128)(2,1)S(1)}, bf16[2,2,96,384]{3,2,1,0:T(8,128)(2,1)S(1)}, u32[]{:S(2)}, u32[]{:S(2)}) collective-permute-start(bf16[2,2,96,384]{3,2,1,0:T(8,128)(2,1)S(1)} %get-tuple-element.206), channel_id=1, source_target_pairs={{0,1},{1,0},{2,3},{3,2},{4,5},{5,4},{6,7},{7,6},{8,9},{9,8},{10,11... | collective-permute-start | bytes 884744 | tf_op jit(solution)/shard_map/ppermute | solution.py:632
  105.3 11.9 %collective-permute-start.20 = (bf16[4,80,384]{2,1,0:T(8,128)(2,1)S(1)}, bf16[4,80,384]{2,1,0:T(8,128)(2,1)S(1)}, u32[]{:S(2)}, u32[]{:S(2)}) collective-permute-start(bf16[4,80,384]{2,1,0:T(8,128)(2,1)S(1)} %get-tuple-element.203), channel_id=1, source_target_pairs={{0,1},{1,0},{2,3},{3,2},{4,5},{5,4},{6,7},{7,6},{8,9},{9,8},{10,11... | collective-permute-start | bytes 737288 | tf_op jit(solution)/shard_map/ppermute | solution.py:632
  106.0 11.2 %collective-permute-start.19 = (bf16[4,80,384]{2,1,0:T(8,128)(2,1)S(1)}, bf16[4,80,384]{2,1,0:T(8,128)(2,1)S(1)}, u32[]{:S(2)}, u32[]{:S(2)}) collective-permute-start(bf16[4,80,384]{2,1,0:T(8,128)(2,1)S(1)} %get-tuple-element.198), channel_id=1, source_target_pairs={{0,4},{1,5},{2,6},{3,7},{4,0},{5,1},{6,2},{7,3},{8,12},{9,13},{10,... | collective-permute-start | bytes 737288 | tf_op jit(solution)/shard_map/ppermute | solution.py:632
  114.0 10.8 %collective-permute-start.22 = (bf16[2,120,384]{2,1,0:T(8,128)(2,1)S(1)}, bf16[2,120,384]{2,1,0:T(8,128)(2,1)S(1)}, u32[]{:S(2)}, u32[]{:S(2)}) collective-permute-start(bf16[2,120,384]{2,1,0:T(8,128)(2,1)S(1)} %get-tuple-element.209), channel_id=1, source_target_pairs={{0,16},{1,17},{2,18},{3,19},{4,20},{5,21},{6,22},{7,23},{8,24},{9,... | collective-permute-start | bytes 552968 | tf_op jit(solution)/shard_map/ppermute | solution.py:632
  118.5 7.0 %collective-permute-start.23 = (bf16[2,96,384]{2,1,0:T(8,128)(2,1)S(1)}, bf16[2,96,384]{2,1,0:T(8,128)(2,1)S(1)}, u32[]{:S(2)}, u32[]{:S(2)}) collective-permute-start(bf16[2,96,384]{2,1,0:T(8,128)(2,1)S(1)} %get-tuple-element.212), channel_id=1, source_target_pairs={{0,4},{1,5},{2,6},{3,7},{4,0},{5,1},{6,2},{7,3},{8,12},{9,13},{10,... | collective-permute-start | bytes 442376 | tf_op jit(solution)/shard_map/ppermute | solution.py:632
  119.9 10.2 %collective-permute-start.24 = (bf16[2,80,384]{2,1,0:T(8,128)(2,1)S(1)}, bf16[2,80,384]{2,1,0:T(8,128)(2,1)S(1)}, u32[]{:S(2)}, u32[]{:S(2)}) collective-permute-start(bf16[2,80,384]{2,1,0:T(8,128)(2,1)S(1)} %get-tuple-element.215), channel_id=1, source_target_pairs={{0,8},{1,9},{2,10},{3,11},{4,12},{5,13},{6,14},{7,15},{8,0},{9,1},... | collective-permute-start | bytes 368648 | tf_op jit(solution)/shard_map/ppermute | solution.py:632
  120.6 12.6 %collective-permute-start.25 = (bf16[2,80,384]{2,1,0:T(8,128)(2,1)S(1)}, bf16[2,80,384]{2,1,0:T(8,128)(2,1)S(1)}, u32[]{:S(2)}, u32[]{:S(2)}) collective-permute-start(bf16[2,80,384]{2,1,0:T(8,128)(2,1)S(1)} %get-tuple-element.216), channel_id=1, source_target_pairs={{0,16},{1,17},{2,18},{3,19},{4,20},{5,21},{6,22},{7,23},{8,24},{9,... | collective-permute-start | bytes 368648 | tf_op jit(solution)/shard_map/ppermute | solution.py:632
  123.7 9.5 %collective-permute-start.26 = (bf16[2,80,384]{2,1,0:T(8,128)(2,1)S(1)}, bf16[2,80,384]{2,1,0:T(8,128)(2,1)S(1)}, u32[]{:S(2)}, u32[]{:S(2)}) collective-permute-start(bf16[2,80,384]{2,1,0:T(8,128)(2,1)S(1)} %get-tuple-element.217), channel_id=1, source_target_pairs={{0,24},{1,25},{2,26},{3,27},{4,28},{5,29},{6,30},{7,31},{8,16},{9,... | collective-permute-start | bytes 368648 | tf_op jit(solution)/shard_map/ppermute | solution.py:632
  125.4 9.9 %collective-permute-start.29 = (f32[120,384]{1,0:T(8,128)S(1)}, f32[120,384]{1,0:T(8,128)S(1)}, u32[]{:S(2)}, u32[]{:S(2)}) collective-permute-start(f32[120,384]{1,0:T(8,128)S(1)} %get-tuple-element.221), channel_id=1, source_target_pairs={{0,2},{1,3},{2,0},{3,1},{4,6},{5,7},{6,4},{7,5},{8,10},{9,11},{10,... | collective-permute-start | bytes 552968 | tf_op jit(solution)/shard_map/ppermute | solution.py:632
  126.1 9.2 %collective-permute-start.28 = (f32[96,384]{1,0:T(8,128)S(1)}, f32[96,384]{1,0:T(8,128)S(1)}, u32[]{:S(2)}, u32[]{:S(2)}) collective-permute-start(f32[96,384]{1,0:T(8,128)S(1)} %get-tuple-element.220), channel_id=1, source_target_pairs={{0,2},{1,3},{2,0},{3,1},{4,6},{5,7},{6,4},{7,5},{8,10},{9,11},{10,... | collective-permute-start | bytes 442376 | tf_op jit(solution)/shard_map/ppermute | solution.py:632
  133.8 1.4 %collective-permute-start.27 = (f32[80,384]{1,0:T(8,128)S(1)}, f32[80,384]{1,0:T(8,128)S(1)}, u32[]{:S(2)}, u32[]{:S(2)}) collective-permute-start(f32[80,384]{1,0:T(8,128)S(1)} %get-tuple-element.219), channel_id=1, source_target_pairs={{0,2},{1,3},{2,0},{3,1},{4,6},{5,7},{6,4},{7,5},{8,10},{9,11},{10,... | collective-permute-start | bytes 368648 | tf_op jit(solution)/shard_map/ppermute | solution.py:632

commit v2 on v1

--- a/solution.py
+++ b/solution.py
@@ -589,11 +589,10 @@
     pos_at, scal, a_own, a_oth, own_early, own_late, oth_early, oth_late, kept_h, sent_h, sums_1, kept_e, sent_e, sums_2, *refs, devices
 ):
     outs, table = refs[:-1], refs[-1]
-    tz = pl.program_id(0)
     x, y, z = (scal[pos_at + n] for n in range(3))
     width = outs[0].shape[-1]
 
-    @pl.when(tz == 0)
+    @pl.when(pl.program_id(0) == 0)
     def _():
         first_core = scal[pos_at - 1] == 0
         ordered = lambda kept, sent: [jnp.where(first_core, kept, sent), jnp.where(first_core, sent, kept)]
@@ -612,15 +611,18 @@
     join = lambda early, late: jnp.concatenate(
         [jnp.concatenate([early[n], late[n]], axis=0) for n in range(early.shape[0])], axis=1
     )
-    values = dot(a_own[0], join(own_early, own_late)) + dot(a_oth[0], join(oth_early, oth_late))
+    own, other = join(own_early, own_late), join(oth_early, oth_late)
     line = lax.broadcasted_iota(jnp.int32, (8, width), 0)
-    rows8 = table[pl.ds(pl.multiple_of(tz * 8, 8), 8)]
-    extra = []
-    for n in range(8):
-        high, low = high_low(rows8[n : n + 1])
-        extra.append(jnp.where(line == 0, high, jnp.where(line == 1, low, 0.0)))
-    pieces = place(values, values.shape[0] // 8, tz, (0, 1), x, y, z, extra, outs)
-    place_y(pieces, tz, (0, 1), x, y, z, outs)
+    for half in range(2):
+        tz = 2 * pl.program_id(0) + half
+        values = dot(a_own[half], own) + dot(a_oth[half], other)
+        rows8 = table[pl.ds(pl.multiple_of(tz * 8, 8), 8)]
+        extra = []
+        for n in range(8):
+            high, low = high_low(rows8[n : n + 1])
+            extra.append(jnp.where(line == 0, high, jnp.where(line == 1, low, 0.0)))
+        pieces = place(values, values.shape[0] // 8, tz, (0, 1), x, y, z, extra, outs)
+        place_y(pieces, tz, (0, 1), x, y, z, outs)
 
 
 class Ring:
@@ -977,7 +979,7 @@
     small, large = D // devices, FF // devices
     whole = lambda a: (a, None, None)
     part = lambda a, n: (a, (1, 2, D // 4, rows), lambda j, s: (n, j, 0, 0))
-    by_z = lambda a: (a, (1, D // 4, rows), lambda j, s: (j, 0, 0))
+    by_z = lambda a: (a, (2, D // 4, rows), lambda j, s: (j, 0, 0))
     by_col = lambda a: (a, (rows, FF // 4), lambda j, s: (0, j))
 
     def group(kernel, name, scal, grid, ins, piece_rows, us, scratch=(), kind=Scatter):
@@ -1068,7 +1070,7 @@
         order = after(scal, expanded.first(after(scal, pj_keep[0])))
         expanded.send_first()
         heads = group(
-            functools.partial(heads_grad_kernel, devices=devices), "grad_heads", order, (4,),
+            functools.partial(heads_grad_kernel, devices=devices), "grad_heads", order, (2,),
             [
                 by_z(tokens_t), by_z(tokens_o), *map(whole, (*pj_keep, *pj_o)),
                 *map(whole, (sum_heads_kept, sum_heads_sent, sums_first, sum_kept, sum_sent, sums_second)),

time: 138 us -> 138 us (level)
  transfers between devices with their start and end apart: 30 -> 30, of which waited for: 9 -> 9; matrix products, arithmetic and copies ran while one was open for 0% -> 0% of each run, Pallas kernels for 46% -> 45%
where the time goes in v2:
time: 138 us; the launch traced here: 137 us
  Pallas kernels  77.9 us (56%)
  starting transfers between devices  30.3 us (22%)
  waiting for transfers between devices  22.7 us (16%)
  local copies, waits for them, and re-layouts  4.69 us (3%)
    pallas_call x24, Pallas kernels, call(): pl.pallas_call(kernel, name=name, grid_spec=pltpu.PrefetchScalarGridSpec(...  77.9 us
    ppermute x30, starting transfers between devices, swap(): lax.ppermute(value, AXES, [(i, i ^ bits) for i in range(self.devices)])  30.3 us
    ppermute x30, waiting for transfers between devices, swap(): lax.ppermute(value, AXES, [(i, i ^ bits) for i in range(self.devices)])  22.7 us
    unnamed x34, local copies, waits for them, and re-layouts  3.21 us
  transfers between devices with their start and end apart: 30, of which 9 were waited for; matrix products, arithmetic and copies ran while one was open for 0% of the time, Pallas kernels for 45%

profile of v2, /device:TPU:0, one launch (start us, length us, event | category | flops | bytes accessed | tf_op | source)
XLA Modules:
  0.0 136.9 jit_solution(17782241382590902107)
XLA Ops:
  0.7 0.7 reshape.81.bk.bv.bq
  1.4 0.7 concatenate.3.scal
  2.1 2.0 %copy-done = bf16[768,2304]{1,0:T(8,128)(2,1)S(1)} copy-done((bf16[768,2304]{1,0:T(8,128)(2,1)S(1)}, bf16[768,2304]{1,0:T(8,128)(2,1)}, u32[]{:S(2)}) %copy-start) | copy-done | bytes 3538968
  4.1 1.1 copy-done.3
  5.3 4.1 %keys_values.1 = (bf16[512,768]{1,0:T(8,128)(2,1)S(1)}, bf16[512,768]{1,0:T(8,128)(2,1)S(1)}, bf16[7,128,128]{2,1,0:T(8,128)(2,1)S(1)}, f32[512,128]{1,0:T(8,128...) custom-call(s32[9]{0:T(128)S(1)} %concatenate.3.scal, bf16[512,768]{1,0:T(8,128)(2,1)S(1)} %copy-done.3, ...), custom_call_target="tpu_custom_call" | custom-call | flops 4600000000 | bytes 1 | tf_op jit(solution)/shard_map/keys_values/pallas_call | solution.py:56
  9.9 2.6 %collective-permute-start.1 = (bf16[7,128,128]{2,1,0:T(8,128)(2,1)S(1)}, bf16[7,128,128]{2,1,0:T(8,128)(2,1)S(1)}, u32[]{:S(2)}, u32[]{:S(2)}) collective-permute-start(bf16[7,128,128]{2,1,0:T(8,128)(2,1)S(1)} %get-tuple-element.134), channel_id=1, source_target_pairs={{0,1},{1,0},{2,3},{3,2},{4,5},{5,4},{6,7},{7,6},{8,9},{9,8},{10,11... | collective-permute-start | bytes 688136 | tf_op jit(solution)/shard_map/ppermute | solution.py:634
  12.5 5.7 %local_attention.1 = (bf16[512,768]{1,0:T(8,128)(2,1)S(1)}, f32[512,768]{1,0:T(8,128)S(1)}, f32[512,768]{1,0:T(8,128)S(1)}) custom-call(s32[9]{0:T(128)S(1)} %concatenate.3.scal, bf16[512,768]{1,0:T(8,128)(2,1)S(1)} %copy-done.3, bf16[768,2304]{1,0:T(8,128)(2,1)S(1)} %copy-done, bf16[1,2304]{1,0:T(2,128)(2,1)S(1)} %reshape.81.bk.bv.bq, ...), custom_call_target="tpu_custom_call" | custom-call | flops 6899999744 | bytes 1 | tf_op jit(solution)/shard_map/local_attention/pallas_call | solution.py:56
  18.7 10.3 %feed_forward.1 = (f32[512,768]{1,0:T(8,128)S(1)}, f32[512,768]{1,0:T(8,128)S(1)}, bf16[512,768]{1,0:T(8,128)(2,1)}, f32[512,768]{1,0:T(8,128)S(1)}, f32[512,128...) custom-call(s32[9]{0:T(128)S(1)} %concatenate.3.scal, ...), custom_call_target="tpu_custom_call" | custom-call | flops 12650000384 | bytes 1 | tf_op jit(solution)/shard_map/feed_forward/pallas_call | solution.py:56
  29.6 2.6 %second_norm.1 = (bf16[512,768]{1,0:T(8,128)(2,1)}, f32[512,768]{1,0:T(8,128)S(1)}, bf16[512,768]{1,0:T(8,128)(2,1)S(1)}, bf16[512,384]{1,0:T(8,128)(2,1)S(1)}, ...) custom-call(s32[9]{0:T(128)S(1)} %concatenate.3.scal, f32[512,768]{1,0:T(8,128)S(1)} %get-tuple-element.135.second, ...), custom_call_target="tpu_custom_call" | custom-call | flops 2990000128 | bytes 1 | tf_op jit(solution)/shard_map/second_norm/pallas_call | solution.py:56
  32.2 5.6 %feed_forward_back_sent.1 = (bf16[2,512,768]{2,1,0:T(8,128)(2,1)S(1)}, f32[1,1536]{1,0:T(1,128)S(1)}, f32[512,768]{1,0:T(8,128)S(1)}) custom-call(s32[9]{0:T(128)S(1)} %concatenate.3.scal, bf16[512,768]{1,0:T(8,128)(2,1)S(1)} %get-tuple-element.138.full, bf16[512,3072]{1,0:T(8,128)(2,1)S(1)} %get-tuple-element.139.slope, bf16[768,3072]{1,0:T(8,128)(2,1)S(1)} %bitcast.15, ...), custom_call_target="tpu_custom_call" | custom-call | flops 5750000128 | bytes 1 | tf_op jit(solution)/shard_map/feed_forward_back_sent/pallas_call | solution.py:56
  38.4 5.4 %grad_reduce.1 = (bf16[2,2,2,2,96,384]{5,4,3,2,1,0:T(8,128)(2,1)S(1)}, bf16[2,2,2,2,96,384]{5,4,3,2,1,0:T(8,128)(2,1)S(1)}) custom-call(s32[9]{0:T(128)S(1)} %concatenate.3.scal, bf16[512,3072]{1,0:T(8,128)(2,1)S(1)} %get-tuple-element.143.a_own, bf16[512,3072]{1,0:T(8,128)(2,1)S(1)} %collective-permute-done.3.a_oth, ...), custom_call_target="tpu_custom_call" | custom-call | flops 6899999744 | bytes 1 | tf_op jit(solution)/shard_map/grad_reduce/pallas_call | solution.py:56
  43.8 1.9 %collective-permute-start.8 = (bf16[2,2,2,2,96,384]{5,4,3,2,1,0:T(8,128)(2,1)S(1)}, bf16[2,2,2,2,96,384]{5,4,3,2,1,0:T(8,128)(2,1)S(1)}, u32[]{:S(2)}, u32[]{:S(2)}) collective-permute-start(bf16[2,2,2,2,96,384]{5,4,3,2,1,0:T(8,128)(2,1)S(1)} %get-tuple-element.146), channel_id=1, source_target_pairs={{0,8},{1,9},{2,10},{3,11},{4,12},{5,13},{6,14},{7,15},{8,0},{9,1},... | collective-permute-start | bytes 3538952 | tf_op jit(solution)/shard_map/ppermute | solution.py:634
  45.7 8.7 %feed_forward_back.1 = (bf16[2,512,768]{2,1,0:T(8,128)(2,1)S(1)}, f32[512,768]{1,0:T(8,128)S(1)}, bf16[512,384]{1,0:T(8,128)(2,1)S(1)}, bf16[512,384]{1,0:T(8,12...) custom-call(s32[9]{0:T(128)S(1)} %concatenate.3.scal, ...), custom_call_target="tpu_custom_call" | custom-call | flops 3449999872 | bytes 1 | tf_op jit(solution)/shard_map/feed_forward_back/pallas_call | solution.py:56
  54.5 1.6 %collective-permute-start.7 = (bf16[7,128,128]{2,1,0:T(8,128)(2,1)S(1)}, bf16[7,128,128]{2,1,0:T(8,128)(2,1)S(1)}, u32[]{:S(2)}, u32[]{:S(2)}) collective-permute-start(bf16[7,128,128]{2,1,0:T(8,128)(2,1)S(1)} %get-tuple-element.157), channel_id=1, source_target_pairs={{0,1},{1,0},{2,3},{3,2},{4,5},{5,4},{6,7},{7,6},{8,9},{9,8},{10,11... | collective-permute-start | bytes 688136 | tf_op jit(solution)/shard_map/ppermute | solution.py:634
  56.2 4.6 %grad_expand.1 = (bf16[2,4,120,384]{3,2,1,0:T(8,128)(2,1)S(1)}, bf16[2,4,120,384]{3,2,1,0:T(8,128)(2,1)S(1)}, bf16[2,4,120,384]{3,2,1,0:T(8,128)(2,1)S(1)}, bf16[2,4,120,384]{3,2,1,0:T(8,128)(2,1)S(1)}) custom-call(s32[9]{0:T(128)S(1)} %concatenate.3.scal, bf16[2,4,192,512]{3,2,1,0:T(8,128)(2,1)S(1)} %get-tuple-element.137.a_own.m_own, ...), custom_call_target="tpu_custom_call" | custom-call | flops 1150000000 | bytes 1 | tf_op jit(solution)/shard_map/grad_expand/pallas_call | solution.py:56
  60.7 1.7 %collective-permute-done.7.later = bf16[7,128,128]{2,1,0:T(8,128)(2,1)S(1)} collective-permute-done((bf16[7,128,128]{2,1,0:T(8,128)(2,1)S(1)}, bf16[7,128,128]{2,1,0:T(8,128)(2,1)S(1)}, u32[]{:S(2)}, u32[]{:S(2)}) %collective-permute-start.7) | collective-permute-done | bytes 229408 | tf_op jit(solution)/shard_map/ppermute | solution.py:634
  62.5 1.5 %collective-permute-start.9 = (bf16[2,4,120,384]{3,2,1,0:T(8,128)(2,1)S(1)}, bf16[2,4,120,384]{3,2,1,0:T(8,128)(2,1)S(1)}, u32[]{:S(2)}, u32[]{:S(2)}) collective-permute-start(bf16[2,4,120,384]{3,2,1,0:T(8,128)(2,1)S(1)} %get-tuple-element.171), channel_id=1, source_target_pairs={{0,1},{1,0},{2,3},{3,2},{4,5},{5,4},{6,7},{7,6},{8,9},{9,8},{10,11... | collective-permute-start | bytes 2211848 | tf_op jit(solution)/shard_map/ppermute | solution.py:634
  64.0 1.5 %collective-permute-start.10 = (bf16[2,4,120,384]{3,2,1,0:T(8,128)(2,1)S(1)}, bf16[2,4,120,384]{3,2,1,0:T(8,128)(2,1)S(1)}, u32[]{:S(2)}, u32[]{:S(2)}) collective-permute-start(bf16[2,4,120,384]{3,2,1,0:T(8,128)(2,1)S(1)} %get-tuple-element.174), channel_id=1, source_target_pairs={{0,4},{1,5},{2,6},{3,7},{4,0},{5,1},{6,2},{7,3},{8,12},{9,13},{10,... | collective-permute-start | bytes 2211848 | tf_op jit(solution)/shard_map/ppermute | solution.py:634
  65.5 5.8 %attention_back_sent.1 = (bf16[3,256,384]{2,1,0:T(8,128)(2,1)S(1)}, bf16[3,256,384]{2,1,0:T(8,128)(2,1)S(1)}, f32[3,8,384]{2,1,0:T(8,128)S(1)}, f32[512,512]{1,0:T(8,128)S(1)}, f32[512,512]{1,0:T(8,128)S(1)}) custom-call(s32[9]{0:T(128)S(1)} %concatenate.3.scal, bf16[512,768]{1,0:T(8,128)(2,1)S(1)} %get-tuple-element.131.refs_0_.rq, ...), custom_call_target="tpu_custom_call" | custom-call | flops 575000000 | bytes 1 | tf_op jit(solution)/shard_map/attention_back_sent/pallas_call | solution.py:56
  71.9 0.8 grad_reduce_add1.1
  72.7 2.8 %collective-permute-start.13 = (bf16[2,2,2,96,384]{4,3,2,1,0:T(8,128)(2,1)S(1)}, bf16[2,2,2,96,384]{4,3,2,1,0:T(8,128)(2,1)S(1)}, u32[]{:S(2)}, u32[]{:S(2)}) collective-permute-start(bf16[2,2,2,96,384]{4,3,2,1,0:T(8,128)(2,1)S(1)} %get-tuple-element.189), channel_id=1, source_target_pairs={{0,16},{1,17},{2,18},{3,19},{4,20},{5,21},{6,22},{7,23},{8,24},{9,... | collective-permute-start | bytes 1769480 | tf_op jit(solution)/shard_map/ppermute | solution.py:634
  75.5 6.3 %attention_back_kept.1 = (bf16[3,256,384]{2,1,0:T(8,128)(2,1)S(1)}, bf16[3,256,384]{2,1,0:T(8,128)(2,1)S(1)}, f32[3,8,384]{2,1,0:T(8,128)S(1)}) custom-call(s32[9]{0:T(128)S(1)} %concatenate.3.scal, bf16[512,768]{1,0:T(8,128)(2,1)S(1)} %get-tuple-element.131.refs_0_.rq, bf16[512,768]{1,0:T(8,128)(2,1)S(1)} %get-tuple-element.127.rk, ...), custom_call_target="tpu_custom_call" | custom-call | flops 575000000 | bytes 1 | tf_op jit(solution)/shard_map/attention_back_kept/pallas_call | solution.py:56
  81.8 0.7 grad_expand_add1.1
  82.5 1.6 %collective-permute-start.15 = (bf16[4,120,384]{2,1,0:T(8,128)(2,1)S(1)}, bf16[4,120,384]{2,1,0:T(8,128)(2,1)S(1)}, u32[]{:S(2)}, u32[]{:S(2)}) collective-permute-start(bf16[4,120,384]{2,1,0:T(8,128)(2,1)S(1)} %get-tuple-element.192), channel_id=1, source_target_pairs={{0,1},{1,0},{2,3},{3,2},{4,5},{5,4},{6,7},{7,6},{8,9},{9,8},{10,11... | collective-permute-start | bytes 1105928 | tf_op jit(solution)/shard_map/ppermute | solution.py:634
  84.0 1.5 %collective-permute-start.14 = (bf16[4,120,384]{2,1,0:T(8,128)(2,1)S(1)}, bf16[4,120,384]{2,1,0:T(8,128)(2,1)S(1)}, u32[]{:S(2)}, u32[]{:S(2)}) collective-permute-start(bf16[4,120,384]{2,1,0:T(8,128)(2,1)S(1)} %get-tuple-element.175), channel_id=1, source_target_pairs={{0,4},{1,5},{2,6},{3,7},{4,0},{5,1},{6,2},{7,3},{8,12},{9,13},{10,... | collective-permute-start | bytes 1105928 | tf_op jit(solution)/shard_map/ppermute | solution.py:634
  85.6 4.8 %grad_heads.1 = (bf16[2,4,80,384]{3,2,1,0:T(8,128)(2,1)S(1)}, bf16[2,4,80,384]{3,2,1,0:T(8,128)(2,1)S(1)}, bf16[2,4,80,384]{3,2,1,0:T(8,128)(2,1)S(1)}, bf16[2,4,80,384]{3,2,1,0:T(8,128)(2,1)S(1)}) custom-call(s32[9]{0:T(128)S(1)} %concatenate.3.scal, bf16[4,192,512]{2,1,0:T(8,128)(2,1)S(1)} %get-tuple-element.125.a_own, ...), custom_call_target="tpu_custom_call" | custom-call | flops 115000000 | bytes 1 | tf_op jit(solution)/shard_map/grad_heads/pallas_call | solution.py:56
  91.5 5.3 %input_grad.1 = f32[512,768]{1,0:T(8,128)} custom-call(s32[9]{0:T(128)S(1)} %concatenate.3.scal, f32[512,768]{1,0:T(8,128)S(1)} %get-tuple-element.187.first, bf16[3,256,384]{2,1,0:T(8,128)(2,1)S(1)} %get-tuple-element.168.own_early.keep_early, bf16[3,256,384]{2,1,0:T(8,128)(2,1)S(1)} %get-tuple-element.177.own_late.keep_late, ...), custom_call_target="tpu_custom_call" | custom-call | flops 115000000 | bytes 1 | tf_op jit(solution)/shard_map/input_grad/pallas_call | solution.py:56
  96.7 4.8 %collective-permute-done.13.got = bf16[2,2,2,96,384]{4,3,2,1,0:T(8,128)(2,1)S(1)} collective-permute-done((bf16[2,2,2,96,384]{4,3,2,1,0:T(8,128)(2,1)S(1)}, bf16[2,2,2,96,384]{4,3,2,1,0:T(8,128)(2,1)S(1)}, u32[]{:S(2)}, u32[]{:S(2)}) %collective-permute-start.13) | collective-permute-done | bytes 589856 | tf_op jit(solution)/shard_map/ppermute | solution.py:634
  101.6 0.6 grad_reduce_add2.1
  102.2 0.8 grad_expand_add2.1
  103.2 1.4 %collective-permute-start.21 = (bf16[2,2,96,384]{3,2,1,0:T(8,128)(2,1)S(1)}, bf16[2,2,96,384]{3,2,1,0:T(8,128)(2,1)S(1)}, u32[]{:S(2)}, u32[]{:S(2)}) collective-permute-start(bf16[2,2,96,384]{3,2,1,0:T(8,128)(2,1)S(1)} %get-tuple-element.206), channel_id=1, source_target_pairs={{0,1},{1,0},{2,3},{3,2},{4,5},{5,4},{6,7},{7,6},{8,9},{9,8},{10,11... | collective-permute-start | bytes 884744 | tf_op jit(solution)/shard_map/ppermute | solution.py:634
  104.6 0.7 grad_heads_add1.1
  105.3 0.7 collective-permute-start.20
  106.0 1.4 %collective-permute-start.19 = (bf16[4,80,384]{2,1,0:T(8,128)(2,1)S(1)}, bf16[4,80,384]{2,1,0:T(8,128)(2,1)S(1)}, u32[]{:S(2)}, u32[]{:S(2)}) collective-permute-start(bf16[4,80,384]{2,1,0:T(8,128)(2,1)S(1)} %get-tuple-element.198), channel_id=1, source_target_pairs={{0,4},{1,5},{2,6},{3,7},{4,0},{5,1},{6,2},{7,3},{8,12},{9,13},{10,... | collective-permute-start | bytes 737288 | tf_op jit(solution)/shard_map/ppermute | solution.py:634
  107.4 6.0 %collective-permute-done.18.got = bf16[2,2,120,384]{3,2,1,0:T(8,128)(2,1)S(1)} collective-permute-done((bf16[2,2,120,384]{3,2,1,0:T(8,128)(2,1)S(1)}, bf16[2,2,120,384]{3,2,1,0:T(8,128)(2,1)S(1)}, u32[]{:S(2)}, u32[]{:S(2)}) %collective-permute-start.18) | collective-permute-done | bytes 368672 | tf_op jit(solution)/shard_map/ppermute | solution.py:634
  113.4 0.6 grad_expand_add3.1
  114.0 1.4 %collective-permute-start.22 = (bf16[2,120,384]{2,1,0:T(8,128)(2,1)S(1)}, bf16[2,120,384]{2,1,0:T(8,128)(2,1)S(1)}, u32[]{:S(2)}, u32[]{:S(2)}) collective-permute-start(bf16[2,120,384]{2,1,0:T(8,128)(2,1)S(1)} %get-tuple-element.209), channel_id=1, source_target_pairs={{0,16},{1,17},{2,18},{3,19},{4,20},{5,21},{6,22},{7,23},{8,24},{9,... | collective-permute-start | bytes 552968 | tf_op jit(solution)/shard_map/ppermute | solution.py:634
  115.4 1.7 %collective-permute-done.20.ym = bf16[4,80,384]{2,1,0:T(8,128)(2,1)S(1)} collective-permute-done((bf16[4,80,384]{2,1,0:T(8,128)(2,1)S(1)}, bf16[4,80,384]{2,1,0:T(8,128)(2,1)S(1)}, u32[]{:S(2)}, u32[]{:S(2)}) %collective-permute-start.20) | collective-permute-done | bytes 245792 | tf_op jit(solution)/shard_map/ppermute | solution.py:634
  117.1 0.7 grad_heads_add2.1
  118.5 1.5 %collective-permute-start.23 = (bf16[2,96,384]{2,1,0:T(8,128)(2,1)S(1)}, bf16[2,96,384]{2,1,0:T(8,128)(2,1)S(1)}, u32[]{:S(2)}, u32[]{:S(2)}) collective-permute-start(bf16[2,96,384]{2,1,0:T(8,128)(2,1)S(1)} %get-tuple-element.212), channel_id=1, source_target_pairs={{0,4},{1,5},{2,6},{3,7},{4,0},{5,1},{6,2},{7,3},{8,12},{9,13},{10,... | collective-permute-start | bytes 442376 | tf_op jit(solution)/shard_map/ppermute | solution.py:634
  119.9 0.7 collective-permute-start.24
  120.6 3.1 %collective-permute-start.25 = (bf16[2,80,384]{2,1,0:T(8,128)(2,1)S(1)}, bf16[2,80,384]{2,1,0:T(8,128)(2,1)S(1)}, u32[]{:S(2)}, u32[]{:S(2)}) collective-permute-start(bf16[2,80,384]{2,1,0:T(8,128)(2,1)S(1)} %get-tuple-element.216), channel_id=1, source_target_pairs={{0,16},{1,17},{2,18},{3,19},{4,20},{5,21},{6,22},{7,23},{8,24},{9,... | collective-permute-start | bytes 368648 | tf_op jit(solution)/shard_map/ppermute | solution.py:634
  123.7 1.1 collective-permute-start.26
  126.6 3.6 %collective-permute-done.24.z1 = bf16[2,80,384]{2,1,0:T(8,128)(2,1)S(1)} collective-permute-done((bf16[2,80,384]{2,1,0:T(8,128)(2,1)S(1)}, bf16[2,80,384]{2,1,0:T(8,128)(2,1)S(1)}, u32[]{:S(2)}, u32[]{:S(2)}) %collective-permute-start.24) | collective-permute-done | bytes 122912 | tf_op jit(solution)/shard_map/ppermute | solution.py:634
  130.2 3.0 %collective-permute-done.25.z2 = bf16[2,80,384]{2,1,0:T(8,128)(2,1)S(1)} collective-permute-done((bf16[2,80,384]{2,1,0:T(8,128)(2,1)S(1)}, bf16[2,80,384]{2,1,0:T(8,128)(2,1)S(1)}, u32[]{:S(2)}, u32[]{:S(2)}) %collective-permute-start.25) | collective-permute-done | bytes 122912 | tf_op jit(solution)/shard_map/ppermute | solution.py:634
  133.2 0.6 grad_heads_add3.1
  133.9 1.3 collective-permute-done.27.got
  135.3 1.5 %finish.1 = (f32[24,2304]{1,0:T(8,128)}, f32[96,768]{1,0:T(8,128)}, f32[24,3072]{1,0:T(8,128)}, f32[24,768]{1,0:T(8,128)}, f32[1,48]{1,0:T(1,128)}, /*index=5*/f...) custom-call(s32[9]{0:T(128)S(1)} %concatenate.3.scal, ...), custom_call_target="tpu_custom_call" | custom-call | flops 115000000 | bytes 1 | tf_op jit(solution)/shard_map/finish/pallas_call | solution.py:56
  (81 shorter events, 6.5 us)
Async XLA Ops:
  2.1 2.0 %copy-start = (bf16[768,2304]{1,0:T(8,128)(2,1)S(1)}, bf16[768,2304]{1,0:T(8,128)(2,1)}, u32[]{:S(2)}) copy-start(bf16[768,2304]{1,0:T(8,128)(2,1)} %w_send.1) | copy-start | bytes 10616836
  4.1 1.1 copy-start.3
  5.3 13.4 %slice-start = ((s8[4718592]{0:T(1024)(128)(4,1)}), s8[4194304]{0:T(1024)(128)(4,1)S(1)}, s32[]{:S(2)}) async-start(s8[4718592]{0:T(1024)(128)(4,1)} %bitcast.14), calls=%async_computation | async-start | bytes 8388608
  5.3 13.4 %slice-start.2 = ((s8[4718592]{0:T(1024)(128)(4,1)}), s8[4194304]{0:T(1024)(128)(4,1)S(1)}, s32[]{:S(2)}) async-start(s8[4718592]{0:T(1024)(128)(4,1)} %bitcast.16), calls=%async_computation.2 | async-start | bytes 8388608
  9.4 9.0 %collective-permute-start = (bf16[4,192,512]{2,1,0:T(8,128)(2,1)S(1)}, bf16[4,192,512]{2,1,0:T(8,128)(2,1)S(1)}, u32[]{:S(2)}, u32[]{:S(2)}) collective-permute-start(bf16[4,192,512]{2,1,0:T(8,128)(2,1)S(1)} %get-tuple-element.125.a_own), channel_id=1, source_target_pairs={{0,2},{1,3},{2,0},{3,1},{4,6},{5,7},{6,4},{7,5},{8,10},{9,11},{10,... | collective-permute-start | bytes 2359304 | tf_op jit(solution)/shard_map/ppermute | solution.py:634
  9.9 8.8 %collective-permute-start.1 = (bf16[7,128,128]{2,1,0:T(8,128)(2,1)S(1)}, bf16[7,128,128]{2,1,0:T(8,128)(2,1)S(1)}, u32[]{:S(2)}, u32[]{:S(2)}) collective-permute-start(bf16[7,128,128]{2,1,0:T(8,128)(2,1)S(1)} %get-tuple-element.134), channel_id=1, source_target_pairs={{0,1},{1,0},{2,3},{3,2},{4,5},{5,4},{6,7},{7,6},{8,9},{9,8},{10,11... | collective-permute-start | bytes 688136 | tf_op jit(solution)/shard_map/ppermute | solution.py:634
  12.4 5.8 %copy-start.7 = (bf16[768]{0:T(1024)(128)(2,1)S(1)}, bf16[768]{0:T(1024)(128)(2,1)}, u32[]{:S(2)}) copy-start(bf16[768]{0:T(1024)(128)(2,1)} %param.20) | copy-start | bytes 4612
  12.4 5.8 %copy-start.8 = (bf16[768]{0:T(1024)(128)(2,1)S(1)}, bf16[768]{0:T(1024)(128)(2,1)}, u32[]{:S(2)}) copy-start(bf16[768]{0:T(1024)(128)(2,1)} %param.19) | copy-start | bytes 4612
  12.4 5.8 %copy-start.9 = (bf16[768]{0:T(1024)(128)(2,1)S(1)}, bf16[768]{0:T(1024)(128)(2,1)}, u32[]{:S(2)}) copy-start(bf16[768]{0:T(1024)(128)(2,1)} %param.21) | copy-start | bytes 4612
  12.4 5.9 %copy-start.10 = (bf16[768]{0:T(1024)(128)(2,1)S(1)}, bf16[768]{0:T(1024)(128)(2,1)}, u32[]{:S(2)}) copy-start(bf16[768]{0:T(1024)(128)(2,1)} %param.25) | copy-start | bytes 4612
  12.5 5.9 %copy-start.6 = (bf16[3072]{0:T(1024)(128)(2,1)S(1)}, bf16[3072]{0:T(1024)(128)(2,1)}, u32[]{:S(2)}) copy-start(bf16[3072]{0:T(1024)(128)(2,1)} %param.23) | copy-start | bytes 18436
  12.5 6.2 %slice-start.1 = ((s8[4718592]{0:T(1024)(128)(4,1)}), s8[524288]{0:T(1024)(128)(4,1)S(1)}, s32[]{:S(2)}) async-start(s8[4718592]{0:T(1024)(128)(4,1)} %bitcast.14), calls=%async_computation.1 | async-start | bytes 1048576
  12.5 6.2 %slice-start.3 = ((s8[4718592]{0:T(1024)(128)(4,1)}), s8[524288]{0:T(1024)(128)(4,1)S(1)}, s32[]{:S(2)}) async-start(s8[4718592]{0:T(1024)(128)(4,1)} %bitcast.16), calls=%async_computation.3 | async-start | bytes 1048576
  12.5 6.2 %copy-start.2 = (bf16[768,768]{1,0:T(8,128)(2,1)S(1)}, bf16[768,768]{1,0:T(8,128)(2,1)}, u32[]{:S(2)}) copy-start(bf16[768,768]{1,0:T(8,128)(2,1)} %w_merge.1) | copy-start | bytes 3538948
  12.5 6.2 %copy-start.4 = (bf16[512,768]{1,0:T(8,128)(2,1)S(1)}, bf16[512,768]{1,0:T(8,128)(2,1)}, u32[]{:S(2)}) copy-start(bf16[512,768]{1,0:T(8,128)(2,1)} %refs_5_.1) | copy-start | bytes 2359300
  18.7 10.9 %copy-start.11 = (bf16[768]{0:T(1024)(128)(2,1)S(1)}, bf16[768]{0:T(1024)(128)(2,1)}, u32[]{:S(2)}) copy-start(bf16[768]{0:T(1024)(128)(2,1)} %param.26) | copy-start | bytes 4612
  18.7 10.9 %copy-start.12 = (bf16[768]{0:T(1024)(128)(2,1)S(1)}, bf16[768]{0:T(1024)(128)(2,1)}, u32[]{:S(2)}) copy-start(bf16[768]{0:T(1024)(128)(2,1)} %param.27) | copy-start | bytes 4612
  18.7 10.9 %copy-start.5 = (bf16[512,768]{1,0:T(8,128)(2,1)S(1)}, bf16[512,768]{1,0:T(8,128)(2,1)}, u32[]{:S(2)}) copy-start(bf16[512,768]{1,0:T(8,128)(2,1)} %cot.1) | copy-start | bytes 2359300
  29.1 9.4 %collective-permute-start.3 = (bf16[512,3072]{1,0:T(8,128)(2,1)S(1)}, bf16[512,3072]{1,0:T(8,128)(2,1)S(1)}, u32[]{:S(2)}, u32[]{:S(2)}) collective-permute-start(bf16[512,3072]{1,0:T(8,128)(2,1)S(1)} %get-tuple-element.143.a_own), channel_id=1, source_target_pairs={{0,2},{1,3},{2,0},{3,1},{4,6},{5,7},{6,4},{7,5},{8,10},{9,11},{10,... | collective-permute-start | bytes 9437192 | tf_op jit(solution)/shard_map/ppermute | solution.py:634
  29.1 9.3 %collective-permute-start.2 = (bf16[2,4,192,512]{3,2,1,0:T(8,128)(2,1)S(1)}, bf16[2,4,192,512]{3,2,1,0:T(8,128)(2,1)S(1)}, u32[]{:S(2)}, u32[]{:S(2)}) collective-permute-start(bf16[2,4,192,512]{3,2,1,0:T(8,128)(2,1)S(1)} %get-tuple-element.137.a_own.m_own), channel_id=1, source_target_pairs={{0,2},{1,3},{2,0},{3,1},{4,6},{5,7},{6,4},{7,5},{8,10},{9,11},{10,... | collective-permute-start | bytes 4718600 | tf_op jit(solution)/shard_map/ppermute | solution.py:634
  32.2 6.2 %collective-permute-start.4 = (bf16[512,384]{1,0:T(8,128)(2,1)S(1)}, bf16[512,384]{1,0:T(8,128)(2,1)S(1)}, u32[]{:S(2)}, u32[]{:S(2)}) collective-permute-start(bf16[512,384]{1,0:T(8,128)(2,1)S(1)} %get-tuple-element.145), channel_id=1, source_target_pairs={{0,2},{1,3},{2,0},{3,1},{4,6},{5,7},{6,4},{7,5},{8,10},{9,11},{10,... | collective-permute-start | bytes 1179656 | tf_op jit(solution)/shard_map/ppermute | solution.py:634
  37.8 18.2 %collective-permute-start.5 = (bf16[2,512,768]{2,1,0:T(8,128)(2,1)S(1)}, bf16[2,512,768]{2,1,0:T(8,128)(2,1)S(1)}, u32[]{:S(2)}, u32[]{:S(2)}) collective-permute-start(bf16[2,512,768]{2,1,0:T(8,128)(2,1)S(1)} %get-tuple-element.153), channel_id=1, source_target_pairs={{0,2},{1,3},{2,0},{3,1},{4,6},{5,7},{6,4},{7,5},{8,10},{9,11},{10,... | collective-permute-start | bytes 4718600 | tf_op jit(solution)/shard_map/ppermute | solution.py:634
  43.8 28.1 %collective-permute-start.8 = (bf16[2,2,2,2,96,384]{5,4,3,2,1,0:T(8,128)(2,1)S(1)}, bf16[2,2,2,2,96,384]{5,4,3,2,1,0:T(8,128)(2,1)S(1)}, u32[]{:S(2)}, u32[]{:S(2)}) collective-permute-start(bf16[2,2,2,2,96,384]{5,4,3,2,1,0:T(8,128)(2,1)S(1)} %get-tuple-element.146), channel_id=1, source_target_pairs={{0,8},{1,9},{2,10},{3,11},{4,12},{5,13},{6,14},{7,15},{8,0},{9,1},... | collective-permute-start | bytes 3538952 | tf_op jit(solution)/shard_map/ppermute | solution.py:634
  54.4 1.8 %collective-permute-start.6 = (bf16[512,384]{1,0:T(8,128)(2,1)S(1)}, bf16[512,384]{1,0:T(8,128)(2,1)S(1)}, u32[]{:S(2)}, u32[]{:S(2)}) collective-permute-start(bf16[512,384]{1,0:T(8,128)(2,1)S(1)} %get-tuple-element.155), channel_id=1, source_target_pairs={{0,2},{1,3},{2,0},{3,1},{4,6},{5,7},{6,4},{7,5},{8,10},{9,11},{10,... | collective-permute-start | bytes 1179656 | tf_op jit(solution)/shard_map/ppermute | solution.py:634
  54.5 8.0 %collective-permute-start.7 = (bf16[7,128,128]{2,1,0:T(8,128)(2,1)S(1)}, bf16[7,128,128]{2,1,0:T(8,128)(2,1)S(1)}, u32[]{:S(2)}, u32[]{:S(2)}) collective-permute-start(bf16[7,128,128]{2,1,0:T(8,128)(2,1)S(1)} %get-tuple-element.157), channel_id=1, source_target_pairs={{0,1},{1,0},{2,3},{3,2},{4,5},{5,4},{6,7},{7,6},{8,9},{9,8},{10,11... | collective-permute-start | bytes 688136 | tf_op jit(solution)/shard_map/ppermute | solution.py:634
  62.5 19.3 %collective-permute-start.9 = (bf16[2,4,120,384]{3,2,1,0:T(8,128)(2,1)S(1)}, bf16[2,4,120,384]{3,2,1,0:T(8,128)(2,1)S(1)}, u32[]{:S(2)}, u32[]{:S(2)}) collective-permute-start(bf16[2,4,120,384]{3,2,1,0:T(8,128)(2,1)S(1)} %get-tuple-element.171), channel_id=1, source_target_pairs={{0,1},{1,0},{2,3},{3,2},{4,5},{5,4},{6,7},{7,6},{8,9},{9,8},{10,11... | collective-permute-start | bytes 2211848 | tf_op jit(solution)/shard_map/ppermute | solution.py:634
  64.0 17.8 %collective-permute-start.10 = (bf16[2,4,120,384]{3,2,1,0:T(8,128)(2,1)S(1)}, bf16[2,4,120,384]{3,2,1,0:T(8,128)(2,1)S(1)}, u32[]{:S(2)}, u32[]{:S(2)}) collective-permute-start(bf16[2,4,120,384]{3,2,1,0:T(8,128)(2,1)S(1)} %get-tuple-element.174), channel_id=1, source_target_pairs={{0,4},{1,5},{2,6},{3,7},{4,0},{5,1},{6,2},{7,3},{8,12},{9,13},{10,... | collective-permute-start | bytes 2211848 | tf_op jit(solution)/shard_map/ppermute | solution.py:634
  71.3 14.3 %collective-permute-start.12 = (bf16[3,256,384]{2,1,0:T(8,128)(2,1)S(1)}, bf16[3,256,384]{2,1,0:T(8,128)(2,1)S(1)}, u32[]{:S(2)}, u32[]{:S(2)}) collective-permute-start(bf16[3,256,384]{2,1,0:T(8,128)(2,1)S(1)} %get-tuple-element.178.send_late), channel_id=1, source_target_pairs={{0,2},{1,3},{2,0},{3,1},{4,6},{5,7},{6,4},{7,5},{8,10},{9,11},{10,... | collective-permute-start | bytes 1769480 | tf_op jit(solution)/shard_map/ppermute | solution.py:634
  71.3 14.2 %collective-permute-start.11 = (bf16[3,256,384]{2,1,0:T(8,128)(2,1)S(1)}, bf16[3,256,384]{2,1,0:T(8,128)(2,1)S(1)}, u32[]{:S(2)}, u32[]{:S(2)}) collective-permute-start(bf16[3,256,384]{2,1,0:T(8,128)(2,1)S(1)} %get-tuple-element.161.send_early), channel_id=1, source_target_pairs={{0,2},{1,3},{2,0},{3,1},{4,6},{5,7},{6,4},{7,5},{8,10},{9,11},{10,... | collective-permute-start | bytes 1769480 | tf_op jit(solution)/shard_map/ppermute | solution.py:634
  72.7 28.9 %collective-permute-start.13 = (bf16[2,2,2,96,384]{4,3,2,1,0:T(8,128)(2,1)S(1)}, bf16[2,2,2,96,384]{4,3,2,1,0:T(8,128)(2,1)S(1)}, u32[]{:S(2)}, u32[]{:S(2)}) collective-permute-start(bf16[2,2,2,96,384]{4,3,2,1,0:T(8,128)(2,1)S(1)} %get-tuple-element.189), channel_id=1, source_target_pairs={{0,16},{1,17},{2,18},{3,19},{4,20},{5,21},{6,22},{7,23},{8,24},{9,... | collective-permute-start | bytes 1769480 | tf_op jit(solution)/shard_map/ppermute | solution.py:634
  82.5 19.7 %collective-permute-start.15 = (bf16[4,120,384]{2,1,0:T(8,128)(2,1)S(1)}, bf16[4,120,384]{2,1,0:T(8,128)(2,1)S(1)}, u32[]{:S(2)}, u32[]{:S(2)}) collective-permute-start(bf16[4,120,384]{2,1,0:T(8,128)(2,1)S(1)} %get-tuple-element.192), channel_id=1, source_target_pairs={{0,1},{1,0},{2,3},{3,2},{4,5},{5,4},{6,7},{7,6},{8,9},{9,8},{10,11... | collective-permute-start | bytes 1105928 | tf_op jit(solution)/shard_map/ppermute | solution.py:634
  84.0 18.2 %collective-permute-start.14 = (bf16[4,120,384]{2,1,0:T(8,128)(2,1)S(1)}, bf16[4,120,384]{2,1,0:T(8,128)(2,1)S(1)}, u32[]{:S(2)}, u32[]{:S(2)}) collective-permute-start(bf16[4,120,384]{2,1,0:T(8,128)(2,1)S(1)} %get-tuple-element.175), channel_id=1, source_target_pairs={{0,4},{1,5},{2,6},{3,7},{4,0},{5,1},{6,2},{7,3},{8,12},{9,13},{10,... | collective-permute-start | bytes 1105928 | tf_op jit(solution)/shard_map/ppermute | solution.py:634
  85.6 5.9 %copy-start.1 = (bf16[768,2304]{1,0:T(8,128)(2,1)S(1)}, bf16[768,2304]{1,0:T(8,128)(2,1)}, u32[]{:S(2)}) copy-start(bf16[768,2304]{1,0:T(8,128)(2,1)} %w_send.1) | copy-start | bytes 10616836
  90.4 14.2 %collective-permute-start.17 = (bf16[2,4,80,384]{3,2,1,0:T(8,128)(2,1)S(1)}, bf16[2,4,80,384]{3,2,1,0:T(8,128)(2,1)S(1)}, u32[]{:S(2)}, u32[]{:S(2)}) collective-permute-start(bf16[2,4,80,384]{3,2,1,0:T(8,128)(2,1)S(1)} %get-tuple-element.197), channel_id=1, source_target_pairs={{0,4},{1,5},{2,6},{3,7},{4,0},{5,1},{6,2},{7,3},{8,12},{9,13},{10,... | collective-permute-start | bytes 1474568 | tf_op jit(solution)/shard_map/ppermute | solution.py:634
  90.9 13.7 %collective-permute-start.16 = (bf16[2,4,80,384]{3,2,1,0:T(8,128)(2,1)S(1)}, bf16[2,4,80,384]{3,2,1,0:T(8,128)(2,1)S(1)}, u32[]{:S(2)}, u32[]{:S(2)}) collective-permute-start(bf16[2,4,80,384]{3,2,1,0:T(8,128)(2,1)S(1)} %get-tuple-element.185), channel_id=1, source_target_pairs={{0,1},{1,0},{2,3},{3,2},{4,5},{5,4},{6,7},{7,6},{8,9},{9,8},{10,11... | collective-permute-start | bytes 1474568 | tf_op jit(solution)/shard_map/ppermute | solution.py:634
  103.1 10.3 %collective-permute-start.18 = (bf16[2,2,120,384]{3,2,1,0:T(8,128)(2,1)S(1)}, bf16[2,2,120,384]{3,2,1,0:T(8,128)(2,1)S(1)}, u32[]{:S(2)}, u32[]{:S(2)}) collective-permute-start(bf16[2,2,120,384]{3,2,1,0:T(8,128)(2,1)S(1)} %get-tuple-element.200), channel_id=1, source_target_pairs={{0,8},{1,9},{2,10},{3,11},{4,12},{5,13},{6,14},{7,15},{8,0},{9,1},... | collective-permute-start | bytes 1105928 | tf_op jit(solution)/shard_map/ppermute | solution.py:634
  103.2 14.7 %collective-permute-start.21 = (bf16[2,2,96,384]{3,2,1,0:T(8,128)(2,1)S(1)}, bf16[2,2,96,384]{3,2,1,0:T(8,128)(2,1)S(1)}, u32[]{:S(2)}, u32[]{:S(2)}) collective-permute-start(bf16[2,2,96,384]{3,2,1,0:T(8,128)(2,1)S(1)} %get-tuple-element.206), channel_id=1, source_target_pairs={{0,1},{1,0},{2,3},{3,2},{4,5},{5,4},{6,7},{7,6},{8,9},{9,8},{10,11... | collective-permute-start | bytes 884744 | tf_op jit(solution)/shard_map/ppermute | solution.py:634
  105.3 11.9 %collective-permute-start.20 = (bf16[4,80,384]{2,1,0:T(8,128)(2,1)S(1)}, bf16[4,80,384]{2,1,0:T(8,128)(2,1)S(1)}, u32[]{:S(2)}, u32[]{:S(2)}) collective-permute-start(bf16[4,80,384]{2,1,0:T(8,128)(2,1)S(1)} %get-tuple-element.203), channel_id=1, source_target_pairs={{0,1},{1,0},{2,3},{3,2},{4,5},{5,4},{6,7},{7,6},{8,9},{9,8},{10,11... | collective-permute-start | bytes 737288 | tf_op jit(solution)/shard_map/ppermute | solution.py:634
  106.0 11.2 %collective-permute-start.19 = (bf16[4,80,384]{2,1,0:T(8,128)(2,1)S(1)}, bf16[4,80,384]{2,1,0:T(8,128)(2,1)S(1)}, u32[]{:S(2)}, u32[]{:S(2)}) collective-permute-start(bf16[4,80,384]{2,1,0:T(8,128)(2,1)S(1)} %get-tuple-element.198), channel_id=1, source_target_pairs={{0,4},{1,5},{2,6},{3,7},{4,0},{5,1},{6,2},{7,3},{8,12},{9,13},{10,... | collective-permute-start | bytes 737288 | tf_op jit(solution)/shard_map/ppermute | solution.py:634
  114.0 10.8 %collective-permute-start.22 = (bf16[2,120,384]{2,1,0:T(8,128)(2,1)S(1)}, bf16[2,120,384]{2,1,0:T(8,128)(2,1)S(1)}, u32[]{:S(2)}, u32[]{:S(2)}) collective-permute-start(bf16[2,120,384]{2,1,0:T(8,128)(2,1)S(1)} %get-tuple-element.209), channel_id=1, source_target_pairs={{0,16},{1,17},{2,18},{3,19},{4,20},{5,21},{6,22},{7,23},{8,24},{9,... | collective-permute-start | bytes 552968 | tf_op jit(solution)/shard_map/ppermute | solution.py:634
  118.5 7.0 %collective-permute-start.23 = (bf16[2,96,384]{2,1,0:T(8,128)(2,1)S(1)}, bf16[2,96,384]{2,1,0:T(8,128)(2,1)S(1)}, u32[]{:S(2)}, u32[]{:S(2)}) collective-permute-start(bf16[2,96,384]{2,1,0:T(8,128)(2,1)S(1)} %get-tuple-element.212), channel_id=1, source_target_pairs={{0,4},{1,5},{2,6},{3,7},{4,0},{5,1},{6,2},{7,3},{8,12},{9,13},{10,... | collective-permute-start | bytes 442376 | tf_op jit(solution)/shard_map/ppermute | solution.py:634
  119.9 10.2 %collective-permute-start.24 = (bf16[2,80,384]{2,1,0:T(8,128)(2,1)S(1)}, bf16[2,80,384]{2,1,0:T(8,128)(2,1)S(1)}, u32[]{:S(2)}, u32[]{:S(2)}) collective-permute-start(bf16[2,80,384]{2,1,0:T(8,128)(2,1)S(1)} %get-tuple-element.215), channel_id=1, source_target_pairs={{0,8},{1,9},{2,10},{3,11},{4,12},{5,13},{6,14},{7,15},{8,0},{9,1},... | collective-permute-start | bytes 368648 | tf_op jit(solution)/shard_map/ppermute | solution.py:634
  120.6 12.6 %collective-permute-start.25 = (bf16[2,80,384]{2,1,0:T(8,128)(2,1)S(1)}, bf16[2,80,384]{2,1,0:T(8,128)(2,1)S(1)}, u32[]{:S(2)}, u32[]{:S(2)}) collective-permute-start(bf16[2,80,384]{2,1,0:T(8,128)(2,1)S(1)} %get-tuple-element.216), channel_id=1, source_target_pairs={{0,16},{1,17},{2,18},{3,19},{4,20},{5,21},{6,22},{7,23},{8,24},{9,... | collective-permute-start | bytes 368648 | tf_op jit(solution)/shard_map/ppermute | solution.py:634
  123.7 9.5 %collective-permute-start.26 = (bf16[2,80,384]{2,1,0:T(8,128)(2,1)S(1)}, bf16[2,80,384]{2,1,0:T(8,128)(2,1)S(1)}, u32[]{:S(2)}, u32[]{:S(2)}) collective-permute-start(bf16[2,80,384]{2,1,0:T(8,128)(2,1)S(1)} %get-tuple-element.217), channel_id=1, source_target_pairs={{0,24},{1,25},{2,26},{3,27},{4,28},{5,29},{6,30},{7,31},{8,16},{9,... | collective-permute-start | bytes 368648 | tf_op jit(solution)/shard_map/ppermute | solution.py:634
  125.4 9.9 %collective-permute-start.29 = (f32[120,384]{1,0:T(8,128)S(1)}, f32[120,384]{1,0:T(8,128)S(1)}, u32[]{:S(2)}, u32[]{:S(2)}) collective-permute-start(f32[120,384]{1,0:T(8,128)S(1)} %get-tuple-element.221), channel_id=1, source_target_pairs={{0,2},{1,3},{2,0},{3,1},{4,6},{5,7},{6,4},{7,5},{8,10},{9,11},{10,... | collective-permute-start | bytes 552968 | tf_op jit(solution)/shard_map/ppermute | solution.py:634
  126.1 9.2 %collective-permute-start.28 = (f32[96,384]{1,0:T(8,128)S(1)}, f32[96,384]{1,0:T(8,128)S(1)}, u32[]{:S(2)}, u32[]{:S(2)}) collective-permute-start(f32[96,384]{1,0:T(8,128)S(1)} %get-tuple-element.220), channel_id=1, source_target_pairs={{0,2},{1,3},{2,0},{3,1},{4,6},{5,7},{6,4},{7,5},{8,10},{9,11},{10,... | collective-permute-start | bytes 442376 | tf_op jit(solution)/shard_map/ppermute | solution.py:634
  133.8 1.4 %collective-permute-start.27 = (f32[80,384]{1,0:T(8,128)S(1)}, f32[80,384]{1,0:T(8,128)S(1)}, u32[]{:S(2)}, u32[]{:S(2)}) collective-permute-start(f32[80,384]{1,0:T(8,128)S(1)} %get-tuple-element.219), channel_id=1, source_target_pairs={{0,2},{1,3},{2,0},{3,1},{4,6},{5,7},{6,4},{7,5},{8,10},{9,11},{10,... | collective-permute-start | bytes 368648 | tf_op jit(solution)/shard_map/ppermute | solution.py:634
